TPU v7x, 32 devices: a whole 2x2x4 slice. The times are simulated.
32 devices in a mesh: section: 2 (over x), fsdp: 4 (over z), seq: 4 (over y, core).
Axes of the slice: x: 2, y: 2, z: 4, core: 2. Of those that a mesh axis runs over, the one named last changes fastest.
Arguments:
- acts: bfloat16 [2, 4, 512, 1536], P('section', 'fsdp', 'seq')
- grad_out: bfloat16 [4, 512, 1536], P('fsdp', 'seq'), may hold values from -6 to 6
- gain: float32 [2, 1536], P('section'), may hold values from 0.5 to 2
- gate: float32 [2, 1536], P('section'), may hold values from 0.5 to 2
- w_query: bfloat16 [2, 1536, 1536], P('section', ('fsdp', 'seq'))
- kept: int32 [4, 2], P('fsdp'), may hold values from 0 to 1, as said below
- links: int32 [4, 4], P('fsdp', 'seq'), may hold values from 0 to 1, as said below
Outputs:
- grad_acts: bfloat16 [2, 4, 512, 1536], P('section', 'fsdp', 'seq')
- grad_wq: bfloat16 [2, 1536, 1536], P('section', ('fsdp', 'seq'))
Inputs may be any that keep to these rules, and one draw needn't show every extreme that they name: `kept`: clip 0 runs every layer; the other entries vary. `links`: in clip 0 every tile after the first attends the tile before it; the other entries vary.
All inputs are finite; a program needn't handle non-finite values.
Results may differ from a plain program's by a relative error of at most 0.025.
The roundings to bfloat16 on the way count: a program that leaves them out, or rounds other values in their place, can miss the bound.
Values may be sent and summed in bfloat16 or wider, within the bound.
No kernel may reach another device: no remote copies, remote signals or barrier semaphores. Data moves between devices by JAX's collectives and lax.ppermute only.
A program may use at most 64 MiB of HBM per device.

v0:
```python
import jax
import jax.numpy as jnp
from jax import lax
from jax.sharding import PartitionSpec as P

HDIM = 128


norm_eps = 1e-06
head_pair = 2


def from_behind(value, axis, steps):
    count = lax.axis_size(axis)
    initial, last = (max(0, -steps), min(count, count - steps))
    return lax.ppermute(value, axis, [(source, source + steps) for source in range(initial, last)])


def split_heads(token_rows):
    tokens_here = token_rows.shape[0]
    return token_rows.reshape(
        tokens_here, token_rows.shape[1] // (head_pair * HDIM), head_pair, HDIM
    ).transpose(1, 2, 0, 3)


def merge_heads(blocks):
    return blocks.transpose(2, 0, 1, 3).reshape(blocks.shape[2], -1)


def head_grads(query_heads, key_heads, grad_heads, key_valid, score_scale):

    def per_group(operands):
        query_part, key_part, grad_part = operands
        scores = (
            jnp.einsum("gid,gjd->gij", query_part, key_part, preferred_element_type=jnp.float32)
            * score_scale
        )
        scores = jnp.where(key_valid[None, None, :], scores, -1e30)
        row_max = jnp.max(scores, axis=-1, keepdims=True)
        exp_scores = jnp.exp(scores - row_max)
        prob_rows = exp_scores / jnp.sum(exp_scores, axis=-1, keepdims=True)
        probs_low = prob_rows.astype(jnp.bfloat16)
        prob_grad = jnp.einsum(
            "gid,gjd->gij", grad_part, key_part, preferred_element_type=jnp.float32
        )
        row_delta = jnp.sum(prob_rows * prob_grad, axis=-1, keepdims=True)
        score_grad = (prob_rows * (prob_grad - row_delta) * score_scale).astype(jnp.bfloat16)
        query_grad = jnp.einsum(
            "gij,gjd->gid", score_grad, key_part, preferred_element_type=jnp.float32
        ).astype(jnp.bfloat16)
        key_grad = jnp.einsum(
            "gij,gid->gjd", score_grad, query_part, preferred_element_type=jnp.float32
        )
        key_grad = key_grad + jnp.einsum(
            "gij,gid->gjd", probs_low, grad_part, preferred_element_type=jnp.float32
        )
        return (query_grad, key_grad)

    return lax.map(per_group, (query_heads, key_heads, grad_heads))


def per_device(acts, grad_out, gain, gate, w_query, kept, links):
    sections = lax.axis_size("section")
    section_idx = lax.axis_index("section")
    seq_idx = lax.axis_index("seq")
    score_scale = HDIM ** (-0.5)
    gain_row = gain[0]
    gate_row = gate[0]
    x_rows = acts[0, 0].astype(jnp.float32)
    inv_rms = lax.rsqrt(jnp.mean(x_rows * x_rows, axis=-1, keepdims=True) + norm_eps)
    normed = (x_rows * inv_rms * gain_row).astype(jnp.bfloat16)
    left_normed = from_behind(normed, "seq", 1)
    weights = lax.all_gather(w_query, ("fsdp", "seq"), axis=1, tiled=True)[0]
    tile_rows = normed.shape[0]
    key_heads = split_heads(jnp.concatenate([left_normed, normed], axis=0))
    linked = links[0, 0] * (seq_idx > 0).astype(jnp.int32) > 0
    key_valid = jnp.concatenate(
        [jnp.broadcast_to(linked, (tile_rows,)), jnp.ones((tile_rows,), dtype=jnp.bool_)]
    )
    keep_flag = lax.dynamic_index_in_dim(kept[0], section_idx, keepdims=False) > 0

    def layer_work(incoming):
        query_rows = jnp.dot(normed, weights, preferred_element_type=jnp.float32).astype(
            jnp.bfloat16
        )
        out_grad = (gate_row * incoming.astype(jnp.float32)).astype(jnp.bfloat16)
        query_grad, key_grad = head_grads(
            split_heads(query_rows), key_heads, split_heads(out_grad), key_valid, score_scale
        )
        query_grad = merge_heads(query_grad)
        key_grad = merge_heads(key_grad)
        own_grad = lax.dot_general(
            query_grad, weights, (((1,), (1,)), ((), ())), preferred_element_type=jnp.float32
        )
        own_grad = own_grad + key_grad[tile_rows:]
        return (query_grad, own_grad, key_grad[:tile_rows].astype(jnp.bfloat16))

    def layer_skip(incoming):
        return (
            jnp.zeros_like(normed),
            jnp.zeros(normed.shape, jnp.float32),
            jnp.zeros_like(normed),
        )

    incoming = jnp.where(section_idx == sections - 1, grad_out[0], jnp.zeros_like(grad_out[0]))
    result = jnp.zeros_like(grad_out[0])
    kept_grad = jnp.zeros_like(normed)
    for tick_index in range(sections):
        active = section_idx == sections - 1 - tick_index
        runs_now = jnp.logical_and(active, keep_flag)
        query_grad, own_grad, leftward = lax.cond(runs_now, layer_work, layer_skip, incoming)
        returned = from_behind(leftward, "seq", -1)
        scaled_grad = (own_grad + returned.astype(jnp.float32)) * gain_row
        mean_term = jnp.mean(x_rows * scaled_grad, axis=-1, keepdims=True)
        change = inv_rms * (scaled_grad - x_rows * inv_rms * inv_rms * mean_term)
        updated = jnp.where(
            runs_now, (incoming.astype(jnp.float32) + change).astype(jnp.bfloat16), incoming
        )
        result = jnp.where(active, updated, result)
        kept_grad = jnp.where(active, query_grad, kept_grad)
        if tick_index + 1 < sections:
            incoming = from_behind(updated, "section", -1)
    grad_rows = lax.psum_scatter(
        lax.dot_general(
            normed, kept_grad, (((0,), (0,)), ((), ())), preferred_element_type=jnp.float32
        ).astype(jnp.bfloat16),
        ("fsdp", "seq"),
        scatter_dimension=0,
        tiled=True,
    )
    return (result[None, None], grad_rows[None])


def solution(mesh):
    placed = (
        P("section", "fsdp", "seq", None),
        P("fsdp", "seq", None),
        P("section", None),
        P("section", None),
        P("section", ("fsdp", "seq"), None),
        P("fsdp", None),
        P("fsdp", "seq"),
    )
    return jax.shard_map(
        per_device,
        mesh=mesh,
        in_specs=placed,
        out_specs=(P("section", "fsdp", "seq", None), P("section", ("fsdp", "seq"), None)),
        check_vma=False,
    )
```

profile of v0, /device:TPU:0, one launch (start us, length us, event | category | flops | bytes accessed | tf_op | source)
XLA Modules:
  0.0 288.5 jit_solution(14729471892961876096)
XLA Ops:
  8.7 1.2 fusion.145
  9.8 1.2 fusion.144
  11.0 2.4 collective-permute-start
  14.1 1.3 fusion.168
  16.6 49.8 %all-gather.2.cloned.1.call-done = bf16[1,1536,1536]{2,1,0:T(8,128)(2,1)} async-done(((bf16[1,96,1536]{2,1,0:T(8,128)(2,1)}), bf16[1,1536,1536]{2,1,0:T(8,128)(2,1)}) %all-gather.2.cloned.1.call-update) | async-done | bytes 4718608 | tf_op jit(solution)/shard_map/all_gather | solution.py:73
  66.4 0.9 conditional.2
  67.3 1.4 collective-permute-start.1
  68.8 2.5 collective-permute-done.1
  71.9 1.3 collective-permute-start.2
  73.9 57.6 %collective-permute-done.2 = bf16[128,1536]{1,0:T(8,128)(2,1)} collective-permute-done((bf16[128,1536]{1,0:T(8,128)(2,1)S(1)}, bf16[128,1536]{1,0:T(8,128)(2,1)}, u32[]{:S(2)}, u32[]{:S(2)}) %collective-permute-start.2) | collective-permute-done | bytes 393248 | tf_op jit(solution)/shard_map/ppermute | solution.py:16
  131.6 68.3 %conditional.3 = (bf16[128,1536]{1,0:T(8,128)(2,1)S(1)}, f32[128,1536]{1,0:T(8,128)S(1)}, bf16[128,1536]{1,0:T(8,128)(2,1)S(1)}) conditional(s32[]{:T(128)} %convert_element_type.89, () %tuple.34, (bf16[128,1536]{1,0:T(8,128)(2,1)S(1)}, bf16[1536,1536]{1,0:T(8,128)(2,1)}, f32[1,1536]{1,0:T(1,128)S(1)}, bf16[128,1536]{1,0:T(8,128)(2,1)}, ...), branch_computations={%region_9.10_spmd, %region_10.16_spmd} | conditional | flops 1311213312 | bytes 31489304 | solution.py:111
  131.6 1.2 copy.38
  133.1 3.1 %convolution_convert_fusion.3 = bf16[128,1536]{1,0:T(8,128)(2,1)S(1)} fusion(bf16[128,1536]{1,0:T(8,128)(2,1)S(1)} %get-tuple-element.105, bf16[1536,1536]{1,0:T(8,128)(2,1)} %get-tuple-element.106), kind=kOutput, calls=%fused_computation.110 | convolution fusion | flops 604176384 | bytes 5505024 | tf_op jit(solution)/shard_map/cond/branch_1_fun/dot_general | solution.py:83
  136.9 51.6 %while.23 = (s32[]{:T(128)}, bf16[6,2,128,128]{3,2,1,0:T(8,128)(2,1)S(1)}, f32[6,2,256,128]{3,2,1,0:T(8,128)}, pred[256]{0:T(512)(128)(4,1)S(1)}, bf16[6,2,128,1...) while((s32[]{:T(128)}, ...), condition=%wide.region_15.15_spmd, body=%wide.region_11.14_spmd.sunk | while | flops 102270720 | bytes 4337761 | solution.py:59
  137.1 1.0 fusion.225
  138.1 2.9 %fusion.227 = f32[2,256,128]{2,1,0:T(8,128)} fusion(f32[2,128,256]{2,1,0:T(8,128)S(1)} %fusion.224, bf16[6,2,128,128]{3,2,1,0:T(8,128)(2,1)S(1)} %get-tuple-element.322, s32[]{:T(128)S(6)} %copy.67, f32[2,128,256]{2,1,0:T(8,128)} %get-tuple-element.267, f32[2,128]{1,0:T(2,128)S(1)} %get-tuple-element.268), kind=kOutput, calls=%fused_computation.68.clone.1 | convolution fusion | flops 17236480 | bytes 1378308 | tf_op jit(solution)/shard_map/cond/branch_1_fun/while/body/eval_jaxpr/gij,gid->gjd/dot_general | solution.py:51
  141.0 2.1 fusion.226
  143.2 2.3 fusion.228
  145.7 1.0 fusion.225
  146.7 2.9 %fusion.227 = f32[2,256,128]{2,1,0:T(8,128)} fusion(f32[2,128,256]{2,1,0:T(8,128)S(1)} %fusion.224, bf16[6,2,128,128]{3,2,1,0:T(8,128)(2,1)S(1)} %get-tuple-element.322, s32[]{:T(128)S(6)} %copy.67, f32[2,128,256]{2,1,0:T(8,128)} %get-tuple-element.267, f32[2,128]{1,0:T(2,128)S(1)} %get-tuple-element.268), kind=kOutput, calls=%fused_computation.68.clone.1 | convolution fusion | flops 17236480 | bytes 1378308 | tf_op jit(solution)/shard_map/cond/branch_1_fun/while/body/eval_jaxpr/gij,gid->gjd/dot_general | solution.py:51
  149.6 2.1 fusion.226
  151.8 2.3 fusion.228
  154.3 1.0 fusion.225
  155.3 2.9 %fusion.227 = f32[2,256,128]{2,1,0:T(8,128)} fusion(f32[2,128,256]{2,1,0:T(8,128)S(1)} %fusion.224, bf16[6,2,128,128]{3,2,1,0:T(8,128)(2,1)S(1)} %get-tuple-element.322, s32[]{:T(128)S(6)} %copy.67, f32[2,128,256]{2,1,0:T(8,128)} %get-tuple-element.267, f32[2,128]{1,0:T(2,128)S(1)} %get-tuple-element.268), kind=kOutput, calls=%fused_computation.68.clone.1 | convolution fusion | flops 17236480 | bytes 1378308 | tf_op jit(solution)/shard_map/cond/branch_1_fun/while/body/eval_jaxpr/gij,gid->gjd/dot_general | solution.py:51
  158.2 2.1 fusion.226
  160.4 2.3 fusion.228
  162.9 1.0 fusion.225
  163.9 2.9 %fusion.227 = f32[2,256,128]{2,1,0:T(8,128)} fusion(f32[2,128,256]{2,1,0:T(8,128)S(1)} %fusion.224, bf16[6,2,128,128]{3,2,1,0:T(8,128)(2,1)S(1)} %get-tuple-element.322, s32[]{:T(128)S(6)} %copy.67, f32[2,128,256]{2,1,0:T(8,128)} %get-tuple-element.267, f32[2,128]{1,0:T(2,128)S(1)} %get-tuple-element.268), kind=kOutput, calls=%fused_computation.68.clone.1 | convolution fusion | flops 17236480 | bytes 1378308 | tf_op jit(solution)/shard_map/cond/branch_1_fun/while/body/eval_jaxpr/gij,gid->gjd/dot_general | solution.py:51
  166.8 2.1 fusion.226
  169.0 2.3 fusion.228
  171.5 1.0 fusion.225
  172.5 2.9 %fusion.227 = f32[2,256,128]{2,1,0:T(8,128)} fusion(f32[2,128,256]{2,1,0:T(8,128)S(1)} %fusion.224, bf16[6,2,128,128]{3,2,1,0:T(8,128)(2,1)S(1)} %get-tuple-element.322, s32[]{:T(128)S(6)} %copy.67, f32[2,128,256]{2,1,0:T(8,128)} %get-tuple-element.267, f32[2,128]{1,0:T(2,128)S(1)} %get-tuple-element.268), kind=kOutput, calls=%fused_computation.68.clone.1 | convolution fusion | flops 17236480 | bytes 1378308 | tf_op jit(solution)/shard_map/cond/branch_1_fun/while/body/eval_jaxpr/gij,gid->gjd/dot_general | solution.py:51
  175.4 2.1 fusion.226
  177.6 2.3 fusion.228
  180.1 1.0 fusion.225
  181.1 2.9 %fusion.227 = f32[2,256,128]{2,1,0:T(8,128)} fusion(f32[2,128,256]{2,1,0:T(8,128)S(1)} %fusion.224, bf16[6,2,128,128]{3,2,1,0:T(8,128)(2,1)S(1)} %get-tuple-element.322, s32[]{:T(128)S(6)} %copy.67, f32[2,128,256]{2,1,0:T(8,128)} %get-tuple-element.267, f32[2,128]{1,0:T(2,128)S(1)} %get-tuple-element.268), kind=kOutput, calls=%fused_computation.68.clone.1 | convolution fusion | flops 17236480 | bytes 1378308 | tf_op jit(solution)/shard_map/cond/branch_1_fun/while/body/eval_jaxpr/gij,gid->gjd/dot_general | solution.py:51
  184.0 2.1 fusion.226
  186.2 2.3 fusion.228
  189.0 1.3 slice.29
  190.4 1.2 slice.24
  191.6 1.5 copy.34
  193.1 1.8 slice.20
  194.9 4.0 %convolution_add_fusion.3 = f32[128,1536]{1,0:T(8,128)S(1)} fusion(f32[128,1536]{1,0:T(8,128)S(1)} %slice.20, bf16[128,1536]{1,0:T(8,128)(2,1)S(1)} %reshape.64, bf16[1536,1536]{1,0:T(8,128)(2,1)} %get-tuple-element.106), kind=kOutput, calls=%fused_computation.109 | convolution fusion | flops 604176384 | bytes 6684672 | tf_op jit(solution)/shard_map/cond/branch_1_fun/dot_general | solution.py:92
  199.9 3.5 %convolution_convert_fusion.4 = bf16[1536,1536]{1,0:T(8,128)(2,1)} fusion(bf16[128,1536]{1,0:T(8,128)(2,1)S(1)} %fusion.144, bf16[128,1536]{1,0:T(8,128)(2,1)S(1)} %get-tuple-element.124, bf16[128,1536]{1,0:T(8,128)(2,1)S(1)} %get-tuple-element.125, pred[]{:T(512)S(6)} %eq.8, pred[]{:T(512)S(6)} %eq.7), kind=kOutput, calls=%fused_computation.114 | convolution fusion | flops 606732288 | bytes 5898242 | tf_op jit(solution)/shard_map/dot_general | solution.py:124
  203.4 1.4 collective-permute-start.3
  204.9 6.7 %collective-permute-done.3 = bf16[128,1536]{1,0:T(8,128)(2,1)S(1)} collective-permute-done((bf16[128,1536]{1,0:T(8,128)(2,1)S(1)}, bf16[128,1536]{1,0:T(8,128)(2,1)S(1)}, u32[]{:S(2)}, u32[]{:S(2)}) %collective-permute-start.3) | collective-permute-done | bytes 393248 | tf_op jit(solution)/shard_map/ppermute | solution.py:16
  211.8 2.3 fusion.155
  214.2 67.5 %reduce-scatter.2.cloned.1.call-done = bf16[96,1536]{1,0:T(8,128)(2,1)} async-done(((bf16[1536,1536]{1,0:T(8,128)(2,1)}), bf16[96,1536]{1,0:T(8,128)(2,1)}) %reduce-scatter.2.cloned.1.call-update) | async-done | bytes 294928 | tf_op jit(solution)/shard_map/reduce_scatter | solution.py:123
  (63 shorter events, 7.4 us)
Async XLA Ops:
  7.2 9.0 %copy-start.6 = (bf16[1,128,1536]{2,1,0:T(8,128)(2,1)S(1)}, bf16[1,128,1536]{2,1,0:T(8,128)(2,1)}, u32[]{:S(2)}) copy-start(bf16[1,128,1536]{2,1,0:T(8,128)(2,1)} %param.16) | copy-start | bytes 1179652
  7.2 59.2 %all-gather.2.cloned.1.call-start = ((), (), s32[]{:S(2)}) async-start(), calls=%async_computation.1 | async-start | bytes 5013504 | tf_op jit(solution)/shard_map/all_gather | solution.py:73
  7.9 273.8 %reduce-scatter.2.cloned.1.call-start = ((), (), s32[]{:S(2)}) async-start(), calls=%async_computation.2 | async-start | bytes 5013504 | tf_op jit(solution)/shard_map/reduce_scatter | solution.py:123
  9.8 6.3 %copy-start.11 = (f32[128]{0:T(128)}, f32[128]{0:T(128)S(1)}, u32[]{:S(2)}) copy-start(f32[128]{0:T(128)S(1)} %add_rsqrt_fusion) | copy-start | bytes 1540
  11.0 5.2 %collective-permute-start = (bf16[128,1536]{1,0:T(8,128)(2,1)S(1)}, bf16[128,1536]{1,0:T(8,128)(2,1)S(1)}, u32[]{:S(2)}, u32[]{:S(2)}) collective-permute-start(bf16[128,1536]{1,0:T(8,128)(2,1)S(1)} %fusion.144), channel_id=1, source_target_pairs={{0,1},{1,2},{2,3},{4,5},{5,6},{6,7},{8,9},{9,10},{10,11},{12,13},{... | collective-permute-start | bytes 1179656 | tf_op jit(solution)/shard_map/ppermute | solution.py:16
  16.1 50.3 %copy-start.14 = (pred[256]{0:T(512)(128)(4,1)}, pred[256]{0:T(512)(128)(4,1)S(1)}, u32[]{:S(2)}) copy-start(pred[256]{0:T(512)(128)(4,1)S(1)} %concatenate.6) | copy-start | bytes 772
  16.2 50.2 %copy-start.10 = (f32[1,1536]{1,0:T(1,128)S(1)}, f32[1,1536]{1,0:T(1,128)}, u32[]{:S(2)}) copy-start(f32[1,1536]{1,0:T(1,128)} %param.18) | copy-start | bytes 18436
  66.4 4.9 %copy-start = (bf16[1,1,128,1536]{3,2,1,0:T(8,128)(2,1)S(1)}, bf16[1,1,128,1536]{3,2,1,0:T(8,128)(2,1)}, u32[]{:S(2)}) copy-start(bf16[1,1,128,1536]{3,2,1,0:T(8,128)(2,1)} %param.15) | copy-start | bytes 1179652
  67.3 4.2 %copy-start.7 = (bf16[1,128,1536]{2,1,0:T(8,128)(2,1)S(1)}, bf16[1,128,1536]{2,1,0:T(8,128)(2,1)}, u32[]{:S(2)}) copy-start(bf16[1,128,1536]{2,1,0:T(8,128)(2,1)} %param.16) | copy-start | bytes 1179652
  67.3 4.2 %copy-start.12 = (f32[128]{0:T(128)S(1)}, f32[128]{0:T(128)}, u32[]{:S(2)}) copy-start(f32[128]{0:T(128)} %copy-done.11) | copy-start | bytes 1540
  67.3 4.0 %collective-permute-start.1 = (bf16[128,1536]{1,0:T(8,128)(2,1)}, bf16[128,1536]{1,0:T(8,128)(2,1)S(1)}, u32[]{:S(2)}, u32[]{:S(2)}) collective-permute-start(bf16[128,1536]{1,0:T(8,128)(2,1)} %get-tuple-element.121), channel_id=1, source_target_pairs={{1,0},{2,1},{3,2},{5,4},{6,5},{7,6},{9,8},{10,9},{11,10},{13,12},{... | collective-permute-start | bytes 1179656 | tf_op jit(solution)/shard_map/ppermute | solution.py:16
  71.9 59.6 %copy-start.8 = (bf16[128,1536]{1,0:T(8,128)(2,1)}, bf16[128,1536]{1,0:T(8,128)(2,1)S(1)}, u32[]{:S(2)}) copy-start(bf16[128,1536]{1,0:T(8,128)(2,1)S(1)} %fusion.149) | copy-start | bytes 1179652
  71.9 59.6 %collective-permute-start.2 = (bf16[128,1536]{1,0:T(8,128)(2,1)S(1)}, bf16[128,1536]{1,0:T(8,128)(2,1)}, u32[]{:S(2)}, u32[]{:S(2)}) collective-permute-start(bf16[128,1536]{1,0:T(8,128)(2,1)S(1)} %fusion.149), channel_id=1, source_target_pairs={{16,0},{17,1},{18,2},{19,3},{20,4},{21,5},{22,6},{23,7},{24,8},{25... | collective-permute-start | bytes 1179656 | tf_op jit(solution)/shard_map/ppermute | solution.py:16
  136.2 0.6 copy-start.15
  189.0 5.8 %copy-start.3 = (bf16[128,1536]{1,0:T(8,128)(2,1)}, bf16[128,1536]{1,0:T(8,128)(2,1)S(1)}, u32[]{:S(2)}) copy-start(bf16[128,1536]{1,0:T(8,128)(2,1)S(1)} %reshape.64) | copy-start | bytes 1179652 | tf_op jit(solution)/shard_map/cond
  198.9 1.0 copy-start.4
  203.4 8.4 %copy-start.9 = (bf16[128,1536]{1,0:T(8,128)(2,1)S(1)}, bf16[128,1536]{1,0:T(8,128)(2,1)}, u32[]{:S(2)}) copy-start(bf16[128,1536]{1,0:T(8,128)(2,1)} %copy-done.8) | copy-start | bytes 1179652
  203.4 8.4 %copy-start.13 = (f32[128]{0:T(128)S(1)}, f32[128]{0:T(128)}, u32[]{:S(2)}) copy-start(f32[128]{0:T(128)} %copy-done.11) | copy-start | bytes 1540
  203.4 8.1 %collective-permute-start.3 = (bf16[128,1536]{1,0:T(8,128)(2,1)S(1)}, bf16[128,1536]{1,0:T(8,128)(2,1)S(1)}, u32[]{:S(2)}, u32[]{:S(2)}) collective-permute-start(bf16[128,1536]{1,0:T(8,128)(2,1)S(1)} %get-tuple-element.123), channel_id=1, source_target_pairs={{1,0},{2,1},{3,2},{5,4},{6,5},{7,6},{9,8},{10,9},{11,10},{13,12},{... | collective-permute-start | bytes 1179656 | tf_op jit(solution)/shard_map/ppermute | solution.py:16
Sparse Core Ops, SparseCore 0:
  10.3 56.0 all-gather.1
  203.5 78.0 reduce-scatter.1
where the time goes:
time: 290 us; the launch traced here: 289 us
  waiting for transfers between devices  185 us (64%)
  matrix products  62.2 us (21%)
  between operations  16.3 us (6%)
  local copies, waits for them, and re-layouts  10.4 us (4%)
  other arithmetic  7.94 us (3%)
  starting transfers between devices  6.6 us (2%)
    reduce_scatter x1, waiting for transfers between devices, per_device(): lax.psum_scatter(lax.dot_general(normed, kept_grad, (((0,), (0,)), ((), (...  67.5 us
    ppermute x4, waiting for transfers between devices, from_behind(): lax.ppermute(value, axis, [(source, source + steps) for source in range(i...  66.8 us
    all_gather x1, waiting for transfers between devices, per_device(): weights = lax.all_gather(w_query, ('fsdp', 'seq'), axis=1, tiled=True)[0]  49.8 us
    dot_general x6, matrix products, per_group(): jnp.einsum('gij,gid->gjd', score_grad, query_part, preferred_element_type...  17.7 us
    dot_general x6, matrix products, per_group(): jnp.einsum('gij,gid->gjd', probs_low, grad_part, preferred_element_type=j...  13.8 us
    dot_general x6, matrix products, per_group(): jnp.einsum('gij,gjd->gid', score_grad, key_part, preferred_element_type=j...  12.8 us
    ppermute x4, starting transfers between devices, from_behind(): lax.ppermute(value, axis, [(source, source + steps) for source in range(i...  6.52 us
    sub x6, matrix products, per_group(): exp_scores = jnp.exp(scores - row_max)  5.95 us
  transfers between devices with their start and end apart: 6, of which 5 were waited for; matrix products, arithmetic and copies ran while one was open for 3% of the time, Pallas kernels for 0%

commit v1 on v0

v1 whole, which is shorter than its diff:
```python
import jax
import jax.numpy as jnp
from jax import lax
from jax.experimental import pallas as pl
from jax.experimental.pallas import tpu as pltpu
from jax.sharding import PartitionSpec as P

HDIM = 128
SCALE = HDIM ** (-0.5)
EPS = 1e-06
NEG = -1e30
BF = jnp.bfloat16
F32 = jnp.float32
VLIMIT = 16 * 1024 * 1024

NN = (((1,), (0,)), ((), ()))
NT = (((1,), (1,)), ((), ()))
TN = (((0,), (0,)), ((), ()))


def mm(a, b, dims):
    return lax.dot_general(a, b, dims, preferred_element_type=F32)


def sds(shape, dtype):
    return jax.ShapeDtypeStruct(shape, dtype)


def call(kernel, outs, flops, name, kept, links, *args, scratch=()):
    nbytes = sum(s.size * s.dtype.itemsize for s in outs) + sum(a.size * a.dtype.itemsize for a in args)
    return pl.pallas_call(
        kernel,
        out_shape=outs,
        in_specs=[pl.BlockSpec(memory_space=pltpu.SMEM)] * 2
        + [pl.BlockSpec(memory_space=pltpu.VMEM)] * len(args),
        out_specs=[pl.BlockSpec(memory_space=pltpu.VMEM)] * len(outs),
        scratch_shapes=list(scratch),
        compiler_params=pltpu.CompilerParams(vmem_limit_bytes=VLIMIT),
        cost_estimate=pl.CostEstimate(flops=flops, bytes_accessed=nbytes, transcendentals=0),
        name=name,
    )(kept, links, *args)


def where_am_i(kept, links):
    section = lax.axis_index("section")
    side = lax.rem(section, 2)
    hi = section - side + 1
    linked = jnp.logical_and(links[0, 0] > 0, lax.axis_index("seq") > 0)
    return side, linked, kept[0, hi] > 0, kept[0, hi - 1] > 0


def pick(side, value, half, other=False):
    first = value[:, :half]
    second = value[:, half:]
    use_first = (side == 1) if other else (side == 0)
    return jnp.where(use_first, first, second)


def hi_of(side, own, other):
    return jnp.where(side == 1, own[...], other[...])


def lo_of(side, own, other):
    return jnp.where(side == 1, other[...], own[...])


def inverse_rms(x):
    return lax.rsqrt(jnp.mean(x * x, axis=-1, keepdims=True) + EPS)


def select_kernel(kept, links, own, other, hi, lo):
    side, _, _, _ = where_am_i(kept, links)
    hi[...] = hi_of(side, own, other)
    lo[...] = lo_of(side, own, other)


def normalize_kernel(offsets, rows, kept, links, acts, acts_in, vecs, vecs_in, dy_full, *outs):
    normed, keys, parts = outs[:2], outs[2], outs[3 : 3 + len(offsets)]
    dy, turned = outs[-2], outs[-1]
    tile, half = dy.shape
    seqs = len(offsets)
    block = parts[0].shape[0] // 2
    side, _, _, _ = where_am_i(kept, links)
    seq = lax.axis_index("seq")
    for which, select in enumerate((hi_of, lo_of)):
        x = select(side, acts, acts_in).astype(F32)
        gain = select(side, vecs, vecs_in)[:1]
        value = (x * inverse_rms(x) * gain).astype(BF)
        normed[which][...] = value
        keys[which * tile : (which + 1) * tile, :] = pick(side, value, half)
        turned[...] = value.astype(F32).T.astype(BF)
        for part, offset in zip(parts, offsets):
            for f in range(block // rows):
                source = pl.multiple_of((f * seqs + jnp.bitwise_xor(seq, offset)) * rows, rows)
                target = which * block + f * rows
                part[target : target + rows, :] = turned[pl.ds(source, rows), :]
    dy[...] = pick(side, dy_full[...], half)


def head_probs(query, keys, linked):
    scores = mm(query, keys, NT) * SCALE
    column = lax.broadcasted_iota(jnp.int32, scores.shape, 1)
    scores = jnp.where(jnp.logical_or(column >= scores.shape[1] // 2, linked), scores, NEG)
    exps = jnp.exp(scores - jnp.max(scores, axis=-1, keepdims=True))
    return exps / jnp.sum(exps, axis=-1, keepdims=True)


def head_backward(query, keys, grads, probs):
    prob_grad = mm(grads, keys, NT)
    row_delta = jnp.sum(probs * prob_grad, axis=-1, keepdims=True)
    score_grad = (probs * (prob_grad - row_delta) * SCALE).astype(BF)
    query_grad = mm(score_grad, keys, NN).astype(BF)
    key_grad = mm(
        jnp.concatenate([score_grad, probs.astype(BF)], axis=0),
        jnp.concatenate([query, grads], axis=0),
        TN,
    )
    return query_grad, key_grad


def pieces(column):
    high = column.astype(BF)
    rest = column - high.astype(F32)
    middle = rest.astype(BF)
    low = (rest - middle.astype(F32)).astype(BF)
    rows = column.shape[0]
    lane = lax.broadcasted_iota(jnp.int32, (rows, HDIM), 1)
    high, middle, low = [jnp.broadcast_to(p.astype(F32), (rows, HDIM)) for p in (high, middle, low)]
    value = jnp.where(lane == 0, high, jnp.where(lane == 1, middle, jnp.where(lane == 2, low, 0.0)))
    return value.astype(BF)


def unpieces(block):
    return jnp.sum(block.astype(F32), axis=-1, keepdims=True)


def heads_of(half):
    return [slice(h * HDIM, (h + 1) * HDIM) for h in range(half // HDIM)]


def pairs_of(half):
    step = 2 * HDIM if half % (2 * HDIM) == 0 else HDIM
    return [slice(c, c + step) for c in range(0, half, step)]


def forward_kernel(which, places, rows, kept, links, normed, left_keys, own_keys, *rest):
    blocks = rest[: len(places)]
    query_out, probs_out, weights = rest[len(places) :]
    tile, half = query_out.shape
    token = slice(which * tile, (which + 1) * tile)
    _, linked, _, _ = where_am_i(kept, links)
    fsdps = lax.axis_size("fsdp")
    seqs = lax.axis_size("seq")
    fsdp, seq = lax.axis_index("fsdp"), lax.axis_index("seq")
    for block, place in zip(blocks, places):
        for index, (shift, offset) in enumerate(place):
            f = lax.rem(fsdp - shift + fsdps, fsdps)
            target = pl.multiple_of((f * seqs + jnp.bitwise_xor(seq, offset)) * rows, rows)
            weights[pl.ds(target, rows), :] = block[index * rows : (index + 1) * rows, :]
    tokens = normed[...]
    for cols in pairs_of(half):
        query = mm(tokens, weights[:, cols], NN).astype(BF)
        query_out[:, cols] = query
        for sub in heads_of(cols.stop - cols.start):
            at = slice(cols.start + sub.start, cols.start + sub.stop)
            keys = jnp.concatenate([left_keys[token, at], own_keys[token, at]], axis=0)
            start = at.start // HDIM * tile
            probs_out[start : start + tile, :] = head_probs(query[:, sub], keys, linked)


def upper_kernel(
    kept, links, dy, acts, acts_in, vecs, vecs_in, query, probs, weights, left_keys, own_keys,
    qg, own, msg, leftward, leftsum,
):
    tile, half = dy.shape
    side, _, keep, _ = where_am_i(kept, links)
    gate = pick(side, hi_of(side, vecs, vecs_in)[1:2], half)
    gain = hi_of(side, vecs, vecs_in)[:1]
    grads = (gate * dy[...].astype(F32)).astype(BF)
    left_total = jnp.zeros((tile, 1), F32)
    for at in heads_of(half):
        left = left_keys[:tile, at]
        keys = jnp.concatenate([left, own_keys[:tile, at]], axis=0)
        start = at.start // HDIM * tile
        query_grad, key_grad = head_backward(query[:, at], keys, grads[:, at], probs[start : start + tile, :])
        qg[:, at] = jnp.where(keep, query_grad, jnp.zeros_like(query_grad))
        back = key_grad[:tile].astype(BF)
        leftward[:, at] = back
        left_total += jnp.sum(back.astype(F32) * left.astype(F32), axis=-1, keepdims=True)
        own[:, at] = key_grad[tile:]
    leftsum[...] = jnp.broadcast_to(left_total, leftsum.shape)
    part = mm(qg[...], weights[...], NT)
    x_gain = hi_of(side, acts, acts_in).astype(F32) * gain
    total = jnp.sum(x_gain * part, axis=-1, keepdims=True)
    total += jnp.sum(pick(side, x_gain, half) * own[...], axis=-1, keepdims=True)
    own[...] += pick(side, part, half)
    msg[:, :half] = pick(side, part, half, other=True).astype(BF)
    msg[:, half:] = pieces(total)


def lower_kernel(
    kept, links, own, msg, msg_in, left_in, sum_other, acts, acts_in, vecs, vecs_in, dy,
    query, probs, left_keys, own_keys, dy_out, qg, key_own, leftward,
):
    tile, half = dy.shape
    side, _, keep_hi, keep_lo = where_am_i(kept, links)
    x = hi_of(side, acts, acts_in).astype(F32)
    inv = inverse_rms(x)
    left = left_in[...].astype(F32)
    x_mine = pick(side, x, half)
    gain = pick(side, hi_of(side, vecs, vecs_in)[:1], half)
    gate_lo = pick(side, lo_of(side, vecs, vecs_in)[1:2], half)
    total = unpieces(msg[:, half:]) + unpieces(msg_in[:, half:])
    total += jnp.sum(x_mine * gain * left, axis=-1, keepdims=True)
    total += sum_other[:, :1] / inv
    mean_term = total / x.shape[1]
    scaled = (own[...] + left + msg_in[:, :half].astype(F32)) * gain
    change = inv * (scaled - x_mine * inv * inv * mean_term)
    dy_old = dy[...]
    dy_new = jnp.where(keep_hi, (dy_old.astype(F32) + change).astype(BF), dy_old)
    dy_out[...] = dy_new
    grads = (gate_lo * dy_new.astype(F32)).astype(BF)
    for at in heads_of(half):
        keys = jnp.concatenate([left_keys[tile:, at], own_keys[tile:, at]], axis=0)
        start = at.start // HDIM * tile
        query_grad, key_grad = head_backward(query[:, at], keys, grads[:, at], probs[start : start + tile, :])
        qg[:, at] = jnp.where(keep_lo, query_grad, jnp.zeros_like(query_grad))
        leftward[:, at] = key_grad[:tile].astype(BF)
        key_own[:, at] = key_grad[tile:]


def project_kernel(kept, links, qg, weights, key_own, left_in, part_out, msg):
    half = qg.shape[1]
    side, _, _, _ = where_am_i(kept, links)
    part = mm(qg[...], weights[...], NT)
    mine = key_own[...] + left_in[...].astype(F32)
    first = part[:, :half] + jnp.where(side == 0, mine, 0.0)
    second = part[:, half:] + jnp.where(side == 1, mine, 0.0)
    part_out[:, :half] = first
    part_out[:, half:] = second
    msg[:, :half] = first.astype(BF)
    msg[:, half:] = second.astype(BF)


def finish_kernel(kept, links, part, msg_in, acts, acts_in, vecs, vecs_in, dy_mine, dy_in, out):
    side, _, _, keep_lo = where_am_i(kept, links)
    mine, other = dy_mine[...], dy_in[...]
    first = jnp.where(side == 0, mine, other)
    second = jnp.where(side == 0, other, mine)
    dy = jnp.concatenate([first, second], axis=1)
    x = lo_of(side, acts, acts_in).astype(F32)
    gain = lo_of(side, vecs, vecs_in)[:1]
    inv = inverse_rms(x)
    scaled = (part[...] + msg_in[...].astype(F32)) * gain
    mean_term = jnp.mean(x * scaled, axis=-1, keepdims=True)
    change = inv * (scaled - x * inv * inv * mean_term)
    updated = jnp.where(keep_lo, (dy.astype(F32) + change).astype(BF), dy)
    out[...] = jnp.where(side == 0, updated, dy)


def weight_grad_kernel(which, count, rows, kept, links, *refs):
    parts, grads, outs = refs[:count], refs[count : 2 * count], refs[2 * count :]
    fsdps = lax.axis_size("fsdp")
    fsdp = lax.axis_index("fsdp")
    block = parts[0].shape[0] // 2
    left = jnp.concatenate([p[which * block : (which + 1) * block, :] for p in parts], axis=1)
    right = jnp.concatenate([g[...] for g in grads], axis=0)
    scratch = outs[fsdps]
    scratch[...] = mm(left, right, NN).astype(BF)
    for shift in range(fsdps):
        source = pl.multiple_of(lax.rem(fsdp + shift, fsdps) * rows, rows)
        outs[shift][...] = scratch[pl.ds(source, rows), :]


def add_kernel(count, kept, links, *refs):
    hi_blocks, lo_blocks, (mine, theirs) = refs[:count], refs[count : 2 * count], refs[2 * count :]
    side, _, _, _ = where_am_i(kept, links)
    sums = []
    for blocks in (hi_blocks, lo_blocks):
        total = blocks[0][...].astype(F32)
        for block in blocks[1:]:
            total += block[...].astype(F32)
        sums.append(total.astype(BF))
    mine[...] = jnp.where(side == 1, sums[0], sums[1])
    theirs[...] = jnp.where(side == 1, sums[1], sums[0])


def tied(value, *others):
    return lax.optimization_barrier((value, *others))[0]


def per_device(acts, grad_out, gain, gate, w_query, kept, links):
    sections = lax.axis_size("section")
    fsdps = lax.axis_size("fsdp")
    seqs = lax.axis_size("seq")
    section_idx = lax.axis_index("section")
    seq_idx = lax.axis_index("seq")
    side = section_idx % 2
    tile, dim = acts.shape[2:]
    rows = w_query.shape[1]
    half = dim // 2
    swap_pairs = [(i, i ^ 1) for i in range(sections)]
    bits = [1 << b for b in reversed(range(seqs.bit_length() - 1))]
    offsets = [0]
    for bit in bits:
        offsets = offsets + [o ^ bit for o in offsets]

    def swap(value):
        return lax.ppermute(value, "section", swap_pairs)

    def across(value, offset):
        return lax.ppermute(value, "seq", [(s, s ^ offset) for s in range(seqs)])

    def along(value, shift):
        return lax.ppermute(value, "fsdp", [(f, (f + shift) % fsdps) for f in range(fsdps)])

    def run(kernel, outs, flops, name, *args, scratch=()):
        return call(kernel, outs, flops, name, kept, links, *args, scratch=scratch)

    first, second = w_query[0][:, :half], w_query[0][:, half:]
    w_own, w_theirs = jnp.where(side == 0, first, second), jnp.where(side == 0, second, first)
    w_other = swap(w_theirs)
    acts_own = acts[0, 0]
    acts_in = swap(acts_own)
    vecs = jnp.concatenate([gain, gate], axis=0)
    vecs_in = swap(vecs)
    top = bits[0]

    w_hi, w_lo = run(select_kernel, [sds((rows, half), BF)] * 2, rows * half, "select_w", w_own, w_other)
    matmul_flops = 2 * tile * dim * half
    head_flops = 2 * tile * 2 * tile * half
    part_shape = sds((2 * fsdps * rows, tile), BF)

    normalized = run(
        lambda *refs: normalize_kernel(offsets, rows, *refs),
        [sds((tile, dim), BF)] * 2 + [sds((2 * tile, half), BF)] + [part_shape] * seqs + [sds((tile, half), BF)],
        20 * tile * dim,
        "normalize",
        acts_own, acts_in, vecs, vecs_in, grad_out[0],
        scratch=[pltpu.VMEM((dim, tile), BF)],
    )
    normed_hi, normed_lo, keys = normalized[:3]
    parts = normalized[3 : 3 + seqs]
    incoming = normalized[-1]
    right_pairs = [(t, t + 1) for t in range(seqs - 1)]
    left_pairs = [(t + 1, t) for t in range(seqs - 1)]
    diagonal_pairs = [
        (s * seqs + t + 1, (s ^ 1) * seqs + t) for s in range(sections) for t in range(seqs - 1)
    ]
    left = lax.ppermute(keys, "seq", right_pairs)

    def over_fsdp(shard):
        return [shard] + [along(shard, shift) for shift in range(1, fsdps)]

    def over_seq(near, after=None):
        far = []
        for index, block in enumerate(near):
            if after is not None and index == fsdps - 1:
                block = tied(block, after)
            far.append(across(block, top))
        held = [(jnp.concatenate(near, axis=0), 0), (jnp.concatenate(far, axis=0), top)]
        for bit in bits[1:]:
            held = held + [(across(value, bit), offset ^ bit) for value, offset in held]
        places = [[(shift, offset) for shift in range(fsdps)] for _, offset in held]
        return far, [value for value, _ in held], places

    near_hi = over_fsdp(w_hi)
    _, blocks_hi, places = over_seq(near_hi, after=normed_hi)
    near_lo = over_fsdp(tied(w_lo, *near_hi[1:]))
    far_lo, blocks_lo, _ = over_seq(near_lo)

    def forward(name, which, normed, blocks):
        return run(
            lambda *refs: forward_kernel(which, places, rows, *refs),
            [sds((tile, half), BF), sds((half // HDIM * tile, 2 * tile), F32), sds((dim, half), BF)],
            matmul_flops + head_flops,
            name, normed, left, keys, *blocks,
        )

    query_hi, probs_hi, weights_hi = forward("forward_hi", 0, normed_hi, blocks_hi)
    query_lo, probs_lo, weights_lo = forward("forward_lo", 1, normed_lo, blocks_lo)

    parts_in = [parts[0]] + [
        across(tied(part, *far_lo), offset) for part, offset in zip(parts[1:], offsets[1:])
    ]

    kept_state = None
    for tick in range(sections // 2):
        qg_hi, own, msg, leftward, leftsum = run(
            upper_kernel,
            [
                sds((tile, half), BF),
                sds((tile, half), F32),
                sds((tile, half + HDIM), BF),
                sds((tile, half), BF),
                sds((tile, HDIM), F32),
            ],
            matmul_flops + 4 * head_flops,
            "upper", incoming, acts_own, acts_in, vecs, vecs_in, query_hi, probs_hi, weights_hi, left, keys,
        )
        msg_in = tied(swap(msg), *parts_in)
        left_in = lax.ppermute(leftward, "seq", left_pairs)
        sum_other = lax.ppermute(leftsum, ("section", "seq"), diagonal_pairs)
        dy_mid, qg_lo, key_own, leftward_lo = run(
            lower_kernel,
            [sds((tile, half), BF), sds((tile, half), BF), sds((tile, half), F32), sds((tile, half), BF)],
            4 * head_flops,
            "lower",
            own, msg, msg_in, left_in, sum_other, acts_own, acts_in, vecs, vecs_in, incoming,
            query_lo, probs_lo, left, keys,
        )
        left_in_lo = lax.ppermute(leftward_lo, "seq", left_pairs)
        dy_in = swap(dy_mid)
        part_lo, msg_lo = run(
            project_kernel, [sds((tile, dim), F32), sds((tile, dim), BF)], matmul_flops, "project_lo",
            qg_lo, weights_lo, key_own, left_in_lo,
        )
        msg_lo_in = lax.ppermute(msg_lo, "section", [(i + 1, i) for i in range(0, sections, 2)])
        (updated,) = run(
            finish_kernel, [sds((tile, dim), BF)], 20 * tile * dim, "finish",
            part_lo, msg_lo_in, acts_own, acts_in, vecs, vecs_in, dy_mid, dy_in,
        )
        state = (updated, qg_hi, qg_lo)
        if kept_state is None:
            kept_state = state
        else:
            active = section_idx // 2 == sections // 2 - 1 - tick
            kept_state = jax.tree.map(lambda new, old: jnp.where(active, new, old), state, kept_state)
        if tick + 1 < sections // 2:
            to_low = lax.ppermute(updated[:, :half], "section", [(i, i - 2) for i in range(2, sections, 2)])
            to_high = lax.ppermute(updated[:, half:], "section", [(i, i - 1) for i in range(2, sections, 2)])
            incoming = jnp.where(side == 0, to_low, to_high)
    result, qg_hi, qg_lo = kept_state

    def weight_grad(name, which, query_grad, after):
        gathered = [query_grad]
        for bit in bits:
            arrived = across(jnp.concatenate(gathered, axis=0) if len(gathered) > 1 else gathered[0], bit)
            gathered = gathered + [arrived[i * tile : (i + 1) * tile] for i in range(len(gathered))]
        if after is not None:
            gathered[-1] = tied(gathered[-1], after)
        terms = run(
            lambda *refs: weight_grad_kernel(which, seqs, rows, *refs),
            [sds((rows, half), BF)] * fsdps,
            2 * fsdps * rows * seqs * tile * half,
            name, *parts_in, *gathered,
            scratch=[pltpu.VMEM((fsdps * rows, half), BF)],
        )
        return [terms[0]] + [along(terms[shift], shift) for shift in range(1, fsdps)]

    terms_hi = weight_grad("weight_grad_hi", 0, qg_hi, qg_lo)
    terms_lo = weight_grad("weight_grad_lo", 1, qg_lo, None)
    terms_lo[-1] = tied(terms_lo[-1], result)
    mine, theirs = run(
        lambda *refs: add_kernel(fsdps, *refs),
        [sds((rows, half), BF)] * 2, 20 * rows * half, "add_clips", *terms_hi, *terms_lo,
    )
    other = swap(theirs)
    first = jnp.where(side == 0, mine, other)
    second = jnp.where(side == 0, other, mine)
    grad_rows = jnp.concatenate([first, second], axis=1)
    return (result[None, None], grad_rows[None])


def solution(mesh):
    placed = (
        P("section", "fsdp", "seq", None),
        P("fsdp", "seq", None),
        P("section", None),
        P("section", None),
        P("section", ("fsdp", "seq"), None),
        P("fsdp", None),
        P("fsdp", "seq"),
    )
    return jax.shard_map(
        per_device,
        mesh=mesh,
        in_specs=placed,
        out_specs=(P("section", "fsdp", "seq", None), P("section", ("fsdp", "seq"), None)),
        check_vma=False,
    )
```

time: 290 us -> 136 us (0.47)
  waiting for transfers between devices: 185 us -> 47.6 us
  matrix products: 62.2 us -> 0 us
  starting transfers between devices: 6.6 us -> 64.9 us
  Pallas kernels: 0 us -> 17.5 us
  between operations: 16.3 us -> 1.68 us
  local copies, waits for them, and re-layouts: 10.4 us -> 0.9 us
  other arithmetic: 7.94 us -> 2.61 us
    reduce_scatter x1 -> x0, waiting for transfers between devices: 67.5 us -> none  [per_device(): lax.psum_scatter(lax.dot_general(normed, kept_grad, (((0,), (0,)), ((), (...]
    ppermute x4 -> x42, starting transfers between devices: 6.52 us -> 64.9 us  [the longest x19 25.1 us: across(): return lax.ppermute(value, 'seq', [(s, s ^ offset) for s in range(seqs)])]
    dot_general x27 -> x0, matrix products: 56.2 us -> none  [the longest x6 17.7 us: per_group(): jnp.einsum('gij,gid->gjd', score_grad, query_part, preferred_element_type...]
    all_gather x1 -> x0, waiting for transfers between devices: 49.8 us -> none  [per_device(): weights = lax.all_gather(w_query, ('fsdp', 'seq'), axis=1, tiled=True)[0]]
    ppermute x4 -> x42, waiting for transfers between devices: 66.8 us -> 47.6 us  [the longest x12 18.2 us: along(): lax.ppermute(value, 'fsdp', [(f, (f + shift) % fsdps) for f in range(fsdp...]
    pallas_call x0 -> x11, Pallas kernels: none -> 17.5 us  [call(): pl.pallas_call(kernel, out_shape=outs, in_specs=[pl.BlockSpec(memory_spac...]
    slice x5 -> x2, local copies, waits for them, and re-layouts: 6.2 us -> 0.05 us  [weight_grad(): arrived[i * tile:(i + 1) * tile]]
    sub x6 -> x0, matrix products: 5.95 us -> none  [per_group(): exp_scores = jnp.exp(scores - row_max)]
  transfers between devices with their start and end apart: 6 -> 42, of which waited for: 5 -> 15; matrix products, arithmetic and copies ran while one was open for 3% -> 1% of each run, Pallas kernels for 0% -> 11%
where the time goes in v1:
time: 136 us; the launch traced here: 135 us
  starting transfers between devices  64.9 us (48%)
  waiting for transfers between devices  47.6 us (35%)
  Pallas kernels  17.5 us (13%)
  other arithmetic  2.61 us (2%)
  between operations  1.68 us (1%)
    ppermute x19, starting transfers between devices, across(): return lax.ppermute(value, 'seq', [(s, s ^ offset) for s in range(seqs)])  25.1 us
    ppermute x12, starting transfers between devices, along(): lax.ppermute(value, 'fsdp', [(f, (f + shift) % fsdps) for f in range(fsdp...  22.8 us
    ppermute x12, waiting for transfers between devices, along(): lax.ppermute(value, 'fsdp', [(f, (f + shift) % fsdps) for f in range(fsdp...  18.2 us
    ppermute x19, waiting for transfers between devices, across(): return lax.ppermute(value, 'seq', [(s, s ^ offset) for s in range(seqs)])  18 us
    pallas_call x11, Pallas kernels, call(): pl.pallas_call(kernel, out_shape=outs, in_specs=[pl.BlockSpec(memory_spac...  17.5 us
    ppermute x6, starting transfers between devices, swap(): return lax.ppermute(value, 'section', swap_pairs)  10.5 us
    ppermute x6, waiting for transfers between devices, swap(): return lax.ppermute(value, 'section', swap_pairs)  8.26 us
  transfers between devices with their start and end apart: 42, of which 15 were waited for; matrix products, arithmetic and copies ran while one was open for 1% of the time, Pallas kernels for 11%

profile of v1, /device:TPU:0, one launch (start us, length us, event | category | flops | bytes accessed | tf_op | source)
XLA Modules:
  0.0 135.2 jit_solution(17043238320563681552)
XLA Ops:
  1.7 3.0 %collective-permute-start.3 = (bf16[96,768]{1,0:T(8,128)(2,1)S(1)}, bf16[96,768]{1,0:T(8,128)(2,1)S(1)}, u32[]{:S(2)}, u32[]{:S(2)}) collective-permute-start(bf16[96,768]{1,0:T(8,128)(2,1)S(1)} %get-tuple-element.98), channel_id=1, source_target_pairs={{0,16},{16,0},{1,17},{17,1},{2,18},{18,2},{3,19},{19,3},{4,20},{20... | collective-permute-start | bytes 442376 | tf_op jit(solution)/shard_map/ppermute | solution.py:309
  5.5 3.9 %collective-permute-done.3.other = bf16[96,768]{1,0:T(8,128)(2,1)S(1)} collective-permute-done((bf16[96,768]{1,0:T(8,128)(2,1)S(1)}, bf16[96,768]{1,0:T(8,128)(2,1)S(1)}, u32[]{:S(2)}, u32[]{:S(2)}) %collective-permute-start.3) | collective-permute-done | bytes 147488 | tf_op jit(solution)/shard_map/ppermute | solution.py:309
  10.7 2.2 %collective-permute-start.4 = (bf16[96,768]{1,0:T(8,128)(2,1)S(1)}, bf16[96,768]{1,0:T(8,128)(2,1)S(1)}, u32[]{:S(2)}, u32[]{:S(2)}) collective-permute-start(bf16[96,768]{1,0:T(8,128)(2,1)S(1)} %get-tuple-element.50), channel_id=1, source_target_pairs={{0,4},{4,8},{8,12},{12,0},{1,5},{5,9},{9,13},{13,1},{2,6},{6,10},{... | collective-permute-start | bytes 442376 | tf_op jit(solution)/shard_map/ppermute | solution.py:315
  12.9 2.6 %collective-permute-start.5 = (bf16[96,768]{1,0:T(8,128)(2,1)S(1)}, bf16[96,768]{1,0:T(8,128)(2,1)S(1)}, u32[]{:S(2)}, u32[]{:S(2)}) collective-permute-start(bf16[96,768]{1,0:T(8,128)(2,1)S(1)} %get-tuple-element.50), channel_id=1, source_target_pairs={{0,8},{4,12},{8,0},{12,4},{1,9},{5,13},{9,1},{13,5},{2,10},{6,14},... | collective-permute-start | bytes 442376 | tf_op jit(solution)/shard_map/ppermute | solution.py:315
  15.4 1.3 collective-permute-start.6
  17.5 1.6 %collective-permute-start.1 = (f32[2,1536]{1,0:T(2,128)S(1)}, f32[2,1536]{1,0:T(2,128)S(1)}, u32[]{:S(2)}, u32[]{:S(2)}) collective-permute-start(f32[2,1536]{1,0:T(2,128)S(1)} %pad_maximum_fusion.2.refs_4_.vecs), channel_id=1, source_target_pairs={{0,16},{16,0},{1,17},{17,1},{2,18},{18,2},{3,19},{19,3},{4,20},{20... | collective-permute-start | bytes 36872 | tf_op jit(solution)/shard_map/ppermute | solution.py:309
  19.8 1.7 %collective-permute-start.7 = (bf16[96,768]{1,0:T(8,128)(2,1)S(1)}, bf16[96,768]{1,0:T(8,128)(2,1)S(1)}, u32[]{:S(2)}, u32[]{:S(2)}) collective-permute-start(bf16[96,768]{1,0:T(8,128)(2,1)S(1)} %get-tuple-element.50), channel_id=1, source_target_pairs={{0,2},{1,3},{2,0},{3,1},{4,6},{5,7},{6,4},{7,5},{8,10},{9,11},{10,... | collective-permute-start | bytes 442376 | tf_op jit(solution)/shard_map/ppermute | solution.py:312
  21.5 1.7 %collective-permute-done.5 = bf16[96,768]{1,0:T(8,128)(2,1)S(1)} collective-permute-done((bf16[96,768]{1,0:T(8,128)(2,1)S(1)}, bf16[96,768]{1,0:T(8,128)(2,1)S(1)}, u32[]{:S(2)}, u32[]{:S(2)}) %collective-permute-start.5) | collective-permute-done | bytes 147488 | tf_op jit(solution)/shard_map/ppermute | solution.py:315
  23.2 1.6 %collective-permute-start.14 = (bf16[96,768]{1,0:T(8,128)(2,1)S(1)}, bf16[96,768]{1,0:T(8,128)(2,1)S(1)}, u32[]{:S(2)}, u32[]{:S(2)}) collective-permute-start(bf16[96,768]{1,0:T(8,128)(2,1)S(1)} %get-tuple-element.60), channel_id=1, source_target_pairs={{0,2},{1,3},{2,0},{3,1},{4,6},{5,7},{6,4},{7,5},{8,10},{9,11},{10,... | collective-permute-start | bytes 442376 | tf_op jit(solution)/shard_map/ppermute | solution.py:312
  24.9 3.4 %collective-permute-start.15 = (bf16[96,768]{1,0:T(8,128)(2,1)S(1)}, bf16[96,768]{1,0:T(8,128)(2,1)S(1)}, u32[]{:S(2)}, u32[]{:S(2)}) collective-permute-start(bf16[96,768]{1,0:T(8,128)(2,1)S(1)} %get-tuple-element.60), channel_id=1, source_target_pairs={{0,4},{4,8},{8,12},{12,0},{1,5},{5,9},{9,13},{13,1},{2,6},{6,10},{... | collective-permute-start | bytes 442376 | tf_op jit(solution)/shard_map/ppermute | solution.py:315
  29.0 4.7 %collective-permute-start.17 = (bf16[96,768]{1,0:T(8,128)(2,1)S(1)}, bf16[96,768]{1,0:T(8,128)(2,1)S(1)}, u32[]{:S(2)}, u32[]{:S(2)}) collective-permute-start(bf16[96,768]{1,0:T(8,128)(2,1)S(1)} %get-tuple-element.60), channel_id=1, source_target_pairs={{0,8},{4,12},{8,0},{12,4},{1,9},{5,13},{9,1},{13,5},{2,10},{6,14},... | collective-permute-start | bytes 442376 | tf_op jit(solution)/shard_map/ppermute | solution.py:315
  33.7 1.2 normalize.1
  35.6 4.5 %collective-permute-done.9 = bf16[96,768]{1,0:T(8,128)(2,1)S(1)} collective-permute-done((bf16[96,768]{1,0:T(8,128)(2,1)S(1)}, bf16[96,768]{1,0:T(8,128)(2,1)S(1)}, u32[]{:S(2)}, u32[]{:S(2)}) %collective-permute-start.9) | collective-permute-done | bytes 147488 | tf_op jit(solution)/shard_map/ppermute | solution.py:312
  40.1 1.3 collective-permute-start.2
  44.8 3.1 %collective-permute-done.10 = bf16[96,768]{1,0:T(8,128)(2,1)S(1)} collective-permute-done((bf16[96,768]{1,0:T(8,128)(2,1)S(1)}, bf16[96,768]{1,0:T(8,128)(2,1)S(1)}, u32[]{:S(2)}, u32[]{:S(2)}) %collective-permute-start.10) | collective-permute-done | bytes 147488 | tf_op jit(solution)/shard_map/ppermute | solution.py:312
  48.0 1.3 collective-permute-start.20
  49.3 1.8 %collective-permute-done.16 = bf16[96,768]{1,0:T(8,128)(2,1)S(1)} collective-permute-done((bf16[96,768]{1,0:T(8,128)(2,1)S(1)}, bf16[96,768]{1,0:T(8,128)(2,1)S(1)}, u32[]{:S(2)}, u32[]{:S(2)}) %collective-permute-start.16) | collective-permute-done | bytes 147488 | tf_op jit(solution)/shard_map/ppermute | solution.py:312
  51.1 5.7 %collective-permute-start.12 = (bf16[384,768]{1,0:T(8,128)(2,1)S(1)}, bf16[384,768]{1,0:T(8,128)(2,1)S(1)}, u32[]{:S(2)}, u32[]{:S(2)}) collective-permute-start(bf16[384,768]{1,0:T(8,128)(2,1)S(1)} %constant_dynamic-update-slice_fusion.4.refs_6_), channel_id=1, source_target_pairs={{0,1},{1,0},{2,3},{3,2},{4,5},{5,4},{6,7},{7,6},{8,9},{9,8},{10,11... | collective-permute-start | bytes 1769480 | tf_op jit(solution)/shard_map/ppermute | solution.py:312
  56.8 1.6 %collective-permute-start.26 = (bf16[384,768]{1,0:T(8,128)(2,1)S(1)}, bf16[384,768]{1,0:T(8,128)(2,1)S(1)}, u32[]{:S(2)}, u32[]{:S(2)}) collective-permute-start(bf16[384,768]{1,0:T(8,128)(2,1)S(1)} %constant_dynamic-update-slice_fusion.8.refs_5_), channel_id=1, source_target_pairs={{0,1},{1,0},{2,3},{3,2},{4,5},{5,4},{6,7},{7,6},{8,9},{9,8},{10,11... | collective-permute-start | bytes 1769480 | tf_op jit(solution)/shard_map/ppermute | solution.py:312
  58.4 1.6 %collective-permute-start.27 = (bf16[384,768]{1,0:T(8,128)(2,1)S(1)}, bf16[384,768]{1,0:T(8,128)(2,1)S(1)}, u32[]{:S(2)}, u32[]{:S(2)}) collective-permute-start(bf16[384,768]{1,0:T(8,128)(2,1)S(1)} %constant_dynamic-update-slice_fusion.12.refs_6_), channel_id=1, source_target_pairs={{0,1},{1,0},{2,3},{3,2},{4,5},{5,4},{6,7},{7,6},{8,9},{9,8},{10,11... | collective-permute-start | bytes 1769480 | tf_op jit(solution)/shard_map/ppermute | solution.py:312
  60.0 2.2 %collective-permute-start.21 = (bf16[768,128]{1,0:T(8,128)(2,1)S(1)}, bf16[768,128]{1,0:T(8,128)(2,1)S(1)}, u32[]{:S(2)}, u32[]{:S(2)}) collective-permute-start(bf16[768,128]{1,0:T(8,128)(2,1)S(1)} %get-tuple-element.61), channel_id=1, source_target_pairs={{0,2},{1,3},{2,0},{3,1},{4,6},{5,7},{6,4},{7,5},{8,10},{9,11},{10,... | collective-permute-start | bytes 589832 | tf_op jit(solution)/shard_map/ppermute | solution.py:312
  62.2 2.0 %forward_hi.1 = (bf16[128,768]{1,0:T(8,128)(2,1)S(1)}, f32[768,256]{1,0:T(8,128)S(1)}, bf16[1536,768]{1,0:T(8,128)(2,1)S(1)}) custom-call(s32[1,2]{1,0:T(1,128)S(1)} %copy-done.2, s32[1,1]{1,0:T(1,128)S(6)} %copy.21.refs_1_.links, bf16[128,1536]{1,0:T(8,128)(2,1)S(1)} %get-tuple-element.48.refs_2_, ...), custom_call_target="tpu_custom_call" | custom-call | flops 352321536 | bytes 6881280 | tf_op jit(solution)/shard_map/forward_hi/pallas_call | solution.py:31
  64.3 2.9 %upper.1 = (bf16[128,768]{1,0:T(8,128)(2,1)S(1)}, f32[128,768]{1,0:T(8,128)S(1)}, bf16[128,896]{1,0:T(8,128)(2,1)S(1)}, bf16[128,768]{1,0:T(8,128)(2,1)S(1)}, f32[128,128]{1,0:T(8,128)S(1)}) custom-call(s32[1,2]{1,0:T(1,128)S(1)} %copy-done.2, s32[1,1]{1,0:T(1,128)S(6)} %copy.21.refs_1_.links, bf16[128,768]{1,0:T(8,128)(2,1)S(1)} %get-tuple-element.47.dy, ...), custom_call_target="tpu_custom_call" | custom-call | flops 503316480 | bytes 6217728 | tf_op jit(solution)/shard_map/upper/pallas_call | solution.py:31
  67.2 1.6 %collective-permute-start.13 = (bf16[128,896]{1,0:T(8,128)(2,1)S(1)}, bf16[128,896]{1,0:T(8,128)(2,1)S(1)}, u32[]{:S(2)}, u32[]{:S(2)}) collective-permute-start(bf16[128,896]{1,0:T(8,128)(2,1)S(1)} %get-tuple-element.56.msg), channel_id=1, source_target_pairs={{0,16},{16,0},{1,17},{17,1},{2,18},{18,2},{3,19},{19,3},{4,20},{20... | collective-permute-start | bytes 688136 | tf_op jit(solution)/shard_map/ppermute | solution.py:309
  68.9 1.3 collective-permute-start.24
  70.2 1.3 collective-permute-start.25
  71.5 2.0 %forward_lo.1 = (bf16[128,768]{1,0:T(8,128)(2,1)S(1)}, f32[768,256]{1,0:T(8,128)S(1)}, bf16[1536,768]{1,0:T(8,128)(2,1)S(1)}) custom-call(s32[1,2]{1,0:T(1,128)S(1)} %copy-done.2, s32[1,1]{1,0:T(1,128)S(6)} %copy.21.refs_1_.links, bf16[128,1536]{1,0:T(8,128)(2,1)S(1)} %get-tuple-element.69.refs_2_, ...), custom_call_target="tpu_custom_call" | custom-call | flops 352321536 | bytes 6881280 | tf_op jit(solution)/shard_map/forward_lo/pallas_call | solution.py:31
  73.6 1.8 %collective-permute-done.23.refs_5_ = bf16[768,128]{1,0:T(8,128)(2,1)S(1)} collective-permute-done((bf16[768,128]{1,0:T(8,128)(2,1)S(1)}, bf16[768,128]{1,0:T(8,128)(2,1)S(1)}, u32[]{:S(2)}, u32[]{:S(2)}) %collective-permute-start.23) | collective-permute-done | bytes 196640 | tf_op jit(solution)/shard_map/ppermute | solution.py:312
  76.1 2.4 %lower.1 = (bf16[128,768]{1,0:T(8,128)(2,1)S(1)}, bf16[128,768]{1,0:T(8,128)(2,1)S(1)}, f32[128,768]{1,0:T(8,128)S(1)}, bf16[128,768]{1,0:T(8,128)(2,1)S(1)}) custom-call(s32[1,2]{1,0:T(1,128)S(1)} %copy-done.2, s32[1,1]{1,0:T(1,128)S(6)} %copy.21.refs_1_.links, f32[128,768]{1,0:T(8,128)S(1)} %get-tuple-element.55.own, ...), custom_call_target="tpu_custom_call" | custom-call | flops 201326592 | bytes 4874240 | tf_op jit(solution)/shard_map/lower/pallas_call | solution.py:31
  78.6 3.0 %collective-permute-start.36 = (bf16[128,768]{1,0:T(8,128)(2,1)S(1)}, bf16[128,768]{1,0:T(8,128)(2,1)S(1)}, u32[]{:S(2)}, u32[]{:S(2)}) collective-permute-start(bf16[128,768]{1,0:T(8,128)(2,1)S(1)} %get-tuple-element.72.qg.refs_6_), channel_id=1, source_target_pairs={{0,2},{1,3},{2,0},{3,1},{4,6},{5,7},{6,4},{7,5},{8,10},{9,11},{10,... | collective-permute-start | bytes 589832 | tf_op jit(solution)/shard_map/ppermute | solution.py:312
  81.6 5.2 %collective-permute-done.36.refs_7_ = bf16[128,768]{1,0:T(8,128)(2,1)S(1)} collective-permute-done((bf16[128,768]{1,0:T(8,128)(2,1)S(1)}, bf16[128,768]{1,0:T(8,128)(2,1)S(1)}, u32[]{:S(2)}, u32[]{:S(2)}) %collective-permute-start.36) | collective-permute-done | bytes 196640 | tf_op jit(solution)/shard_map/ppermute | solution.py:312
  86.9 1.2 collective-permute-start.37
  88.1 1.3 collective-permute-start.28
  89.4 1.5 %collective-permute-done.31.refs_7_ = bf16[128,768]{1,0:T(8,128)(2,1)S(1)} collective-permute-done((bf16[128,768]{1,0:T(8,128)(2,1)S(1)}, bf16[128,768]{1,0:T(8,128)(2,1)S(1)}, u32[]{:S(2)}, u32[]{:S(2)}) %collective-permute-start.31) | collective-permute-done | bytes 196640 | tf_op jit(solution)/shard_map/ppermute | solution.py:312
  91.4 1.5 %collective-permute-start.30 = (bf16[128,768]{1,0:T(8,128)(2,1)S(1)}, bf16[128,768]{1,0:T(8,128)(2,1)S(1)}, u32[]{:S(2)}, u32[]{:S(2)}) collective-permute-start(bf16[128,768]{1,0:T(8,128)(2,1)S(1)} %get-tuple-element.78.dy_mine), channel_id=1, source_target_pairs={{0,16},{16,0},{1,17},{17,1},{2,18},{18,2},{3,19},{19,3},{4,20},{20... | collective-permute-start | bytes 589832 | tf_op jit(solution)/shard_map/ppermute | solution.py:309
  92.9 1.4 %project_lo.1 = (f32[128,1536]{1,0:T(8,128)S(1)}, bf16[128,1536]{1,0:T(8,128)(2,1)S(1)}) custom-call(s32[1,2]{1,0:T(1,128)S(1)} %copy-done.2, s32[1,1]{1,0:T(1,128)S(6)} %copy.21.refs_1_.links, bf16[128,768]{1,0:T(8,128)(2,1)S(1)} %get-tuple-element.72.qg.refs_6_, bf16[1536,768]{1,0:T(8,128)(2,1)S(1)} %get-tuple-element.73.weights, ...), custom_call_target="tpu_custom_call" | custom-call | flops 301989888 | bytes 4325376 | tf_op jit(solution)/shard_map/project_lo/pallas_call | solution.py:31
  94.4 1.3 collective-permute-start.29
  96.8 1.6 %collective-permute-start.40 = (bf16[96,768]{1,0:T(8,128)(2,1)S(1)}, bf16[96,768]{1,0:T(8,128)(2,1)S(1)}, u32[]{:S(2)}, u32[]{:S(2)}) collective-permute-start(bf16[96,768]{1,0:T(8,128)(2,1)S(1)} %get-tuple-element.88), channel_id=1, source_target_pairs={{0,12},{4,0},{8,4},{12,8},{1,13},{5,1},{9,5},{13,9},{2,14},{6,2},{... | collective-permute-start | bytes 442376 | tf_op jit(solution)/shard_map/ppermute | solution.py:315
  100.0 1.5 %collective-permute-start.34 = (bf16[96,768]{1,0:T(8,128)(2,1)S(1)}, bf16[96,768]{1,0:T(8,128)(2,1)S(1)}, u32[]{:S(2)}, u32[]{:S(2)}) collective-permute-start(bf16[96,768]{1,0:T(8,128)(2,1)S(1)} %get-tuple-element.83), channel_id=1, source_target_pairs={{0,8},{4,12},{8,0},{12,4},{1,9},{5,13},{9,1},{13,5},{2,10},{6,14},... | collective-permute-start | bytes 442376 | tf_op jit(solution)/shard_map/ppermute | solution.py:315
  101.5 2.8 %collective-permute-start.35 = (bf16[96,768]{1,0:T(8,128)(2,1)S(1)}, bf16[96,768]{1,0:T(8,128)(2,1)S(1)}, u32[]{:S(2)}, u32[]{:S(2)}) collective-permute-start(bf16[96,768]{1,0:T(8,128)(2,1)S(1)} %get-tuple-element.84), channel_id=1, source_target_pairs={{0,12},{4,0},{8,4},{12,8},{1,13},{5,1},{9,5},{13,9},{2,14},{6,2},{... | collective-permute-start | bytes 442376 | tf_op jit(solution)/shard_map/ppermute | solution.py:315
  104.4 2.3 %collective-permute-done.29.msg_in = bf16[128,1536]{1,0:T(8,128)(2,1)S(1)} collective-permute-done((bf16[128,1536]{1,0:T(8,128)(2,1)S(1)}, bf16[128,1536]{1,0:T(8,128)(2,1)S(1)}, u32[]{:S(2)}, u32[]{:S(2)}) %collective-permute-start.29) | collective-permute-done | bytes 393248 | tf_op jit(solution)/shard_map/ppermute | solution.py:418
  106.7 2.0 %collective-permute-start.38 = (bf16[96,768]{1,0:T(8,128)(2,1)S(1)}, bf16[96,768]{1,0:T(8,128)(2,1)S(1)}, u32[]{:S(2)}, u32[]{:S(2)}) collective-permute-start(bf16[96,768]{1,0:T(8,128)(2,1)S(1)} %get-tuple-element.86), channel_id=1, source_target_pairs={{0,4},{4,8},{8,12},{12,0},{1,5},{5,9},{9,13},{13,1},{2,6},{6,10},{... | collective-permute-start | bytes 442376 | tf_op jit(solution)/shard_map/ppermute | solution.py:315
  108.8 2.0 %finish.1 = bf16[128,1536]{1,0:T(8,128)(2,1)} custom-call(s32[1,2]{1,0:T(1,128)S(1)} %copy-done.2, s32[1,1]{1,0:T(1,128)S(6)} %copy.21.refs_1_.links, f32[128,1536]{1,0:T(8,128)S(1)} %get-tuple-element.76.part, bf16[128,1536]{1,0:T(8,128)(2,1)S(1)} %collective-permute-done.29.msg_in, bf16[128,1536]{1,0:T(8,128)(2,1)S(1)} %bitcast.10, ...), custom_call_target="tpu_custom_call" | custom-call | flops 3932160 | bytes 2777088 | tf_op jit(solution)/shard_map/finish/pallas_call | solution.py:31
  110.8 3.8 %collective-permute-done.34.refs_4_ = bf16[96,768]{1,0:T(8,128)(2,1)S(1)} collective-permute-done((bf16[96,768]{1,0:T(8,128)(2,1)S(1)}, bf16[96,768]{1,0:T(8,128)(2,1)S(1)}, u32[]{:S(2)}, u32[]{:S(2)}) %collective-permute-start.34) | collective-permute-done | bytes 147488 | tf_op jit(solution)/shard_map/ppermute | solution.py:315
  114.7 1.8 %collective-permute-done.38.refs_7_ = bf16[96,768]{1,0:T(8,128)(2,1)S(1)} collective-permute-done((bf16[96,768]{1,0:T(8,128)(2,1)S(1)}, bf16[96,768]{1,0:T(8,128)(2,1)S(1)}, u32[]{:S(2)}, u32[]{:S(2)}) %collective-permute-start.38) | collective-permute-done | bytes 147488 | tf_op jit(solution)/shard_map/ppermute | solution.py:315
  116.5 10.1 %collective-permute-done.39.refs_8_ = bf16[96,768]{1,0:T(8,128)(2,1)S(1)} collective-permute-done((bf16[96,768]{1,0:T(8,128)(2,1)S(1)}, bf16[96,768]{1,0:T(8,128)(2,1)S(1)}, u32[]{:S(2)}, u32[]{:S(2)}) %collective-permute-start.39) | collective-permute-done | bytes 147488 | tf_op jit(solution)/shard_map/ppermute | solution.py:315
  127.3 2.8 %collective-permute-start.41 = (bf16[96,768]{1,0:T(8,128)(2,1)S(1)}, bf16[96,768]{1,0:T(8,128)(2,1)S(1)}, u32[]{:S(2)}, u32[]{:S(2)}) collective-permute-start(bf16[96,768]{1,0:T(8,128)(2,1)S(1)} %get-tuple-element.91), channel_id=1, source_target_pairs={{0,16},{16,0},{1,17},{17,1},{2,18},{18,2},{3,19},{19,3},{4,20},{20... | collective-permute-start | bytes 442376 | tf_op jit(solution)/shard_map/ppermute | solution.py:309
  130.1 4.3 %collective-permute-done.41 = bf16[96,768]{1,0:T(8,128)(2,1)S(1)} collective-permute-done((bf16[96,768]{1,0:T(8,128)(2,1)S(1)}, bf16[96,768]{1,0:T(8,128)(2,1)S(1)}, u32[]{:S(2)}, u32[]{:S(2)}) %collective-permute-start.41) | collective-permute-done | bytes 147488 | tf_op jit(solution)/shard_map/ppermute | solution.py:309
  (77 shorter events, 14.4 us)
Async XLA Ops:
  0.6 33.0 %copy-start = (bf16[1,1,128,1536]{3,2,1,0:T(8,128)(2,1)S(1)}, bf16[1,1,128,1536]{3,2,1,0:T(8,128)(2,1)}, u32[]{:S(2)}) copy-start(bf16[1,1,128,1536]{3,2,1,0:T(8,128)(2,1)} %param.7) | copy-start | bytes 1179652
  0.6 33.0 %copy-start.1 = (bf16[1,128,1536]{2,1,0:T(8,128)(2,1)S(1)}, bf16[1,128,1536]{2,1,0:T(8,128)(2,1)}, u32[]{:S(2)}) copy-start(bf16[1,128,1536]{2,1,0:T(8,128)(2,1)} %param.8) | copy-start | bytes 1179652
  1.7 7.7 %collective-permute-start.3 = (bf16[96,768]{1,0:T(8,128)(2,1)S(1)}, bf16[96,768]{1,0:T(8,128)(2,1)S(1)}, u32[]{:S(2)}, u32[]{:S(2)}) collective-permute-start(bf16[96,768]{1,0:T(8,128)(2,1)S(1)} %get-tuple-element.98), channel_id=1, source_target_pairs={{0,16},{16,0},{1,17},{17,1},{2,18},{18,2},{3,19},{19,3},{4,20},{20... | collective-permute-start | bytes 442376 | tf_op jit(solution)/shard_map/ppermute | solution.py:309
  4.7 28.9 %collective-permute-start = (bf16[128,1536]{1,0:T(8,128)(2,1)}, bf16[128,1536]{1,0:T(8,128)(2,1)S(1)}, u32[]{:S(2)}, u32[]{:S(2)}) collective-permute-start(bf16[128,1536]{1,0:T(8,128)(2,1)} %bitcast.6), channel_id=1, source_target_pairs={{0,16},{16,0},{1,17},{17,1},{2,18},{18,2},{3,19},{19,3},{4,20},{20... | collective-permute-start | bytes 1179656 | tf_op jit(solution)/shard_map/ppermute | solution.py:309
  9.4 0.7 copy-start.2
  10.7 9.1 %collective-permute-start.4 = (bf16[96,768]{1,0:T(8,128)(2,1)S(1)}, bf16[96,768]{1,0:T(8,128)(2,1)S(1)}, u32[]{:S(2)}, u32[]{:S(2)}) collective-permute-start(bf16[96,768]{1,0:T(8,128)(2,1)S(1)} %get-tuple-element.50), channel_id=1, source_target_pairs={{0,4},{4,8},{8,12},{12,0},{1,5},{5,9},{9,13},{13,1},{2,6},{6,10},{... | collective-permute-start | bytes 442376 | tf_op jit(solution)/shard_map/ppermute | solution.py:315
  12.9 10.4 %collective-permute-start.5 = (bf16[96,768]{1,0:T(8,128)(2,1)S(1)}, bf16[96,768]{1,0:T(8,128)(2,1)S(1)}, u32[]{:S(2)}, u32[]{:S(2)}) collective-permute-start(bf16[96,768]{1,0:T(8,128)(2,1)S(1)} %get-tuple-element.50), channel_id=1, source_target_pairs={{0,8},{4,12},{8,0},{12,4},{1,9},{5,13},{9,1},{13,5},{2,10},{6,14},... | collective-permute-start | bytes 442376 | tf_op jit(solution)/shard_map/ppermute | solution.py:315
  15.4 7.8 %collective-permute-start.6 = (bf16[96,768]{1,0:T(8,128)(2,1)S(1)}, bf16[96,768]{1,0:T(8,128)(2,1)S(1)}, u32[]{:S(2)}, u32[]{:S(2)}) collective-permute-start(bf16[96,768]{1,0:T(8,128)(2,1)S(1)} %get-tuple-element.50), channel_id=1, source_target_pairs={{0,12},{4,0},{8,4},{12,8},{1,13},{5,1},{9,5},{13,9},{2,14},{6,2},{... | collective-permute-start | bytes 442376 | tf_op jit(solution)/shard_map/ppermute | solution.py:315
  17.5 11.4 %collective-permute-start.1 = (f32[2,1536]{1,0:T(2,128)S(1)}, f32[2,1536]{1,0:T(2,128)S(1)}, u32[]{:S(2)}, u32[]{:S(2)}) collective-permute-start(f32[2,1536]{1,0:T(2,128)S(1)} %pad_maximum_fusion.2.refs_4_.vecs), channel_id=1, source_target_pairs={{0,16},{16,0},{1,17},{17,1},{2,18},{18,2},{3,19},{19,3},{4,20},{20... | collective-permute-start | bytes 36872 | tf_op jit(solution)/shard_map/ppermute | solution.py:309
  19.8 8.6 %collective-permute-start.7 = (bf16[96,768]{1,0:T(8,128)(2,1)S(1)}, bf16[96,768]{1,0:T(8,128)(2,1)S(1)}, u32[]{:S(2)}, u32[]{:S(2)}) collective-permute-start(bf16[96,768]{1,0:T(8,128)(2,1)S(1)} %get-tuple-element.50), channel_id=1, source_target_pairs={{0,2},{1,3},{2,0},{3,1},{4,6},{5,7},{6,4},{7,5},{8,10},{9,11},{10,... | collective-permute-start | bytes 442376 | tf_op jit(solution)/shard_map/ppermute | solution.py:312
  23.2 11.6 %collective-permute-start.14 = (bf16[96,768]{1,0:T(8,128)(2,1)S(1)}, bf16[96,768]{1,0:T(8,128)(2,1)S(1)}, u32[]{:S(2)}, u32[]{:S(2)}) collective-permute-start(bf16[96,768]{1,0:T(8,128)(2,1)S(1)} %get-tuple-element.60), channel_id=1, source_target_pairs={{0,2},{1,3},{2,0},{3,1},{4,6},{5,7},{6,4},{7,5},{8,10},{9,11},{10,... | collective-permute-start | bytes 442376 | tf_op jit(solution)/shard_map/ppermute | solution.py:312
  24.9 16.6 %collective-permute-start.15 = (bf16[96,768]{1,0:T(8,128)(2,1)S(1)}, bf16[96,768]{1,0:T(8,128)(2,1)S(1)}, u32[]{:S(2)}, u32[]{:S(2)}) collective-permute-start(bf16[96,768]{1,0:T(8,128)(2,1)S(1)} %get-tuple-element.60), channel_id=1, source_target_pairs={{0,4},{4,8},{8,12},{12,0},{1,5},{5,9},{9,13},{13,1},{2,6},{6,10},{... | collective-permute-start | bytes 442376 | tf_op jit(solution)/shard_map/ppermute | solution.py:315
  28.4 7.1 %collective-permute-start.8 = (bf16[96,768]{1,0:T(8,128)(2,1)S(1)}, bf16[96,768]{1,0:T(8,128)(2,1)S(1)}, u32[]{:S(2)}, u32[]{:S(2)}) collective-permute-start(bf16[96,768]{1,0:T(8,128)(2,1)S(1)} %collective-permute-done.4), channel_id=1, source_target_pairs={{0,2},{1,3},{2,0},{3,1},{4,6},{5,7},{6,4},{7,5},{8,10},{9,11},{10,... | collective-permute-start | bytes 442376 | tf_op jit(solution)/shard_map/ppermute | solution.py:312
  29.0 13.7 %collective-permute-start.17 = (bf16[96,768]{1,0:T(8,128)(2,1)S(1)}, bf16[96,768]{1,0:T(8,128)(2,1)S(1)}, u32[]{:S(2)}, u32[]{:S(2)}) collective-permute-start(bf16[96,768]{1,0:T(8,128)(2,1)S(1)} %get-tuple-element.60), channel_id=1, source_target_pairs={{0,8},{4,12},{8,0},{12,4},{1,9},{5,13},{9,1},{13,5},{2,10},{6,14},... | collective-permute-start | bytes 442376 | tf_op jit(solution)/shard_map/ppermute | solution.py:315
  33.6 10.0 %collective-permute-start.19 = (bf16[96,768]{1,0:T(8,128)(2,1)S(1)}, bf16[96,768]{1,0:T(8,128)(2,1)S(1)}, u32[]{:S(2)}, u32[]{:S(2)}) collective-permute-start(bf16[96,768]{1,0:T(8,128)(2,1)S(1)} %get-tuple-element.60), channel_id=1, source_target_pairs={{0,12},{4,0},{8,4},{12,8},{1,13},{5,1},{9,5},{13,9},{2,14},{6,2},{... | collective-permute-start | bytes 442376 | tf_op jit(solution)/shard_map/ppermute | solution.py:315
  34.9 5.2 %collective-permute-start.9 = (bf16[96,768]{1,0:T(8,128)(2,1)S(1)}, bf16[96,768]{1,0:T(8,128)(2,1)S(1)}, u32[]{:S(2)}, u32[]{:S(2)}) collective-permute-start(bf16[96,768]{1,0:T(8,128)(2,1)S(1)} %collective-permute-done.5), channel_id=1, source_target_pairs={{0,2},{1,3},{2,0},{3,1},{4,6},{5,7},{6,4},{7,5},{8,10},{9,11},{10,... | collective-permute-start | bytes 442376 | tf_op jit(solution)/shard_map/ppermute | solution.py:312
  35.5 26.8 %collective-permute-start.11 = (bf16[384,768]{1,0:T(8,128)(2,1)S(1)}, bf16[384,768]{1,0:T(8,128)(2,1)S(1)}, u32[]{:S(2)}, u32[]{:S(2)}) collective-permute-start(bf16[384,768]{1,0:T(8,128)(2,1)S(1)} %constant_dynamic-update-slice_fusion.refs_5_), channel_id=1, source_target_pairs={{0,1},{1,0},{2,3},{3,2},{4,5},{5,4},{6,7},{7,6},{8,9},{9,8},{10,11... | collective-permute-start | bytes 1769480 | tf_op jit(solution)/shard_map/ppermute | solution.py:312
  40.1 19.9 %collective-permute-start.2 = (bf16[256,768]{1,0:T(8,128)(2,1)S(1)}, bf16[256,768]{1,0:T(8,128)(2,1)S(1)}, u32[]{:S(2)}, u32[]{:S(2)}) collective-permute-start(bf16[256,768]{1,0:T(8,128)(2,1)S(1)} %get-tuple-element.49.refs_4_.own_keys), channel_id=1, source_target_pairs={{0,1},{1,2},{2,3},{4,5},{5,6},{6,7},{8,9},{9,10},{10,11},{12,13},{... | collective-permute-start | bytes 1179656 | tf_op jit(solution)/shard_map/ppermute | solution.py:350
  41.4 6.5 %collective-permute-start.10 = (bf16[96,768]{1,0:T(8,128)(2,1)S(1)}, bf16[96,768]{1,0:T(8,128)(2,1)S(1)}, u32[]{:S(2)}, u32[]{:S(2)}) collective-permute-start(bf16[96,768]{1,0:T(8,128)(2,1)S(1)} %collective-permute-done.6), channel_id=1, source_target_pairs={{0,2},{1,3},{2,0},{3,1},{4,6},{5,7},{6,4},{7,5},{8,10},{9,11},{10,... | collective-permute-start | bytes 442376 | tf_op jit(solution)/shard_map/ppermute | solution.py:312
  42.6 8.5 %collective-permute-start.16 = (bf16[96,768]{1,0:T(8,128)(2,1)S(1)}, bf16[96,768]{1,0:T(8,128)(2,1)S(1)}, u32[]{:S(2)}, u32[]{:S(2)}) collective-permute-start(bf16[96,768]{1,0:T(8,128)(2,1)S(1)} %collective-permute-done.15), channel_id=1, source_target_pairs={{0,2},{1,3},{2,0},{3,1},{4,6},{5,7},{6,4},{7,5},{8,10},{9,11},{10,... | collective-permute-start | bytes 442376 | tf_op jit(solution)/shard_map/ppermute | solution.py:312
  43.6 13.2 %collective-permute-start.18 = (bf16[96,768]{1,0:T(8,128)(2,1)S(1)}, bf16[96,768]{1,0:T(8,128)(2,1)S(1)}, u32[]{:S(2)}, u32[]{:S(2)}) collective-permute-start(bf16[96,768]{1,0:T(8,128)(2,1)S(1)} %collective-permute-done.17), channel_id=1, source_target_pairs={{0,2},{1,3},{2,0},{3,1},{4,6},{5,7},{6,4},{7,5},{8,10},{9,11},{10,... | collective-permute-start | bytes 442376 | tf_op jit(solution)/shard_map/ppermute | solution.py:312
  48.0 10.4 %collective-permute-start.20 = (bf16[96,768]{1,0:T(8,128)(2,1)S(1)}, bf16[96,768]{1,0:T(8,128)(2,1)S(1)}, u32[]{:S(2)}, u32[]{:S(2)}) collective-permute-start(bf16[96,768]{1,0:T(8,128)(2,1)S(1)} %collective-permute-done.19), channel_id=1, source_target_pairs={{0,2},{1,3},{2,0},{3,1},{4,6},{5,7},{6,4},{7,5},{8,10},{9,11},{10,... | collective-permute-start | bytes 442376 | tf_op jit(solution)/shard_map/ppermute | solution.py:312
  51.1 11.1 %collective-permute-start.12 = (bf16[384,768]{1,0:T(8,128)(2,1)S(1)}, bf16[384,768]{1,0:T(8,128)(2,1)S(1)}, u32[]{:S(2)}, u32[]{:S(2)}) collective-permute-start(bf16[384,768]{1,0:T(8,128)(2,1)S(1)} %constant_dynamic-update-slice_fusion.4.refs_6_), channel_id=1, source_target_pairs={{0,1},{1,0},{2,3},{3,2},{4,5},{5,4},{6,7},{7,6},{8,9},{9,8},{10,11... | collective-permute-start | bytes 1769480 | tf_op jit(solution)/shard_map/ppermute | solution.py:312
  56.8 12.1 %collective-permute-start.26 = (bf16[384,768]{1,0:T(8,128)(2,1)S(1)}, bf16[384,768]{1,0:T(8,128)(2,1)S(1)}, u32[]{:S(2)}, u32[]{:S(2)}) collective-permute-start(bf16[384,768]{1,0:T(8,128)(2,1)S(1)} %constant_dynamic-update-slice_fusion.8.refs_5_), channel_id=1, source_target_pairs={{0,1},{1,0},{2,3},{3,2},{4,5},{5,4},{6,7},{7,6},{8,9},{9,8},{10,11... | collective-permute-start | bytes 1769480 | tf_op jit(solution)/shard_map/ppermute | solution.py:312
  58.4 11.8 %collective-permute-start.27 = (bf16[384,768]{1,0:T(8,128)(2,1)S(1)}, bf16[384,768]{1,0:T(8,128)(2,1)S(1)}, u32[]{:S(2)}, u32[]{:S(2)}) collective-permute-start(bf16[384,768]{1,0:T(8,128)(2,1)S(1)} %constant_dynamic-update-slice_fusion.12.refs_6_), channel_id=1, source_target_pairs={{0,1},{1,0},{2,3},{3,2},{4,5},{5,4},{6,7},{7,6},{8,9},{9,8},{10,11... | collective-permute-start | bytes 1769480 | tf_op jit(solution)/shard_map/ppermute | solution.py:312
  60.0 8.8 %collective-permute-start.21 = (bf16[768,128]{1,0:T(8,128)(2,1)S(1)}, bf16[768,128]{1,0:T(8,128)(2,1)S(1)}, u32[]{:S(2)}, u32[]{:S(2)}) collective-permute-start(bf16[768,128]{1,0:T(8,128)(2,1)S(1)} %get-tuple-element.61), channel_id=1, source_target_pairs={{0,2},{1,3},{2,0},{3,1},{4,6},{5,7},{6,4},{7,5},{8,10},{9,11},{10,... | collective-permute-start | bytes 589832 | tf_op jit(solution)/shard_map/ppermute | solution.py:312
  67.2 8.1 %collective-permute-start.13 = (bf16[128,896]{1,0:T(8,128)(2,1)S(1)}, bf16[128,896]{1,0:T(8,128)(2,1)S(1)}, u32[]{:S(2)}, u32[]{:S(2)}) collective-permute-start(bf16[128,896]{1,0:T(8,128)(2,1)S(1)} %get-tuple-element.56.msg), channel_id=1, source_target_pairs={{0,16},{16,0},{1,17},{17,1},{2,18},{18,2},{3,19},{19,3},{4,20},{20... | collective-permute-start | bytes 688136 | tf_op jit(solution)/shard_map/ppermute | solution.py:309
  68.8 4.8 %collective-permute-start.22 = (bf16[768,128]{1,0:T(8,128)(2,1)S(1)}, bf16[768,128]{1,0:T(8,128)(2,1)S(1)}, u32[]{:S(2)}, u32[]{:S(2)}) collective-permute-start(bf16[768,128]{1,0:T(8,128)(2,1)S(1)} %get-tuple-element.63), channel_id=1, source_target_pairs={{0,1},{1,0},{2,3},{3,2},{4,5},{5,4},{6,7},{7,6},{8,9},{9,8},{10,11... | collective-permute-start | bytes 589832 | tf_op jit(solution)/shard_map/ppermute | solution.py:312
  68.8 6.6 %collective-permute-start.23 = (bf16[768,128]{1,0:T(8,128)(2,1)S(1)}, bf16[768,128]{1,0:T(8,128)(2,1)S(1)}, u32[]{:S(2)}, u32[]{:S(2)}) collective-permute-start(bf16[768,128]{1,0:T(8,128)(2,1)S(1)} %get-tuple-element.65), channel_id=1, source_target_pairs={{0,3},{1,2},{2,1},{3,0},{4,7},{5,6},{6,5},{7,4},{8,11},{9,10},{10,... | collective-permute-start | bytes 589832 | tf_op jit(solution)/shard_map/ppermute | solution.py:312
  68.9 7.2 %collective-permute-start.24 = (bf16[128,768]{1,0:T(8,128)(2,1)S(1)}, bf16[128,768]{1,0:T(8,128)(2,1)S(1)}, u32[]{:S(2)}, u32[]{:S(2)}) collective-permute-start(bf16[128,768]{1,0:T(8,128)(2,1)S(1)} %get-tuple-element.67), channel_id=1, source_target_pairs={{1,0},{2,1},{3,2},{5,4},{6,5},{7,6},{9,8},{10,9},{11,10},{13,12},{... | collective-permute-start | bytes 589832 | tf_op jit(solution)/shard_map/ppermute | solution.py:402
  70.2 5.9 %collective-permute-start.25 = (f32[128,128]{1,0:T(8,128)S(1)}, f32[128,128]{1,0:T(8,128)S(1)}, u32[]{:S(2)}, u32[]{:S(2)}) collective-permute-start(f32[128,128]{1,0:T(8,128)S(1)} %get-tuple-element.68), channel_id=1, source_target_pairs={{1,16},{2,17},{3,18},{17,0},{18,1},{19,2},{5,20},{6,21},{7,22},{21... | collective-permute-start | bytes 196616 | tf_op jit(solution)/shard_map/ppermute | solution.py:403
  78.6 8.3 %collective-permute-start.36 = (bf16[128,768]{1,0:T(8,128)(2,1)S(1)}, bf16[128,768]{1,0:T(8,128)(2,1)S(1)}, u32[]{:S(2)}, u32[]{:S(2)}) collective-permute-start(bf16[128,768]{1,0:T(8,128)(2,1)S(1)} %get-tuple-element.72.qg.refs_6_), channel_id=1, source_target_pairs={{0,2},{1,3},{2,0},{3,1},{4,6},{5,7},{6,4},{7,5},{8,10},{9,11},{10,... | collective-permute-start | bytes 589832 | tf_op jit(solution)/shard_map/ppermute | solution.py:312
  81.5 9.4 %collective-permute-start.31 = (bf16[128,768]{1,0:T(8,128)(2,1)S(1)}, bf16[128,768]{1,0:T(8,128)(2,1)S(1)}, u32[]{:S(2)}, u32[]{:S(2)}) collective-permute-start(bf16[128,768]{1,0:T(8,128)(2,1)S(1)} %get-tuple-element.79.refs_6_), channel_id=1, source_target_pairs={{0,2},{1,3},{2,0},{3,1},{4,6},{5,7},{6,4},{7,5},{8,10},{9,11},{10,... | collective-permute-start | bytes 589832 | tf_op jit(solution)/shard_map/ppermute | solution.py:312
  86.9 8.8 %collective-permute-start.37 = (bf16[256,768]{1,0:T(8,128)(2,1)S(1)}, bf16[256,768]{1,0:T(8,128)(2,1)S(1)}, u32[]{:S(2)}, u32[]{:S(2)}) collective-permute-start(bf16[256,768]{1,0:T(8,128)(2,1)S(1)} %pad_maximum_fusion.1), channel_id=1, source_target_pairs={{0,1},{1,0},{2,3},{3,2},{4,5},{5,4},{6,7},{7,6},{8,9},{9,8},{10,11... | collective-permute-start | bytes 1179656 | tf_op jit(solution)/shard_map/ppermute | solution.py:312
  88.1 4.8 %collective-permute-start.28 = (bf16[128,768]{1,0:T(8,128)(2,1)S(1)}, bf16[128,768]{1,0:T(8,128)(2,1)S(1)}, u32[]{:S(2)}, u32[]{:S(2)}) collective-permute-start(bf16[128,768]{1,0:T(8,128)(2,1)S(1)} %get-tuple-element.75), channel_id=1, source_target_pairs={{1,0},{2,1},{3,2},{5,4},{6,5},{7,6},{9,8},{10,9},{11,10},{13,12},{... | collective-permute-start | bytes 589832 | tf_op jit(solution)/shard_map/ppermute | solution.py:412
  90.9 7.4 %collective-permute-start.32 = (bf16[256,768]{1,0:T(8,128)(2,1)S(1)}, bf16[256,768]{1,0:T(8,128)(2,1)S(1)}, u32[]{:S(2)}, u32[]{:S(2)}) collective-permute-start(bf16[256,768]{1,0:T(8,128)(2,1)S(1)} %pad_maximum_fusion), channel_id=1, source_target_pairs={{0,1},{1,0},{2,3},{3,2},{4,5},{5,4},{6,7},{7,6},{8,9},{9,8},{10,11... | collective-permute-start | bytes 1179656 | tf_op jit(solution)/shard_map/ppermute | solution.py:312
  91.4 10.1 %collective-permute-start.30 = (bf16[128,768]{1,0:T(8,128)(2,1)S(1)}, bf16[128,768]{1,0:T(8,128)(2,1)S(1)}, u32[]{:S(2)}, u32[]{:S(2)}) collective-permute-start(bf16[128,768]{1,0:T(8,128)(2,1)S(1)} %get-tuple-element.78.dy_mine), channel_id=1, source_target_pairs={{0,16},{16,0},{1,17},{17,1},{2,18},{18,2},{3,19},{19,3},{4,20},{20... | collective-permute-start | bytes 589832 | tf_op jit(solution)/shard_map/ppermute | solution.py:309
  94.4 12.3 %collective-permute-start.29 = (bf16[128,1536]{1,0:T(8,128)(2,1)S(1)}, bf16[128,1536]{1,0:T(8,128)(2,1)S(1)}, u32[]{:S(2)}, u32[]{:S(2)}) collective-permute-start(bf16[128,1536]{1,0:T(8,128)(2,1)S(1)} %get-tuple-element.77), channel_id=1, source_target_pairs={{16,0},{17,1},{18,2},{19,3},{20,4},{21,5},{22,6},{23,7},{24,8},{25... | collective-permute-start | bytes 1179656 | tf_op jit(solution)/shard_map/ppermute | solution.py:418
  96.8 11.9 %collective-permute-start.40 = (bf16[96,768]{1,0:T(8,128)(2,1)S(1)}, bf16[96,768]{1,0:T(8,128)(2,1)S(1)}, u32[]{:S(2)}, u32[]{:S(2)}) collective-permute-start(bf16[96,768]{1,0:T(8,128)(2,1)S(1)} %get-tuple-element.88), channel_id=1, source_target_pairs={{0,12},{4,0},{8,4},{12,8},{1,13},{5,1},{9,5},{13,9},{2,14},{6,2},{... | collective-permute-start | bytes 442376 | tf_op jit(solution)/shard_map/ppermute | solution.py:315
  99.4 11.4 %collective-permute-start.33 = (bf16[96,768]{1,0:T(8,128)(2,1)S(1)}, bf16[96,768]{1,0:T(8,128)(2,1)S(1)}, u32[]{:S(2)}, u32[]{:S(2)}) collective-permute-start(bf16[96,768]{1,0:T(8,128)(2,1)S(1)} %get-tuple-element.82), channel_id=1, source_target_pairs={{0,4},{4,8},{8,12},{12,0},{1,5},{5,9},{9,13},{13,1},{2,6},{6,10},{... | collective-permute-start | bytes 442376 | tf_op jit(solution)/shard_map/ppermute | solution.py:315
  100.0 14.7 %collective-permute-start.34 = (bf16[96,768]{1,0:T(8,128)(2,1)S(1)}, bf16[96,768]{1,0:T(8,128)(2,1)S(1)}, u32[]{:S(2)}, u32[]{:S(2)}) collective-permute-start(bf16[96,768]{1,0:T(8,128)(2,1)S(1)} %get-tuple-element.83), channel_id=1, source_target_pairs={{0,8},{4,12},{8,0},{12,4},{1,9},{5,13},{9,1},{13,5},{2,10},{6,14},... | collective-permute-start | bytes 442376 | tf_op jit(solution)/shard_map/ppermute | solution.py:315
  101.5 13.2 %collective-permute-start.35 = (bf16[96,768]{1,0:T(8,128)(2,1)S(1)}, bf16[96,768]{1,0:T(8,128)(2,1)S(1)}, u32[]{:S(2)}, u32[]{:S(2)}) collective-permute-start(bf16[96,768]{1,0:T(8,128)(2,1)S(1)} %get-tuple-element.84), channel_id=1, source_target_pairs={{0,12},{4,0},{8,4},{12,8},{1,13},{5,1},{9,5},{13,9},{2,14},{6,2},{... | collective-permute-start | bytes 442376 | tf_op jit(solution)/shard_map/ppermute | solution.py:315
  106.7 9.8 %collective-permute-start.38 = (bf16[96,768]{1,0:T(8,128)(2,1)S(1)}, bf16[96,768]{1,0:T(8,128)(2,1)S(1)}, u32[]{:S(2)}, u32[]{:S(2)}) collective-permute-start(bf16[96,768]{1,0:T(8,128)(2,1)S(1)} %get-tuple-element.86), channel_id=1, source_target_pairs={{0,4},{4,8},{8,12},{12,0},{1,5},{5,9},{9,13},{13,1},{2,6},{6,10},{... | collective-permute-start | bytes 442376 | tf_op jit(solution)/shard_map/ppermute | solution.py:315
  108.7 17.9 %collective-permute-start.39 = (bf16[96,768]{1,0:T(8,128)(2,1)S(1)}, bf16[96,768]{1,0:T(8,128)(2,1)S(1)}, u32[]{:S(2)}, u32[]{:S(2)}) collective-permute-start(bf16[96,768]{1,0:T(8,128)(2,1)S(1)} %get-tuple-element.87), channel_id=1, source_target_pairs={{0,8},{4,12},{8,0},{12,4},{1,9},{5,13},{9,1},{13,5},{2,10},{6,14},... | collective-permute-start | bytes 442376 | tf_op jit(solution)/shard_map/ppermute | solution.py:315
  127.3 7.1 %collective-permute-start.41 = (bf16[96,768]{1,0:T(8,128)(2,1)S(1)}, bf16[96,768]{1,0:T(8,128)(2,1)S(1)}, u32[]{:S(2)}, u32[]{:S(2)}) collective-permute-start(bf16[96,768]{1,0:T(8,128)(2,1)S(1)} %get-tuple-element.91), channel_id=1, source_target_pairs={{0,16},{16,0},{1,17},{17,1},{2,18},{18,2},{3,19},{19,3},{4,20},{20... | collective-permute-start | bytes 442376 | tf_op jit(solution)/shard_map/ppermute | solution.py:309

commit v2 on v1

v2 whole, which is shorter than its diff:
```python
import jax
import jax.numpy as jnp
from jax import lax
from jax.experimental import pallas as pl
from jax.experimental.pallas import tpu as pltpu
from jax.sharding import PartitionSpec as P

HDIM = 128
SCALE = HDIM ** (-0.5)
EPS = 1e-06
NEG = -1e30
BF = jnp.bfloat16
F32 = jnp.float32
VLIMIT = 16 * 1024 * 1024

NN = (((1,), (0,)), ((), ()))
NT = (((1,), (1,)), ((), ()))
TN = (((0,), (0,)), ((), ()))


def mm(a, b, dims):
    return lax.dot_general(a, b, dims, preferred_element_type=F32)


def sds(shape, dtype):
    return jax.ShapeDtypeStruct(shape, dtype)


def call(kernel, outs, flops, name, *args, scalars=(), scratch=()):
    nbytes = sum(s.size * s.dtype.itemsize for s in outs) + sum(a.size * a.dtype.itemsize for a in args)
    return pl.pallas_call(
        kernel,
        out_shape=outs,
        in_specs=[pl.BlockSpec(memory_space=pltpu.SMEM)] * len(scalars)
        + [pl.BlockSpec(memory_space=pltpu.VMEM)] * len(args),
        out_specs=[pl.BlockSpec(memory_space=pltpu.VMEM)] * len(outs),
        scratch_shapes=list(scratch),
        compiler_params=pltpu.CompilerParams(vmem_limit_bytes=VLIMIT),
        cost_estimate=pl.CostEstimate(flops=flops, bytes_accessed=nbytes, transcendentals=0),
        name=name,
    )(*scalars, *args)


def my_side():
    return lax.rem(lax.axis_index("section"), 2)


def is_kept(kept, section_hi):
    hi = lax.axis_index("section") - my_side() + 1
    return kept[0, hi if section_hi else hi - 1] > 0


def pick(side, value, half, other=False):
    first = value[:, :half]
    second = value[:, half:]
    use_first = (side == 1) if other else (side == 0)
    return jnp.where(use_first, first, second)


def inverse_rms(x):
    return lax.rsqrt(jnp.mean(x * x, axis=-1, keepdims=True) + EPS)


def three_terms(value):
    high = value.astype(BF)
    rest = value - high.astype(F32)
    middle = rest.astype(BF)
    return high, middle, (rest - middle.astype(F32)).astype(BF)


def pack_kernel(acts, gain, gate, packed):
    tile = acts.shape[0]
    packed[:tile, :] = acts[...]
    shape = (packed.shape[0] - tile, acts.shape[1])
    row = lax.broadcasted_iota(jnp.int32, shape, 0)
    terms = jnp.zeros(shape, F32)
    for index, term in enumerate(three_terms(gain[...]) + three_terms(gate[...])):
        terms = jnp.where(row == index, jnp.broadcast_to(term.astype(F32), shape), terms)
    packed[tile:, :] = terms.astype(BF)


def select_kernel(own, other, hi, lo):
    side = my_side()
    hi[...] = jnp.where(side == 1, own[...], other[...])
    lo[...] = jnp.where(side == 1, other[...], own[...])


def row_blocks(value, offsets, rows, parts, turned):
    seqs = len(offsets)
    block = parts[0].shape[0] // (seqs // 2)
    seq = lax.axis_index("seq")
    turned[...] = value.astype(F32).T.astype(BF)
    for offset in offsets:
        part = parts[0] if offset < seqs // 2 else parts[1]
        base = offset % (seqs // 2) * block
        for f in range(block // rows):
            source = pl.multiple_of((f * seqs + jnp.bitwise_xor(seq, offset)) * rows, rows)
            part[base + f * rows : base + (f + 1) * rows, :] = turned[pl.ds(source, rows), :]


def normalize_own_kernel(offsets, rows, acts, gain, normed, low, high, turned):
    x = acts[...].astype(F32)
    value = (x * inverse_rms(x) * gain[...]).astype(BF)
    normed[...] = value
    row_blocks(value, offsets, rows, (low, high), turned)


def normalize_kernel(acts, packed, gain, gate, dy_full, normed_own, *outs):
    xs, normed, (keys, vecs, dy) = outs[:2], outs[2:4], outs[4:]
    tile, half = dy.shape
    extra = packed[tile:, :].astype(F32)
    gain_in = extra[0:1] + extra[1:2] + extra[2:3]
    gate_in = extra[3:4] + extra[4:5] + extra[5:6]
    x = packed[:tile, :].astype(F32)
    value = (x * inverse_rms(x) * gain_in).astype(BF)
    own = acts[...], normed_own[...], gain[...], gate[...]
    other = packed[:tile, :], value, gain_in, gate_in
    side = my_side()
    for which in range(2):
        take_own = side == 1 - which
        x_low, rounded, gain_row, gate_row = [jnp.where(take_own, a, b) for a, b in zip(own, other)]
        xs[which][...] = x_low
        normed[which][...] = rounded
        vecs[2 * which : 2 * which + 1, :] = gain_row
        vecs[2 * which + 1 : 2 * which + 2, :] = gate_row
        keys[which * tile : (which + 1) * tile, :] = pick(side, rounded, half)
    dy[...] = pick(side, dy_full[...], half)


def head_probs(query, keys, linked):
    scores = mm(query, keys, NT) * SCALE
    column = lax.broadcasted_iota(jnp.int32, scores.shape, 1)
    scores = jnp.where(jnp.logical_or(column >= scores.shape[1] // 2, linked), scores, NEG)
    exps = jnp.exp(scores - jnp.max(scores, axis=-1, keepdims=True))
    return exps / jnp.sum(exps, axis=-1, keepdims=True)


def head_backward(query, keys, grads, probs):
    prob_grad = mm(grads, keys, NT)
    row_delta = jnp.sum(probs * prob_grad, axis=-1, keepdims=True)
    score_grad = (probs * (prob_grad - row_delta) * SCALE).astype(BF)
    query_grad = mm(score_grad, keys, NN).astype(BF)
    key_grad = mm(
        jnp.concatenate([score_grad, probs.astype(BF)], axis=0),
        jnp.concatenate([query, grads], axis=0),
        TN,
    )
    return query_grad, key_grad


def pieces(column):
    rows = column.shape[0]
    lane = lax.broadcasted_iota(jnp.int32, (rows, HDIM), 1)
    high, middle, low = [jnp.broadcast_to(p.astype(F32), (rows, HDIM)) for p in three_terms(column)]
    value = jnp.where(lane == 0, high, jnp.where(lane == 1, middle, jnp.where(lane == 2, low, 0.0)))
    return value.astype(BF)


def unpieces(block):
    return jnp.sum(block.astype(F32), axis=-1, keepdims=True)


def heads_of(half):
    return [slice(h * HDIM, (h + 1) * HDIM) for h in range(half // HDIM)]


def pairs_of(half):
    step = 2 * HDIM if half % (2 * HDIM) == 0 else HDIM
    return [slice(c, c + step) for c in range(0, half, step)]


def forward_kernel(which, places, rows, links, normed, left_keys, own_keys, *rest):
    blocks = rest[: len(places)]
    query_out, probs_out, weights = rest[len(places) :]
    tile, half = query_out.shape
    token = slice(which * tile, (which + 1) * tile)
    seqs = lax.axis_size("seq")
    fsdp, seq = lax.axis_index("fsdp"), lax.axis_index("seq")
    linked = jnp.logical_and(links[0, 0] > 0, seq > 0)
    for block, place in zip(blocks, places):
        for index, (flip, offset) in enumerate(place):
            f = jnp.bitwise_xor(fsdp, flip)
            target = pl.multiple_of((f * seqs + jnp.bitwise_xor(seq, offset)) * rows, rows)
            weights[pl.ds(target, rows), :] = block[index * rows : (index + 1) * rows, :]
    tokens = normed[...]
    for cols in pairs_of(half):
        query = mm(tokens, weights[:, cols], NN).astype(BF)
        query_out[:, cols] = query
        for sub in heads_of(cols.stop - cols.start):
            at = slice(cols.start + sub.start, cols.start + sub.stop)
            keys = jnp.concatenate([left_keys[token, at], own_keys[token, at]], axis=0)
            start = at.start // HDIM * tile
            probs_out[start : start + tile, :] = head_probs(query[:, sub], keys, linked)


def upper_kernel(
    kept, dy, acts, vecs, query, probs, weights, left_keys, own_keys, qg, own, msg, leftward, leftsum
):
    tile, half = dy.shape
    side = my_side()
    keep = is_kept(kept, True)
    gate = pick(side, vecs[1:2, :], half)
    grads = (gate * dy[...].astype(F32)).astype(BF)
    left_total = jnp.zeros((tile, 1), F32)
    for at in heads_of(half):
        left = left_keys[:tile, at]
        keys = jnp.concatenate([left, own_keys[:tile, at]], axis=0)
        start = at.start // HDIM * tile
        query_grad, key_grad = head_backward(query[:, at], keys, grads[:, at], probs[start : start + tile, :])
        qg[:, at] = jnp.where(keep, query_grad, jnp.zeros_like(query_grad))
        back = key_grad[:tile].astype(BF)
        leftward[:, at] = back
        left_total += jnp.sum(back.astype(F32) * left.astype(F32), axis=-1, keepdims=True)
        own[:, at] = key_grad[tile:]
    leftsum[...] = jnp.broadcast_to(left_total, leftsum.shape)
    part = mm(qg[...], weights[...], NT)
    x_gain = acts[...].astype(F32) * vecs[:1, :]
    total = jnp.sum(x_gain * part, axis=-1, keepdims=True)
    total += jnp.sum(pick(side, x_gain, half) * own[...], axis=-1, keepdims=True)
    own[...] += pick(side, part, half)
    msg[:, :half] = pick(side, part, half, other=True).astype(BF)
    msg[:, half:] = pieces(total)


def lower_kernel(
    kept, own, msg, msg_in, left_in, sum_other, acts, vecs, dy, query, probs, left_keys, own_keys,
    dy_out, qg, key_own, leftward,
):
    tile, half = dy.shape
    side = my_side()
    keep_hi, keep_lo = is_kept(kept, True), is_kept(kept, False)
    x = acts[...].astype(F32)
    inv = inverse_rms(x)
    left = left_in[...].astype(F32)
    x_mine = pick(side, x, half)
    gain = pick(side, vecs[:1, :], half)
    gate_lo = pick(side, vecs[3:4, :], half)
    total = unpieces(msg[:, half:]) + unpieces(msg_in[:, half:])
    total += jnp.sum(x_mine * gain * left, axis=-1, keepdims=True)
    total += sum_other[:, :1] / inv
    mean_term = total / x.shape[1]
    scaled = (own[...] + left + msg_in[:, :half].astype(F32)) * gain
    change = inv * (scaled - x_mine * inv * inv * mean_term)
    dy_old = dy[...]
    dy_new = jnp.where(keep_hi, (dy_old.astype(F32) + change).astype(BF), dy_old)
    dy_out[...] = dy_new
    grads = (gate_lo * dy_new.astype(F32)).astype(BF)
    for at in heads_of(half):
        keys = jnp.concatenate([left_keys[tile:, at], own_keys[tile:, at]], axis=0)
        start = at.start // HDIM * tile
        query_grad, key_grad = head_backward(query[:, at], keys, grads[:, at], probs[start : start + tile, :])
        qg[:, at] = jnp.where(keep_lo, query_grad, jnp.zeros_like(query_grad))
        leftward[:, at] = key_grad[:tile].astype(BF)
        key_own[:, at] = key_grad[tile:]


def project_kernel(qg, weights, key_own, left_in, dy, part_out, msg):
    half = qg.shape[1]
    side = my_side()
    part = mm(qg[...], weights[...], NT)
    mine = key_own[...] + left_in[...].astype(F32)
    first = part[:, :half] + jnp.where(side == 0, mine, 0.0)
    second = part[:, half:] + jnp.where(side == 1, mine, 0.0)
    part_out[:, :half] = first
    part_out[:, half:] = second
    msg[:, :half] = first.astype(BF)
    msg[:, half : 2 * half] = second.astype(BF)
    msg[:, 2 * half :] = dy[...]


def finish_kernel(kept, part, msg_in, acts, vecs, dy_mine, out):
    half = dy_mine.shape[1]
    side = my_side()
    mine, other = dy_mine[...], msg_in[:, 2 * half :]
    first = jnp.where(side == 0, mine, other)
    second = jnp.where(side == 0, other, mine)
    dy = jnp.concatenate([first, second], axis=1)
    x = acts[...].astype(F32)
    inv = inverse_rms(x)
    scaled = (part[...] + msg_in[:, : 2 * half].astype(F32)) * vecs[2:3, :]
    mean_term = jnp.mean(x * scaled, axis=-1, keepdims=True)
    change = inv * (scaled - x * inv * inv * mean_term)
    updated = jnp.where(is_kept(kept, False), (dy.astype(F32) + change).astype(BF), dy)
    out[...] = jnp.where(side == 0, updated, dy)


def weight_grad_kernel(section_hi, flips, rows, own, other, *refs):
    grads, (kept_rows, sent_rows, scratch) = refs[:-3], refs[-3:]
    fsdp = lax.axis_index("fsdp")
    block = scratch.shape[0]
    take_own = (my_side() == 1) if section_hi else (my_side() == 0)
    parts = jnp.where(take_own, own[...], other[...])
    left = jnp.concatenate([parts[i : i + block] for i in range(0, parts.shape[0], block)], axis=1)
    right = jnp.concatenate([g[...] for g in grads], axis=0)
    scratch[...] = mm(left, right, NN).astype(BF)
    count = len(flips) // 2
    for index, flip in enumerate(flips):
        source = pl.multiple_of(jnp.bitwise_xor(fsdp, flip) * rows, rows)
        out = kept_rows if index < count else sent_rows
        target = index % count * rows
        out[target : target + rows, :] = scratch[pl.ds(source, rows), :]


def add_halves_kernel(kept_rows, arrived, mine, sent):
    total = (kept_rows[...].astype(F32) + arrived[...].astype(F32)).astype(BF)
    count = mine.shape[0]
    mine[...] = total[:count]
    sent[...] = total[count:]


def add_kernel(hi_mine, hi_arrived, lo_mine, lo_arrived, mine, theirs):
    side = my_side()
    grad_hi = (hi_mine[...].astype(F32) + hi_arrived[...].astype(F32)).astype(BF)
    grad_lo = (lo_mine[...].astype(F32) + lo_arrived[...].astype(F32)).astype(BF)
    mine[...] = jnp.where(side == 1, grad_hi, grad_lo)
    theirs[...] = jnp.where(side == 1, grad_lo, grad_hi)


def tied(value, *others):
    return lax.optimization_barrier((value, *others))[0]


def per_device(acts, grad_out, gain, gate, w_query, kept, links):
    sections = lax.axis_size("section")
    fsdps = lax.axis_size("fsdp")
    seqs = lax.axis_size("seq")
    section_idx = lax.axis_index("section")
    side = section_idx % 2
    tile, dim = acts.shape[2:]
    rows = w_query.shape[1]
    half = dim // 2
    swap_pairs = [(i, i ^ 1) for i in range(sections)]
    bits = [1 << b for b in reversed(range(seqs.bit_length() - 1))]
    top = bits[0]
    steps = [1 << b for b in reversed(range(fsdps.bit_length() - 1))]
    flips = [0]
    for step in steps:
        flips = flips + [f ^ step for f in flips]
    owners = [0]
    for step in steps:
        owners = owners + [f ^ step for f in owners]
    offsets = list(range(seqs))
    right_pairs = [(t, t + 1) for t in range(seqs - 1)]
    left_pairs = [(t + 1, t) for t in range(seqs - 1)]
    diagonal_pairs = [
        (s * seqs + t + 1, (s ^ 1) * seqs + t) for s in range(sections) for t in range(seqs - 1)
    ]
    matmul_flops = 2 * tile * dim * half
    head_flops = 2 * tile * 2 * tile * half

    def swap(value):
        return lax.ppermute(value, "section", swap_pairs)

    def across(value, offset):
        return lax.ppermute(value, "seq", [(s, s ^ offset) for s in range(seqs)])

    def along(value, flip):
        return lax.ppermute(value, "fsdp", [(f, f ^ flip) for f in range(fsdps)])

    def join(values):
        return values[0] if len(values) == 1 else jnp.concatenate(values, axis=0)

    acts_own = acts[0, 0]
    first, second = w_query[0][:, :half], w_query[0][:, half:]
    w_own, w_theirs = jnp.where(side == 0, first, second), jnp.where(side == 0, second, first)
    w_other = swap(w_theirs)
    (packed,) = call(
        pack_kernel, [sds((tile + 16, dim), BF)], 10 * tile * dim, "pack", acts_own, gain, gate
    )
    packed_in = swap(packed)

    unit = fsdps * rows
    part_shapes = [sds((seqs // 2 * unit, tile), BF)] * 2
    turned = pltpu.VMEM((dim, tile), BF)

    def to_row_owners(low, high):
        parts = [(low, [0]), (across(high, top), [0])]
        for bit in bits[1:]:
            sent = [v[b + bit * unit : b + 2 * bit * unit] for v, begins in parts for b in begins]
            arrived = across(join(sent), bit)
            parts = parts + [(arrived, [i * bit * unit for i in range(len(sent))])]
        return join([v[b : b + unit] for v, begins in parts for b in begins])

    normed_own, low_own, high_own = call(
        lambda *refs: normalize_own_kernel(offsets, rows, *refs),
        [sds((tile, dim), BF)] + part_shapes, 20 * tile * dim,
        "normalize_own", acts_own, gain, scratch=[turned],
    )
    w_hi, w_lo = call(
        select_kernel, [sds((rows, half), BF)] * 2, rows * half,
        "select_w", w_own, tied(w_other, packed, high_own),
    )
    parts_own = to_row_owners(low_own, high_own)
    def over_fsdp(shard):
        near = [shard]
        for step in steps:
            near = near + [along(join(near), step)]
        return near

    def over_seq(near, after=(), after_last=()):
        sent = [join(near[:2])] + near[2:]
        if after:
            sent = [tied(value, *after) for value in sent]
        if after_last:
            sent[-1] = tied(sent[-1], *after_last)
        return [across(value, top) for value in sent]

    def between_cores(near, far, after=()):
        if after:
            far = [tied(value, *after) for value in far]
        held = [join(near + far)]
        places = [[(f, 0) for f in flips] + [(f, top) for f in flips]]
        for bit in bits[1:]:
            held = held + [across(v, bit) for v in held]
            places = places + [[(f, o ^ bit) for f, o in place] for place in places]
        return held, places

    near_hi = over_fsdp(w_hi)
    far_hi = over_seq(near_hi, after_last=[packed_in, parts_own])
    x_hi, x_lo, normed_hi, normed_lo, keys, vecs, incoming = call(
        normalize_kernel,
        [sds((tile, dim), BF)] * 4 + [sds((2 * tile, half), BF), sds((8, dim), F32), sds((tile, half), BF)],
        30 * tile * dim,
        "normalize", acts_own, packed_in, gain, gate, grad_out[0], tied(normed_own, far_hi[0]),
    )
    left = lax.ppermute(keys, "seq", right_pairs)
    near_lo = over_fsdp(tied(w_lo, near_hi[1], packed_in))
    blocks_hi, places = between_cores(near_hi, far_hi, after=[near_lo[-1], left])
    far_lo = over_seq(near_lo, after=[left])

    def forward(name, which, normed, blocks):
        return call(
            lambda *refs: forward_kernel(which, places, rows, *refs),
            [sds((tile, half), BF), sds((half // HDIM * tile, 2 * tile), F32), sds((dim, half), BF)],
            matmul_flops + head_flops,
            name, normed, left, keys, *blocks, scalars=[links],
        )

    query_hi, probs_hi, weights_hi = forward("forward_hi", 0, normed_hi, blocks_hi)
    def over_tiles(query_grad):
        gathered = [query_grad]
        for bit in bits:
            gathered = gathered + [across(join(gathered), bit)]
        return gathered

    def weight_grad(name, section_hi, gathered):
        halves = [sds((fsdps // 2 * rows, half), BF)] * 2
        return call(
            lambda *refs: weight_grad_kernel(section_hi, owners, rows, *refs),
            halves,
            2 * fsdps * rows * seqs * tile * half,
            name, parts_own, parts_other, *gathered,
            scratch=[pltpu.VMEM((fsdps * rows, half), BF)],
        )

    def over_clips(name, mine, sent):
        arrived = along(sent, steps[-1])
        for step in reversed(steps[:-1]):
            count = mine.shape[0] // 2
            mine, sent = call(
                add_halves_kernel, [sds((count, half), BF)] * 2, 4 * count * half, name, mine, arrived
            )
            arrived = along(sent, step)
        return mine, arrived

    kept_state = None
    single = sections == 2
    for tick in range(sections // 2):
        qg_hi, own, msg, leftward, leftsum = call(
            upper_kernel,
            [
                sds((tile, half), BF),
                sds((tile, half), F32),
                sds((tile, half + HDIM), BF),
                sds((tile, half), BF),
                sds((tile, HDIM), F32),
            ],
            matmul_flops + 4 * head_flops,
            "upper", incoming, x_hi, vecs, query_hi, probs_hi, weights_hi, left, keys, scalars=[kept],
        )
        msg_in = swap(msg)
        left_in = lax.ppermute(leftward, "seq", left_pairs)
        sum_other = lax.ppermute(leftsum, ("section", "seq"), diagonal_pairs)
        exchanged = [msg_in, left_in, sum_other]
        if tick == 0:
            parts_other = swap(tied(parts_own, msg_in))
            blocks_lo, _ = between_cores(near_lo, far_lo, after=exchanged)
            query_lo, probs_lo, weights_lo = forward("forward_lo", 1, normed_lo, blocks_lo)
        dy_mid, qg_lo, key_own, leftward_lo = call(
            lower_kernel,
            [sds((tile, half), BF), sds((tile, half), BF), sds((tile, half), F32), sds((tile, half), BF)],
            4 * head_flops,
            "lower", own, msg, msg_in, left_in, sum_other, x_hi, vecs, incoming,
            query_lo, probs_lo, left, keys, scalars=[kept],
        )
        left_in_lo = lax.ppermute(leftward_lo, "seq", left_pairs)
        if single:
            gathered_hi = over_tiles(tied(qg_hi, *exchanged))
            gathered_hi[-1] = tied(gathered_hi[-1], qg_lo)
            clips_hi = over_clips("add_pair_hi", *weight_grad("weight_grad_hi", True, gathered_hi))
            clips_lo = over_clips("add_pair_lo", *weight_grad("weight_grad_lo", False, over_tiles(qg_lo)))
            left_in_lo = tied(left_in_lo, clips_hi[0])
        part_lo, msg_lo = call(
            project_kernel, [sds((tile, dim), F32), sds((tile, dim + half), BF)], matmul_flops,
            "project_lo", qg_lo, weights_lo, key_own, left_in_lo, dy_mid,
        )
        msg_lo_in = swap(msg_lo)
        (updated,) = call(
            finish_kernel, [sds((tile, dim), BF)], 20 * tile * dim,
            "finish", part_lo, msg_lo_in, x_lo, vecs, dy_mid, scalars=[kept],
        )
        state = (updated, qg_hi, qg_lo)
        if kept_state is None:
            kept_state = state
        else:
            active = section_idx // 2 == sections // 2 - 1 - tick
            kept_state = jax.tree.map(lambda new, old: jnp.where(active, new, old), state, kept_state)
        if tick + 1 < sections // 2:
            to_low = lax.ppermute(updated[:, :half], "section", [(i, i - 2) for i in range(2, sections, 2)])
            to_high = lax.ppermute(updated[:, half:], "section", [(i, i - 1) for i in range(2, sections, 2)])
            incoming = jnp.where(side == 0, to_low, to_high)
    result, qg_hi, qg_lo = kept_state
    if not single:
        clips_hi = over_clips("add_pair_hi", *weight_grad("weight_grad_hi", True, over_tiles(qg_hi)))
        clips_lo = over_clips("add_pair_lo", *weight_grad("weight_grad_lo", False, over_tiles(qg_lo)))

    mine, theirs = call(
        add_kernel, [sds((rows, half), BF)] * 2, 20 * rows * half,
        "add_clips", *clips_hi, clips_lo[0], tied(clips_lo[1], result),
    )
    other = swap(theirs)
    first = jnp.where(side == 0, mine, other)
    second = jnp.where(side == 0, other, mine)
    grad_rows = jnp.concatenate([first, second], axis=1)
    return (result[None, None], grad_rows[None])


def solution(mesh):
    placed = (
        P("section", "fsdp", "seq", None),
        P("fsdp", "seq", None),
        P("section", None),
        P("section", None),
        P("section", ("fsdp", "seq"), None),
        P("fsdp", None),
        P("fsdp", "seq"),
    )
    return jax.shard_map(
        per_device,
        mesh=mesh,
        in_specs=placed,
        out_specs=(P("section", "fsdp", "seq", None), P("section", ("fsdp", "seq"), None)),
        check_vma=False,
    )
```

time: 136 us -> 122 us (0.90)
  starting transfers between devices: 64.9 us -> 37.7 us
  waiting for transfers between devices: 47.6 us -> 64.5 us
  Pallas kernels: 17.5 us -> 13.3 us
  local copies, waits for them, and re-layouts: 0.9 us -> 2.64 us
    ppermute x19 -> x12, starting transfers between devices: 25.1 us -> 9.64 us  [across(): return lax.ppermute(value, 'seq', [(s, s ^ offset) for s in range(seqs)])]
    ppermute x13 -> x8, waiting for transfers between devices: 20.5 us -> 33.7 us  [along(): return lax.ppermute(value, 'fsdp', [(f, f ^ flip) for f in range(fsdps)])]
    ppermute x13 -> x8, starting transfers between devices: 24.1 us -> 14.9 us  [along(): return lax.ppermute(value, 'fsdp', [(f, f ^ flip) for f in range(fsdps)])]
    pallas_call x11 -> x15, Pallas kernels: 17.5 us -> 13.3 us  [call(): pl.pallas_call(kernel, out_shape=outs, in_specs=[pl.BlockSpec(memory_spac...]
    ppermute x1, waiting for transfers between devices: 0.77 us -> 4.24 us  [per_device(): sum_other = lax.ppermute(leftsum, ('section', 'seq'), diagonal_pairs)]
    ppermute x6, waiting for transfers between devices: 8.26 us -> 11.7 us  [swap(): return lax.ppermute(value, 'section', swap_pairs)]
    ppermute x19 -> x12, waiting for transfers between devices: 18 us -> 14.8 us  [across(): return lax.ppermute(value, 'seq', [(s, s ^ offset) for s in range(seqs)])]
    ppermute x6, starting transfers between devices: 10.5 us -> 7.95 us  [swap(): return lax.ppermute(value, 'section', swap_pairs)]
  transfers between devices with their start and end apart: 42 -> 30, of which waited for: 15 -> 15; matrix products, arithmetic and copies ran while one was open for 1% -> 0% of each run, Pallas kernels for 11% -> 11%
where the time goes in v2:
time: 122 us
  waiting for transfers between devices  64.5 us (53%)
  starting transfers between devices  37.7 us (31%)
  Pallas kernels  13.3 us (11%)
  local copies, waits for them, and re-layouts  2.64 us (2%)
  other arithmetic  1.87 us (2%)
  between operations  1.62 us (1%)
    ppermute x8, waiting for transfers between devices, along(): return lax.ppermute(value, 'fsdp', [(f, f ^ flip) for f in range(fsdps)])  33.7 us
    ppermute x8, starting transfers between devices, along(): return lax.ppermute(value, 'fsdp', [(f, f ^ flip) for f in range(fsdps)])  14.9 us
    ppermute x12, waiting for transfers between devices, across(): return lax.ppermute(value, 'seq', [(s, s ^ offset) for s in range(seqs)])  14.8 us
    pallas_call x15, Pallas kernels, call(): pl.pallas_call(kernel, out_shape=outs, in_specs=[pl.BlockSpec(memory_spac...  13.3 us
    ppermute x6, waiting for transfers between devices, swap(): return lax.ppermute(value, 'section', swap_pairs)  11.7 us
    ppermute x12, starting transfers between devices, across(): return lax.ppermute(value, 'seq', [(s, s ^ offset) for s in range(seqs)])  9.64 us
    ppermute x6, starting transfers between devices, swap(): return lax.ppermute(value, 'section', swap_pairs)  7.95 us
    ppermute x1, waiting for transfers between devices, per_device(): sum_other = lax.ppermute(leftsum, ('section', 'seq'), diagonal_pairs)  4.24 us
  transfers between devices with their start and end apart: 30, of which 15 were waited for; matrix products, arithmetic and copies ran while one was open for 0% of the time, Pallas kernels for 11%

profile of v2, /device:TPU:0, one launch (start us, length us, event | category | flops | bytes accessed | tf_op | source)
XLA Modules:
  0.0 121.6 jit_solution(6425813088421538729)
XLA Ops:
  0.6 1.0 broadcast_select_fusion.2
  1.7 3.0 %collective-permute-start.1 = (bf16[96,768]{1,0:T(8,128)(2,1)S(1)}, bf16[96,768]{1,0:T(8,128)(2,1)S(1)}, u32[]{:S(2)}, u32[]{:S(2)}) collective-permute-start(bf16[96,768]{1,0:T(8,128)(2,1)S(1)} %get-tuple-element.112), channel_id=1, source_target_pairs={{0,16},{16,0},{1,17},{17,1},{2,18},{18,2},{3,19},{19,3},{4,20},{20... | collective-permute-start | bytes 442376 | tf_op jit(solution)/shard_map/ppermute | solution.py:352
  4.7 1.0 copy-done
  5.7 0.7 copy-done.3
  6.3 0.7 copy-done.4
  7.5 2.1 %collective-permute-start.8 = (bf16[768,128]{1,0:T(8,128)(2,1)S(1)}, bf16[768,128]{1,0:T(8,128)(2,1)S(1)}, u32[]{:S(2)}, u32[]{:S(2)}) collective-permute-start(bf16[768,128]{1,0:T(8,128)(2,1)S(1)} %get-tuple-element.57), channel_id=1, source_target_pairs={{0,2},{1,3},{2,0},{3,1},{4,6},{5,7},{6,4},{7,5},{8,10},{9,11},{10,... | collective-permute-start | bytes 589832 | tf_op jit(solution)/shard_map/ppermute | solution.py:355
  9.7 2.7 %collective-permute-start.2 = (bf16[96,768]{1,0:T(8,128)(2,1)S(1)}, bf16[96,768]{1,0:T(8,128)(2,1)S(1)}, u32[]{:S(2)}, u32[]{:S(2)}) collective-permute-start(bf16[96,768]{1,0:T(8,128)(2,1)S(1)} %get-tuple-element.59), channel_id=1, source_target_pairs={{0,8},{4,12},{8,0},{12,4},{1,9},{5,13},{9,1},{13,5},{2,10},{6,14},... | collective-permute-start | bytes 442376 | tf_op jit(solution)/shard_map/ppermute | solution.py:358
  12.4 1.6 %collective-permute-done.8 = bf16[768,128]{1,0:T(8,128)(2,1)S(1)} collective-permute-done((bf16[768,128]{1,0:T(8,128)(2,1)S(1)}, bf16[768,128]{1,0:T(8,128)(2,1)S(1)}, u32[]{:S(2)}, u32[]{:S(2)}) %collective-permute-start.8) | collective-permute-done | bytes 196640 | tf_op jit(solution)/shard_map/ppermute | solution.py:355
  14.2 4.4 %collective-permute-done.2 = bf16[96,768]{1,0:T(8,128)(2,1)S(1)} collective-permute-done((bf16[96,768]{1,0:T(8,128)(2,1)S(1)}, bf16[96,768]{1,0:T(8,128)(2,1)S(1)}, u32[]{:S(2)}, u32[]{:S(2)}) %collective-permute-start.2) | collective-permute-done | bytes 147488 | tf_op jit(solution)/shard_map/ppermute | solution.py:358
  18.6 0.7 collective-permute-start.5
  19.9 3.4 %collective-permute-start.6 = (bf16[96,768]{1,0:T(8,128)(2,1)S(1)}, bf16[96,768]{1,0:T(8,128)(2,1)S(1)}, u32[]{:S(2)}, u32[]{:S(2)}) collective-permute-start(bf16[96,768]{1,0:T(8,128)(2,1)S(1)} %get-tuple-element.67), channel_id=1, source_target_pairs={{0,8},{4,12},{8,0},{12,4},{1,9},{5,13},{9,1},{13,5},{2,10},{6,14},... | collective-permute-start | bytes 442376 | tf_op jit(solution)/shard_map/ppermute | solution.py:358
  23.4 4.3 %collective-permute-done.3 = bf16[192,768]{1,0:T(8,128)(2,1)S(1)} collective-permute-done((bf16[192,768]{1,0:T(8,128)(2,1)S(1)}, bf16[192,768]{1,0:T(8,128)(2,1)S(1)}, u32[]{:S(2)}, u32[]{:S(2)}) %collective-permute-start.3) | collective-permute-done | bytes 294944 | tf_op jit(solution)/shard_map/ppermute | solution.py:355
  28.1 1.3 %collective-permute-start.4 = (bf16[256,768]{1,0:T(8,128)(2,1)S(1)}, bf16[256,768]{1,0:T(8,128)(2,1)S(1)}, u32[]{:S(2)}, u32[]{:S(2)}) collective-permute-start(bf16[256,768]{1,0:T(8,128)(2,1)S(1)} %get-tuple-element.65.refs_3_.own_keys), channel_id=1, source_target_pairs={{0,1},{1,2},{2,3},{4,5},{5,6},{6,7},{8,9},{9,10},{10,11},{12,13},{... | collective-permute-start | bytes 1179656 | tf_op jit(solution)/shard_map/ppermute | solution.py:426
  29.4 3.4 %collective-permute-start.7 = (bf16[192,768]{1,0:T(8,128)(2,1)S(1)}, bf16[192,768]{1,0:T(8,128)(2,1)S(1)}, u32[]{:S(2)}, u32[]{:S(2)}) collective-permute-start(bf16[192,768]{1,0:T(8,128)(2,1)S(1)} %get-tuple-element.80), channel_id=1, source_target_pairs={{0,4},{4,0},{8,12},{12,8},{1,5},{5,1},{9,13},{13,9},{2,6},{6,2},{1... | collective-permute-start | bytes 884744 | tf_op jit(solution)/shard_map/ppermute | solution.py:358
  33.4 6.3 %collective-permute-done.7 = bf16[192,768]{1,0:T(8,128)(2,1)S(1)} collective-permute-done((bf16[192,768]{1,0:T(8,128)(2,1)S(1)}, bf16[192,768]{1,0:T(8,128)(2,1)S(1)}, u32[]{:S(2)}, u32[]{:S(2)}) %collective-permute-start.7) | collective-permute-done | bytes 294944 | tf_op jit(solution)/shard_map/ppermute | solution.py:358
  39.6 1.2 collective-permute-done.10
  40.9 0.9 collective-permute-start.11
  42.4 2.3 %collective-permute-start.16 = (bf16[192,768]{1,0:T(8,128)(2,1)S(1)}, bf16[192,768]{1,0:T(8,128)(2,1)S(1)}, u32[]{:S(2)}, u32[]{:S(2)}) collective-permute-start(bf16[192,768]{1,0:T(8,128)(2,1)S(1)} %collective-permute-done.7), channel_id=1, source_target_pairs={{0,2},{1,3},{2,0},{3,1},{4,6},{5,7},{6,4},{7,5},{8,10},{9,11},{10,... | collective-permute-start | bytes 884744 | tf_op jit(solution)/shard_map/ppermute | solution.py:355
  44.7 1.5 %forward_hi.1 = (bf16[128,768]{1,0:T(8,128)(2,1)S(1)}, f32[768,256]{1,0:T(8,128)S(1)}, bf16[1536,768]{1,0:T(8,128)(2,1)S(1)}) custom-call(s32[1,1]{1,0:T(1,128)S(6)} %copy.19.refs_0_, bf16[128,1536]{1,0:T(8,128)(2,1)S(1)} %get-tuple-element.64.refs_1_, bf16[256,768]{1,0:T(8,128)(2,1)S(1)} %collective-permute-done.4.refs_2_.left_keys, ...), custom_call_target="tpu_custom_call" | custom-call | flops 352321536 | bytes 6881280 | tf_op jit(solution)/shard_map/forward_hi/pallas_call | solution.py:31
  46.3 2.9 %upper.1 = (bf16[128,768]{1,0:T(8,128)(2,1)S(1)}, f32[128,768]{1,0:T(8,128)S(1)}, bf16[128,896]{1,0:T(8,128)(2,1)S(1)}, bf16[128,768]{1,0:T(8,128)(2,1)S(1)}, f32[128,128]{1,0:T(8,128)S(1)}) custom-call(s32[1,2]{1,0:T(1,128)S(1)} %copy-done.6, bf16[128,768]{1,0:T(8,128)(2,1)S(1)} %get-tuple-element.61.dy, bf16[128,1536]{1,0:T(8,128)(2,1)S(1)} %get-tuple-element.62.acts, ...), custom_call_target="tpu_custom_call" | custom-call | flops 503316480 | bytes 5849088 | tf_op jit(solution)/shard_map/upper/pallas_call | solution.py:31
  49.1 1.3 %collective-permute-start.12 = (bf16[128,896]{1,0:T(8,128)(2,1)S(1)}, bf16[128,896]{1,0:T(8,128)(2,1)S(1)}, u32[]{:S(2)}, u32[]{:S(2)}) collective-permute-start(bf16[128,896]{1,0:T(8,128)(2,1)S(1)} %get-tuple-element.76.msg), channel_id=1, source_target_pairs={{0,16},{16,0},{1,17},{17,1},{2,18},{18,2},{3,19},{19,3},{4,20},{20... | collective-permute-start | bytes 688136 | tf_op jit(solution)/shard_map/ppermute | solution.py:352
  50.5 1.3 %collective-permute-start.13 = (bf16[128,768]{1,0:T(8,128)(2,1)S(1)}, bf16[128,768]{1,0:T(8,128)(2,1)S(1)}, u32[]{:S(2)}, u32[]{:S(2)}) collective-permute-start(bf16[128,768]{1,0:T(8,128)(2,1)S(1)} %get-tuple-element.77), channel_id=1, source_target_pairs={{1,0},{2,1},{3,2},{5,4},{6,5},{7,6},{9,8},{10,9},{11,10},{13,12},{... | collective-permute-start | bytes 589832 | tf_op jit(solution)/shard_map/ppermute | solution.py:482
  51.8 1.3 %collective-permute-start.14 = (f32[128,128]{1,0:T(8,128)S(1)}, f32[128,128]{1,0:T(8,128)S(1)}, u32[]{:S(2)}, u32[]{:S(2)}) collective-permute-start(f32[128,128]{1,0:T(8,128)S(1)} %get-tuple-element.78), channel_id=1, source_target_pairs={{1,16},{2,17},{3,18},{17,0},{18,1},{19,2},{5,20},{6,21},{7,22},{21... | collective-permute-start | bytes 196616 | tf_op jit(solution)/shard_map/ppermute | solution.py:483
  53.1 4.2 %collective-permute-done.14.sum_other = f32[128,128]{1,0:T(8,128)S(1)} collective-permute-done((f32[128,128]{1,0:T(8,128)S(1)}, f32[128,128]{1,0:T(8,128)S(1)}, u32[]{:S(2)}, u32[]{:S(2)}) %collective-permute-start.14) | collective-permute-done | bytes 65568 | tf_op jit(solution)/shard_map/ppermute | solution.py:483
  57.4 0.8 collective-permute-done.15
  58.2 2.7 %collective-permute-start.17 = (bf16[768,768]{1,0:T(8,128)(2,1)S(1)}, bf16[768,768]{1,0:T(8,128)(2,1)S(1)}, u32[]{:S(2)}, u32[]{:S(2)}) collective-permute-start(bf16[768,768]{1,0:T(8,128)(2,1)S(1)} %constant_dynamic-update-slice_fusion.9.refs_4_), channel_id=1, source_target_pairs={{0,1},{1,0},{2,3},{3,2},{4,5},{5,4},{6,7},{7,6},{8,9},{9,8},{10,11... | collective-permute-start | bytes 3538952 | tf_op jit(solution)/shard_map/ppermute | solution.py:355
  60.9 6.9 %collective-permute-done.20.refs_3_ = bf16[128,768]{1,0:T(8,128)(2,1)S(1)} collective-permute-done((bf16[128,768]{1,0:T(8,128)(2,1)S(1)}, bf16[128,768]{1,0:T(8,128)(2,1)S(1)}, u32[]{:S(2)}, u32[]{:S(2)}) %collective-permute-start.20) | collective-permute-done | bytes 196640 | tf_op jit(solution)/shard_map/ppermute | solution.py:355
  67.9 1.3 %collective-permute-start.19 = (bf16[1536,128]{1,0:T(8,128)(2,1)S(1)}, bf16[1536,128]{1,0:T(8,128)(2,1)S(1)}, u32[]{:S(2)}, u32[]{:S(2)}) collective-permute-start(bf16[1536,128]{1,0:T(8,128)(2,1)S(1)} %pad_maximum_fusion.refs_0_), channel_id=1, source_target_pairs={{0,16},{16,0},{1,17},{17,1},{2,18},{18,2},{3,19},{19,3},{4,20},{20... | collective-permute-start | bytes 1179656 | tf_op jit(solution)/shard_map/ppermute | solution.py:352
  69.3 1.5 %forward_lo.1 = (bf16[128,768]{1,0:T(8,128)(2,1)S(1)}, f32[768,256]{1,0:T(8,128)S(1)}, bf16[1536,768]{1,0:T(8,128)(2,1)S(1)}) custom-call(s32[1,1]{1,0:T(1,128)S(6)} %copy.19.refs_0_, bf16[128,1536]{1,0:T(8,128)(2,1)S(1)} %get-tuple-element.79.refs_1_, bf16[256,768]{1,0:T(8,128)(2,1)S(1)} %collective-permute-done.4.refs_2_.left_keys, ...), custom_call_target="tpu_custom_call" | custom-call | flops 352321536 | bytes 6881280 | tf_op jit(solution)/shard_map/forward_lo/pallas_call | solution.py:31
  70.8 2.4 %lower.1 = (bf16[128,768]{1,0:T(8,128)(2,1)S(1)}, bf16[128,768]{1,0:T(8,128)(2,1)S(1)}, f32[128,768]{1,0:T(8,128)S(1)}, bf16[128,768]{1,0:T(8,128)(2,1)S(1)}) custom-call(s32[1,2]{1,0:T(1,128)S(1)} %copy-done.6, f32[128,768]{1,0:T(8,128)S(1)} %get-tuple-element.75.own, bf16[128,896]{1,0:T(8,128)(2,1)S(1)} %get-tuple-element.76.msg, ...), custom_call_target="tpu_custom_call" | custom-call | flops 201326592 | bytes 4505600 | tf_op jit(solution)/shard_map/lower/pallas_call | solution.py:31
  73.5 5.9 %collective-permute-done.19.refs_1_ = bf16[1536,128]{1,0:T(8,128)(2,1)S(1)} collective-permute-done((bf16[1536,128]{1,0:T(8,128)(2,1)S(1)}, bf16[1536,128]{1,0:T(8,128)(2,1)S(1)}, u32[]{:S(2)}, u32[]{:S(2)}) %collective-permute-start.19) | collective-permute-done | bytes 393248 | tf_op jit(solution)/shard_map/ppermute | solution.py:352
  79.4 0.5 weight_grad_hi.1
  80.0 0.7 collective-permute-start.22
  80.8 1.3 %collective-permute-start.18 = (bf16[128,768]{1,0:T(8,128)(2,1)S(1)}, bf16[128,768]{1,0:T(8,128)(2,1)S(1)}, u32[]{:S(2)}, u32[]{:S(2)}) collective-permute-start(bf16[128,768]{1,0:T(8,128)(2,1)S(1)} %get-tuple-element.89), channel_id=1, source_target_pairs={{1,0},{2,1},{3,2},{5,4},{6,5},{7,6},{9,8},{10,9},{11,10},{13,12},{... | collective-permute-start | bytes 589832 | tf_op jit(solution)/shard_map/ppermute | solution.py:496
  82.1 6.5 %collective-permute-done.22.arrived = bf16[192,768]{1,0:T(8,128)(2,1)S(1)} collective-permute-done((bf16[192,768]{1,0:T(8,128)(2,1)S(1)}, bf16[192,768]{1,0:T(8,128)(2,1)S(1)}, u32[]{:S(2)}, u32[]{:S(2)}) %collective-permute-start.22) | collective-permute-done | bytes 294944 | tf_op jit(solution)/shard_map/ppermute | solution.py:358
  88.7 0.9 project_lo.1
  89.6 1.4 %collective-permute-start.23 = (bf16[128,2304]{1,0:T(8,128)(2,1)S(1)}, bf16[128,2304]{1,0:T(8,128)(2,1)S(1)}, u32[]{:S(2)}, u32[]{:S(2)}) collective-permute-start(bf16[128,2304]{1,0:T(8,128)(2,1)S(1)} %get-tuple-element.100), channel_id=1, source_target_pairs={{0,16},{16,0},{1,17},{17,1},{2,18},{18,2},{3,19},{19,3},{4,20},{20... | collective-permute-start | bytes 1769480 | tf_op jit(solution)/shard_map/ppermute | solution.py:352
  91.0 0.5 weight_grad_lo.1
  91.5 0.9 collective-permute-start.27
  92.4 7.8 %collective-permute-done.27.arrived = bf16[192,768]{1,0:T(8,128)(2,1)S(1)} collective-permute-done((bf16[192,768]{1,0:T(8,128)(2,1)S(1)}, bf16[192,768]{1,0:T(8,128)(2,1)S(1)}, u32[]{:S(2)}, u32[]{:S(2)}) %collective-permute-start.27) | collective-permute-done | bytes 294944 | tf_op jit(solution)/shard_map/ppermute | solution.py:358
  100.3 3.0 %collective-permute-start.28 = (bf16[96,768]{1,0:T(8,128)(2,1)S(1)}, bf16[96,768]{1,0:T(8,128)(2,1)S(1)}, u32[]{:S(2)}, u32[]{:S(2)}) collective-permute-start(bf16[96,768]{1,0:T(8,128)(2,1)S(1)} %get-tuple-element.106), channel_id=1, source_target_pairs={{0,8},{4,12},{8,0},{12,4},{1,9},{5,13},{9,1},{13,5},{2,10},{6,14},... | collective-permute-start | bytes 442376 | tf_op jit(solution)/shard_map/ppermute | solution.py:358
  103.4 1.4 %collective-permute-done.23.msg_in = bf16[128,2304]{1,0:T(8,128)(2,1)S(1)} collective-permute-done((bf16[128,2304]{1,0:T(8,128)(2,1)S(1)}, bf16[128,2304]{1,0:T(8,128)(2,1)S(1)}, u32[]{:S(2)}, u32[]{:S(2)}) %collective-permute-start.23) | collective-permute-done | bytes 589856 | tf_op jit(solution)/shard_map/ppermute | solution.py:352
  104.8 2.0 %finish.1 = bf16[128,1536]{1,0:T(8,128)(2,1)} custom-call(s32[1,2]{1,0:T(1,128)S(1)} %copy-done.6, f32[128,1536]{1,0:T(8,128)S(1)} %get-tuple-element.99.part, bf16[128,2304]{1,0:T(8,128)(2,1)S(1)} %collective-permute-done.23.msg_in, bf16[128,1536]{1,0:T(8,128)(2,1)S(1)} %get-tuple-element.101.acts, f32[8,1536]{1,0:T(8,128)S(1)} %get-tuple-element.63.vecs, ...), custom_call_target="tpu_custom_call" | custom-call | flops 3932160 | bytes 2408448 | tf_op jit(solution)/shard_map/finish/pallas_call | solution.py:31
  106.8 7.2 %collective-permute-done.28.lo_arrived = bf16[96,768]{1,0:T(8,128)(2,1)S(1)} collective-permute-done((bf16[96,768]{1,0:T(8,128)(2,1)S(1)}, bf16[96,768]{1,0:T(8,128)(2,1)S(1)}, u32[]{:S(2)}, u32[]{:S(2)}) %collective-permute-start.28) | collective-permute-done | bytes 147488 | tf_op jit(solution)/shard_map/ppermute | solution.py:358
  113.9 1.6 %collective-permute-done.24.hi_arrived = bf16[96,768]{1,0:T(8,128)(2,1)S(1)} collective-permute-done((bf16[96,768]{1,0:T(8,128)(2,1)S(1)}, bf16[96,768]{1,0:T(8,128)(2,1)S(1)}, u32[]{:S(2)}, u32[]{:S(2)}) %collective-permute-start.24) | collective-permute-done | bytes 147488 | tf_op jit(solution)/shard_map/ppermute | solution.py:358
  115.6 0.8 collective-permute-start.29
  116.4 4.4 %collective-permute-done.29 = bf16[96,768]{1,0:T(8,128)(2,1)S(1)} collective-permute-done((bf16[96,768]{1,0:T(8,128)(2,1)S(1)}, bf16[96,768]{1,0:T(8,128)(2,1)S(1)}, u32[]{:S(2)}, u32[]{:S(2)}) %collective-permute-start.29) | collective-permute-done | bytes 147488 | tf_op jit(solution)/shard_map/ppermute | solution.py:352
  120.9 0.7 maximum_bitcast_fusion
  (60 shorter events, 3.4 us)
Async XLA Ops:
  1.7 8.0 %collective-permute-start.1 = (bf16[96,768]{1,0:T(8,128)(2,1)S(1)}, bf16[96,768]{1,0:T(8,128)(2,1)S(1)}, u32[]{:S(2)}, u32[]{:S(2)}) collective-permute-start(bf16[96,768]{1,0:T(8,128)(2,1)S(1)} %get-tuple-element.112), channel_id=1, source_target_pairs={{0,16},{16,0},{1,17},{17,1},{2,18},{18,2},{3,19},{19,3},{4,20},{20... | collective-permute-start | bytes 442376 | tf_op jit(solution)/shard_map/ppermute | solution.py:352
  4.7 1.0 copy-start
  5.7 0.7 copy-start.3
  6.3 0.7 copy-start.4
  7.1 12.8 %collective-permute-start = (bf16[144,1536]{1,0:T(8,128)(2,1)S(1)}, bf16[144,1536]{1,0:T(8,128)(2,1)S(1)}, u32[]{:S(2)}, u32[]{:S(2)}) collective-permute-start(bf16[144,1536]{1,0:T(8,128)(2,1)S(1)} %pack.1), channel_id=1, source_target_pairs={{0,16},{16,0},{1,17},{17,1},{2,18},{18,2},{3,19},{19,3},{4,20},{20... | collective-permute-start | bytes 1327112 | tf_op jit(solution)/shard_map/ppermute | solution.py:352
  7.5 6.5 %collective-permute-start.8 = (bf16[768,128]{1,0:T(8,128)(2,1)S(1)}, bf16[768,128]{1,0:T(8,128)(2,1)S(1)}, u32[]{:S(2)}, u32[]{:S(2)}) collective-permute-start(bf16[768,128]{1,0:T(8,128)(2,1)S(1)} %get-tuple-element.57), channel_id=1, source_target_pairs={{0,2},{1,3},{2,0},{3,1},{4,6},{5,7},{6,4},{7,5},{8,10},{9,11},{10,... | collective-permute-start | bytes 589832 | tf_op jit(solution)/shard_map/ppermute | solution.py:355
  9.7 8.9 %collective-permute-start.2 = (bf16[96,768]{1,0:T(8,128)(2,1)S(1)}, bf16[96,768]{1,0:T(8,128)(2,1)S(1)}, u32[]{:S(2)}, u32[]{:S(2)}) collective-permute-start(bf16[96,768]{1,0:T(8,128)(2,1)S(1)} %get-tuple-element.59), channel_id=1, source_target_pairs={{0,8},{4,12},{8,0},{12,4},{1,9},{5,13},{9,1},{13,5},{2,10},{6,14},... | collective-permute-start | bytes 442376 | tf_op jit(solution)/shard_map/ppermute | solution.py:358
  14.0 13.6 %copy-start.1 = (bf16[1,1,128,1536]{3,2,1,0:T(8,128)(2,1)S(1)}, bf16[1,1,128,1536]{3,2,1,0:T(8,128)(2,1)}, u32[]{:S(2)}) copy-start(bf16[1,1,128,1536]{3,2,1,0:T(8,128)(2,1)} %param.7) | copy-start | bytes 1179652
  14.0 13.6 %copy-start.2 = (bf16[1,128,1536]{2,1,0:T(8,128)(2,1)S(1)}, bf16[1,128,1536]{2,1,0:T(8,128)(2,1)}, u32[]{:S(2)}) copy-start(bf16[1,128,1536]{2,1,0:T(8,128)(2,1)} %param.8) | copy-start | bytes 1179652
  14.1 13.6 %copy-start.5 = (f32[1,1536]{1,0:T(1,128)S(1)}, f32[1,1536]{1,0:T(1,128)}, u32[]{:S(2)}) copy-start(f32[1,1536]{1,0:T(1,128)} %gate.3) | copy-start | bytes 18436
  14.1 9.2 %collective-permute-start.9 = (bf16[768,128]{1,0:T(8,128)(2,1)S(1)}, bf16[768,128]{1,0:T(8,128)(2,1)S(1)}, u32[]{:S(2)}, u32[]{:S(2)}) collective-permute-start(bf16[768,128]{1,0:T(8,128)(2,1)S(1)} %pad_maximum_fusion.3), channel_id=1, source_target_pairs={{0,1},{1,0},{2,3},{3,2},{4,5},{5,4},{6,7},{7,6},{8,9},{9,8},{10,11... | collective-permute-start | bytes 589832 | tf_op jit(solution)/shard_map/ppermute | solution.py:355
  18.6 14.2 %collective-permute-start.5 = (bf16[192,768]{1,0:T(8,128)(2,1)S(1)}, bf16[192,768]{1,0:T(8,128)(2,1)S(1)}, u32[]{:S(2)}, u32[]{:S(2)}) collective-permute-start(bf16[192,768]{1,0:T(8,128)(2,1)S(1)} %get-tuple-element.123), channel_id=1, source_target_pairs={{0,4},{4,0},{8,12},{12,8},{1,5},{5,1},{9,13},{13,9},{2,6},{6,2},{1... | collective-permute-start | bytes 884744 | tf_op jit(solution)/shard_map/ppermute | solution.py:358
  19.4 8.3 %collective-permute-start.3 = (bf16[192,768]{1,0:T(8,128)(2,1)S(1)}, bf16[192,768]{1,0:T(8,128)(2,1)S(1)}, u32[]{:S(2)}, u32[]{:S(2)}) collective-permute-start(bf16[192,768]{1,0:T(8,128)(2,1)S(1)} %get-tuple-element.123), channel_id=1, source_target_pairs={{0,2},{1,3},{2,0},{3,1},{4,6},{5,7},{6,4},{7,5},{8,10},{9,11},{10,... | collective-permute-start | bytes 884744 | tf_op jit(solution)/shard_map/ppermute | solution.py:355
  19.9 9.5 %collective-permute-start.6 = (bf16[96,768]{1,0:T(8,128)(2,1)S(1)}, bf16[96,768]{1,0:T(8,128)(2,1)S(1)}, u32[]{:S(2)}, u32[]{:S(2)}) collective-permute-start(bf16[96,768]{1,0:T(8,128)(2,1)S(1)} %get-tuple-element.67), channel_id=1, source_target_pairs={{0,8},{4,12},{8,0},{12,4},{1,9},{5,13},{9,1},{13,5},{2,10},{6,14},... | collective-permute-start | bytes 442376 | tf_op jit(solution)/shard_map/ppermute | solution.py:358
  28.1 12.7 %collective-permute-start.4 = (bf16[256,768]{1,0:T(8,128)(2,1)S(1)}, bf16[256,768]{1,0:T(8,128)(2,1)S(1)}, u32[]{:S(2)}, u32[]{:S(2)}) collective-permute-start(bf16[256,768]{1,0:T(8,128)(2,1)S(1)} %get-tuple-element.65.refs_3_.own_keys), channel_id=1, source_target_pairs={{0,1},{1,2},{2,3},{4,5},{5,6},{6,7},{8,9},{9,10},{10,11},{12,13},{... | collective-permute-start | bytes 1179656 | tf_op jit(solution)/shard_map/ppermute | solution.py:426
  29.4 10.2 %collective-permute-start.7 = (bf16[192,768]{1,0:T(8,128)(2,1)S(1)}, bf16[192,768]{1,0:T(8,128)(2,1)S(1)}, u32[]{:S(2)}, u32[]{:S(2)}) collective-permute-start(bf16[192,768]{1,0:T(8,128)(2,1)S(1)} %get-tuple-element.80), channel_id=1, source_target_pairs={{0,4},{4,0},{8,12},{12,8},{1,5},{5,1},{9,13},{13,9},{2,6},{6,2},{1... | collective-permute-start | bytes 884744 | tf_op jit(solution)/shard_map/ppermute | solution.py:358
  32.8 8.0 %collective-permute-start.10 = (bf16[192,768]{1,0:T(8,128)(2,1)S(1)}, bf16[192,768]{1,0:T(8,128)(2,1)S(1)}, u32[]{:S(2)}, u32[]{:S(2)}) collective-permute-start(bf16[192,768]{1,0:T(8,128)(2,1)S(1)} %collective-permute-done.5), channel_id=1, source_target_pairs={{0,2},{1,3},{2,0},{3,1},{4,6},{5,7},{6,4},{7,5},{8,10},{9,11},{10,... | collective-permute-start | bytes 884744 | tf_op jit(solution)/shard_map/ppermute | solution.py:355
  40.9 3.9 %collective-permute-start.11 = (bf16[768,768]{1,0:T(8,128)(2,1)S(1)}, bf16[768,768]{1,0:T(8,128)(2,1)S(1)}, u32[]{:S(2)}, u32[]{:S(2)}) collective-permute-start(bf16[768,768]{1,0:T(8,128)(2,1)S(1)} %constant_dynamic-update-slice_fusion.4.refs_4_), channel_id=1, source_target_pairs={{0,1},{1,0},{2,3},{3,2},{4,5},{5,4},{6,7},{7,6},{8,9},{9,8},{10,11... | collective-permute-start | bytes 3538952 | tf_op jit(solution)/shard_map/ppermute | solution.py:355
  42.4 10.7 %collective-permute-start.16 = (bf16[192,768]{1,0:T(8,128)(2,1)S(1)}, bf16[192,768]{1,0:T(8,128)(2,1)S(1)}, u32[]{:S(2)}, u32[]{:S(2)}) collective-permute-start(bf16[192,768]{1,0:T(8,128)(2,1)S(1)} %collective-permute-done.7), channel_id=1, source_target_pairs={{0,2},{1,3},{2,0},{3,1},{4,6},{5,7},{6,4},{7,5},{8,10},{9,11},{10,... | collective-permute-start | bytes 884744 | tf_op jit(solution)/shard_map/ppermute | solution.py:355
  44.7 13.5 %collective-permute-start.15 = (bf16[192,768]{1,0:T(8,128)(2,1)S(1)}, bf16[192,768]{1,0:T(8,128)(2,1)S(1)}, u32[]{:S(2)}, u32[]{:S(2)}) collective-permute-start(bf16[192,768]{1,0:T(8,128)(2,1)S(1)} %get-tuple-element.80), channel_id=1, source_target_pairs={{0,2},{1,3},{2,0},{3,1},{4,6},{5,7},{6,4},{7,5},{8,10},{9,11},{10,... | collective-permute-start | bytes 884744 | tf_op jit(solution)/shard_map/ppermute | solution.py:355
  44.7 1.5 %copy-start.6 = (s32[1,2]{1,0:T(1,128)S(1)}, s32[1,2]{1,0:T(1,128)}, u32[]{:S(2)}) copy-start(s32[1,2]{1,0:T(1,128)} %kept.5) | copy-start | bytes 28
  49.1 8.2 %collective-permute-start.12 = (bf16[128,896]{1,0:T(8,128)(2,1)S(1)}, bf16[128,896]{1,0:T(8,128)(2,1)S(1)}, u32[]{:S(2)}, u32[]{:S(2)}) collective-permute-start(bf16[128,896]{1,0:T(8,128)(2,1)S(1)} %get-tuple-element.76.msg), channel_id=1, source_target_pairs={{0,16},{16,0},{1,17},{17,1},{2,18},{18,2},{3,19},{19,3},{4,20},{20... | collective-permute-start | bytes 688136 | tf_op jit(solution)/shard_map/ppermute | solution.py:352
  50.5 6.9 %collective-permute-start.13 = (bf16[128,768]{1,0:T(8,128)(2,1)S(1)}, bf16[128,768]{1,0:T(8,128)(2,1)S(1)}, u32[]{:S(2)}, u32[]{:S(2)}) collective-permute-start(bf16[128,768]{1,0:T(8,128)(2,1)S(1)} %get-tuple-element.77), channel_id=1, source_target_pairs={{1,0},{2,1},{3,2},{5,4},{6,5},{7,6},{9,8},{10,9},{11,10},{13,12},{... | collective-permute-start | bytes 589832 | tf_op jit(solution)/shard_map/ppermute | solution.py:482
  51.8 5.6 %collective-permute-start.14 = (f32[128,128]{1,0:T(8,128)S(1)}, f32[128,128]{1,0:T(8,128)S(1)}, u32[]{:S(2)}, u32[]{:S(2)}) collective-permute-start(f32[128,128]{1,0:T(8,128)S(1)} %get-tuple-element.78), channel_id=1, source_target_pairs={{1,16},{2,17},{3,18},{17,0},{18,1},{19,2},{5,20},{6,21},{7,22},{21... | collective-permute-start | bytes 196616 | tf_op jit(solution)/shard_map/ppermute | solution.py:483
  58.2 11.0 %collective-permute-start.17 = (bf16[768,768]{1,0:T(8,128)(2,1)S(1)}, bf16[768,768]{1,0:T(8,128)(2,1)S(1)}, u32[]{:S(2)}, u32[]{:S(2)}) collective-permute-start(bf16[768,768]{1,0:T(8,128)(2,1)S(1)} %constant_dynamic-update-slice_fusion.9.refs_4_), channel_id=1, source_target_pairs={{0,1},{1,0},{2,3},{3,2},{4,5},{5,4},{6,7},{7,6},{8,9},{9,8},{10,11... | collective-permute-start | bytes 3538952 | tf_op jit(solution)/shard_map/ppermute | solution.py:355
  60.9 6.9 %collective-permute-start.20 = (bf16[128,768]{1,0:T(8,128)(2,1)S(1)}, bf16[128,768]{1,0:T(8,128)(2,1)S(1)}, u32[]{:S(2)}, u32[]{:S(2)}) collective-permute-start(bf16[128,768]{1,0:T(8,128)(2,1)S(1)} %get-tuple-element.92.refs_2_), channel_id=1, source_target_pairs={{0,2},{1,3},{2,0},{3,1},{4,6},{5,7},{6,4},{7,5},{8,10},{9,11},{10,... | collective-permute-start | bytes 589832 | tf_op jit(solution)/shard_map/ppermute | solution.py:355
  67.8 5.7 %collective-permute-start.21 = (bf16[256,768]{1,0:T(8,128)(2,1)S(1)}, bf16[256,768]{1,0:T(8,128)(2,1)S(1)}, u32[]{:S(2)}, u32[]{:S(2)}) collective-permute-start(bf16[256,768]{1,0:T(8,128)(2,1)S(1)} %pad_maximum_fusion.1), channel_id=1, source_target_pairs={{0,1},{1,0},{2,3},{3,2},{4,5},{5,4},{6,7},{7,6},{8,9},{9,8},{10,11... | collective-permute-start | bytes 1179656 | tf_op jit(solution)/shard_map/ppermute | solution.py:355
  67.9 11.5 %collective-permute-start.19 = (bf16[1536,128]{1,0:T(8,128)(2,1)S(1)}, bf16[1536,128]{1,0:T(8,128)(2,1)S(1)}, u32[]{:S(2)}, u32[]{:S(2)}) collective-permute-start(bf16[1536,128]{1,0:T(8,128)(2,1)S(1)} %pad_maximum_fusion.refs_0_), channel_id=1, source_target_pairs={{0,16},{16,0},{1,17},{17,1},{2,18},{18,2},{3,19},{19,3},{4,20},{20... | collective-permute-start | bytes 1179656 | tf_op jit(solution)/shard_map/ppermute | solution.py:352
  73.2 7.6 %collective-permute-start.25 = (bf16[128,768]{1,0:T(8,128)(2,1)S(1)}, bf16[128,768]{1,0:T(8,128)(2,1)S(1)}, u32[]{:S(2)}, u32[]{:S(2)}) collective-permute-start(bf16[128,768]{1,0:T(8,128)(2,1)S(1)} %get-tuple-element.86.qg.refs_2_), channel_id=1, source_target_pairs={{0,2},{1,3},{2,0},{3,1},{4,6},{5,7},{6,4},{7,5},{8,10},{9,11},{10,... | collective-permute-start | bytes 589832 | tf_op jit(solution)/shard_map/ppermute | solution.py:355
  80.0 8.6 %collective-permute-start.22 = (bf16[192,768]{1,0:T(8,128)(2,1)S(1)}, bf16[192,768]{1,0:T(8,128)(2,1)S(1)}, u32[]{:S(2)}, u32[]{:S(2)}) collective-permute-start(bf16[192,768]{1,0:T(8,128)(2,1)S(1)} %get-tuple-element.95), channel_id=1, source_target_pairs={{0,4},{4,0},{8,12},{12,8},{1,5},{5,1},{9,13},{13,9},{2,6},{6,2},{1... | collective-permute-start | bytes 884744 | tf_op jit(solution)/shard_map/ppermute | solution.py:358
  80.8 10.2 %collective-permute-start.26 = (bf16[256,768]{1,0:T(8,128)(2,1)S(1)}, bf16[256,768]{1,0:T(8,128)(2,1)S(1)}, u32[]{:S(2)}, u32[]{:S(2)}) collective-permute-start(bf16[256,768]{1,0:T(8,128)(2,1)S(1)} %pad_maximum_fusion.2), channel_id=1, source_target_pairs={{0,1},{1,0},{2,3},{3,2},{4,5},{5,4},{6,7},{7,6},{8,9},{9,8},{10,11... | collective-permute-start | bytes 1179656 | tf_op jit(solution)/shard_map/ppermute | solution.py:355
  80.8 7.9 %collective-permute-start.18 = (bf16[128,768]{1,0:T(8,128)(2,1)S(1)}, bf16[128,768]{1,0:T(8,128)(2,1)S(1)}, u32[]{:S(2)}, u32[]{:S(2)}) collective-permute-start(bf16[128,768]{1,0:T(8,128)(2,1)S(1)} %get-tuple-element.89), channel_id=1, source_target_pairs={{1,0},{2,1},{3,2},{5,4},{6,5},{7,6},{9,8},{10,9},{11,10},{13,12},{... | collective-permute-start | bytes 589832 | tf_op jit(solution)/shard_map/ppermute | solution.py:496
  89.6 15.2 %collective-permute-start.23 = (bf16[128,2304]{1,0:T(8,128)(2,1)S(1)}, bf16[128,2304]{1,0:T(8,128)(2,1)S(1)}, u32[]{:S(2)}, u32[]{:S(2)}) collective-permute-start(bf16[128,2304]{1,0:T(8,128)(2,1)S(1)} %get-tuple-element.100), channel_id=1, source_target_pairs={{0,16},{16,0},{1,17},{17,1},{2,18},{18,2},{3,19},{19,3},{4,20},{20... | collective-permute-start | bytes 1769480 | tf_op jit(solution)/shard_map/ppermute | solution.py:352
  91.5 8.7 %collective-permute-start.27 = (bf16[192,768]{1,0:T(8,128)(2,1)S(1)}, bf16[192,768]{1,0:T(8,128)(2,1)S(1)}, u32[]{:S(2)}, u32[]{:S(2)}) collective-permute-start(bf16[192,768]{1,0:T(8,128)(2,1)S(1)} %get-tuple-element.104), channel_id=1, source_target_pairs={{0,4},{4,0},{8,12},{12,8},{1,5},{5,1},{9,13},{13,9},{2,6},{6,2},{1... | collective-permute-start | bytes 884744 | tf_op jit(solution)/shard_map/ppermute | solution.py:358
  100.3 13.6 %collective-permute-start.28 = (bf16[96,768]{1,0:T(8,128)(2,1)S(1)}, bf16[96,768]{1,0:T(8,128)(2,1)S(1)}, u32[]{:S(2)}, u32[]{:S(2)}) collective-permute-start(bf16[96,768]{1,0:T(8,128)(2,1)S(1)} %get-tuple-element.106), channel_id=1, source_target_pairs={{0,8},{4,12},{8,0},{12,4},{1,9},{5,13},{9,1},{13,5},{2,10},{6,14},... | collective-permute-start | bytes 442376 | tf_op jit(solution)/shard_map/ppermute | solution.py:358
  103.3 12.2 %collective-permute-start.24 = (bf16[96,768]{1,0:T(8,128)(2,1)S(1)}, bf16[96,768]{1,0:T(8,128)(2,1)S(1)}, u32[]{:S(2)}, u32[]{:S(2)}) collective-permute-start(bf16[96,768]{1,0:T(8,128)(2,1)S(1)} %get-tuple-element.102), channel_id=1, source_target_pairs={{0,8},{4,12},{8,0},{12,4},{1,9},{5,13},{9,1},{13,5},{2,10},{6,14},... | collective-permute-start | bytes 442376 | tf_op jit(solution)/shard_map/ppermute | solution.py:358
  115.6 5.2 %collective-permute-start.29 = (bf16[96,768]{1,0:T(8,128)(2,1)S(1)}, bf16[96,768]{1,0:T(8,128)(2,1)S(1)}, u32[]{:S(2)}, u32[]{:S(2)}) collective-permute-start(bf16[96,768]{1,0:T(8,128)(2,1)S(1)} %get-tuple-element.109), channel_id=1, source_target_pairs={{0,16},{16,0},{1,17},{17,1},{2,18},{18,2},{3,19},{19,3},{4,20},{20... | collective-permute-start | bytes 442376 | tf_op jit(solution)/shard_map/ppermute | solution.py:352

commit v3 on v2

--- a/solution.py
+++ b/solution.py
@@ -254,7 +254,7 @@
         key_own[:, at] = key_grad[tile:]
 
 
-def project_kernel(qg, weights, key_own, left_in, dy, part_out, msg):
+def project_kernel(qg, weights, key_own, left_in, part_out, msg):
     half = qg.shape[1]
     side = my_side()
     part = mm(qg[...], weights[...], NT)
@@ -264,20 +264,18 @@
     part_out[:, :half] = first
     part_out[:, half:] = second
     msg[:, :half] = first.astype(BF)
-    msg[:, half : 2 * half] = second.astype(BF)
-    msg[:, 2 * half :] = dy[...]
-
-
-def finish_kernel(kept, part, msg_in, acts, vecs, dy_mine, out):
-    half = dy_mine.shape[1]
-    side = my_side()
-    mine, other = dy_mine[...], msg_in[:, 2 * half :]
+    msg[:, half:] = second.astype(BF)
+
+
+def finish_kernel(kept, part, msg_in, acts, vecs, dy_mine, dy_in, out):
+    side = my_side()
+    mine, other = dy_mine[...], dy_in[...]
     first = jnp.where(side == 0, mine, other)
     second = jnp.where(side == 0, other, mine)
     dy = jnp.concatenate([first, second], axis=1)
     x = acts[...].astype(F32)
     inv = inverse_rms(x)
-    scaled = (part[...] + msg_in[:, : 2 * half].astype(F32)) * vecs[2:3, :]
+    scaled = (part[...] + msg_in[...].astype(F32)) * vecs[2:3, :]
     mean_term = jnp.mean(x * scaled, axis=-1, keepdims=True)
     change = inv * (scaled - x * inv * inv * mean_term)
     updated = jnp.where(is_kept(kept, False), (dy.astype(F32) + change).astype(BF), dy)
@@ -405,11 +403,13 @@
             sent[-1] = tied(sent[-1], *after_last)
         return [across(value, top) for value in sent]
 
-    def between_cores(near, far, after=()):
+    def between_cores(near, far, after=(), apart=False):
         if after:
             far = [tied(value, *after) for value in far]
-        held = [join(near + far)]
-        places = [[(f, 0) for f in flips] + [(f, top) for f in flips]]
+        places = [[(f, 0) for f in flips], [(f, top) for f in flips]]
+        held = [join(near), join(far)]
+        if not apart:
+            held, places = [join(held)], [places[0] + places[1]]
         for bit in bits[1:]:
             held = held + [across(v, bit) for v in held]
             places = places + [[(f, o ^ bit) for f, o in place] for place in places]
@@ -425,10 +425,11 @@
     )
     left = lax.ppermute(keys, "seq", right_pairs)
     near_lo = over_fsdp(tied(w_lo, near_hi[1], packed_in))
-    blocks_hi, places = between_cores(near_hi, far_hi, after=[near_lo[-1], left])
+    parts_other = swap(tied(parts_own, packed_in))
+    blocks_hi, places = between_cores(near_hi, far_hi, after=[near_lo[-1], left, parts_other])
     far_lo = over_seq(near_lo, after=[left])
 
-    def forward(name, which, normed, blocks):
+    def forward(name, which, normed, blocks, places):
         return call(
             lambda *refs: forward_kernel(which, places, rows, *refs),
             [sds((tile, half), BF), sds((half // HDIM * tile, 2 * tile), F32), sds((dim, half), BF)],
@@ -436,11 +437,14 @@
             name, normed, left, keys, *blocks, scalars=[links],
         )
 
-    query_hi, probs_hi, weights_hi = forward("forward_hi", 0, normed_hi, blocks_hi)
-    def over_tiles(query_grad):
+    query_hi, probs_hi, weights_hi = forward("forward_hi", 0, normed_hi, blocks_hi, places)
+    def over_tiles(query_grad, after=()):
         gathered = [query_grad]
         for bit in bits:
-            gathered = gathered + [across(join(gathered), bit)]
+            arrived = across(join(gathered), bit)
+            if after and bit == top:
+                arrived = tied(arrived, *after)
+            gathered = gathered + [arrived]
         return gathered
 
     def weight_grad(name, section_hi, gathered):
@@ -453,8 +457,9 @@
             scratch=[pltpu.VMEM((fsdps * rows, half), BF)],
         )
 
-    def over_clips(name, mine, sent):
-        arrived = along(sent, steps[-1])
+    def over_clips(name, mine, arrived, after=()):
+        if after:
+            arrived = tied(arrived, *after)
         for step in reversed(steps[:-1]):
             count = mine.shape[0] // 2
             mine, sent = call(
@@ -483,9 +488,8 @@
         sum_other = lax.ppermute(leftsum, ("section", "seq"), diagonal_pairs)
         exchanged = [msg_in, left_in, sum_other]
         if tick == 0:
-            parts_other = swap(tied(parts_own, msg_in))
-            blocks_lo, _ = between_cores(near_lo, far_lo, after=exchanged)
-            query_lo, probs_lo, weights_lo = forward("forward_lo", 1, normed_lo, blocks_lo)
+            blocks_lo, places_lo = between_cores(near_lo, far_lo, after=exchanged, apart=True)
+            query_lo, probs_lo, weights_lo = forward("forward_lo", 1, normed_lo, blocks_lo, places_lo)
         dy_mid, qg_lo, key_own, leftward_lo = call(
             lower_kernel,
             [sds((tile, half), BF), sds((tile, half), BF), sds((tile, half), F32), sds((tile, half), BF)],
@@ -494,20 +498,27 @@
             query_lo, probs_lo, left, keys, scalars=[kept],
         )
         left_in_lo = lax.ppermute(leftward_lo, "seq", left_pairs)
+        dy_in = swap(dy_mid)
         if single:
-            gathered_hi = over_tiles(tied(qg_hi, *exchanged))
-            gathered_hi[-1] = tied(gathered_hi[-1], qg_lo)
-            clips_hi = over_clips("add_pair_hi", *weight_grad("weight_grad_hi", True, gathered_hi))
-            clips_lo = over_clips("add_pair_lo", *weight_grad("weight_grad_lo", False, over_tiles(qg_lo)))
-            left_in_lo = tied(left_in_lo, clips_hi[0])
+            gathered_hi = over_tiles(tied(qg_hi, *exchanged), after=[qg_lo])
+            mine_hi, sent_hi = weight_grad("weight_grad_hi", True, gathered_hi)
+            first_hi = along(sent_hi, steps[-1])
+            left_in_lo = tied(left_in_lo, mine_hi)
         part_lo, msg_lo = call(
-            project_kernel, [sds((tile, dim), F32), sds((tile, dim + half), BF)], matmul_flops,
-            "project_lo", qg_lo, weights_lo, key_own, left_in_lo, dy_mid,
+            project_kernel, [sds((tile, dim), F32), sds((tile, dim), BF)], matmul_flops,
+            "project_lo", qg_lo, weights_lo, key_own, left_in_lo,
         )
-        msg_lo_in = swap(msg_lo)
+        if single:
+            gathered_lo = over_tiles(qg_lo, after=[first_hi, msg_lo, dy_in])
+            clips_hi = over_clips("add_pair_hi", mine_hi, first_hi)
+            gathered_lo[-1] = tied(gathered_lo[-1], clips_hi[0])
+            mine_lo, sent_lo = weight_grad("weight_grad_lo", False, gathered_lo)
+            first_lo = along(sent_lo, steps[-1])
+            clips_lo = over_clips("add_pair_lo", mine_lo, first_lo, after=clips_hi[1:])
+        msg_lo_in = lax.ppermute(msg_lo, "section", [(i + 1, i) for i in range(0, sections, 2)])
         (updated,) = call(
             finish_kernel, [sds((tile, dim), BF)], 20 * tile * dim,
-            "finish", part_lo, msg_lo_in, x_lo, vecs, dy_mid, scalars=[kept],
+            "finish", part_lo, msg_lo_in, x_lo, vecs, dy_mid, dy_in, scalars=[kept],
         )
         state = (updated, qg_hi, qg_lo)
         if kept_state is None:
@@ -521,8 +532,11 @@
             incoming = jnp.where(side == 0, to_low, to_high)
     result, qg_hi, qg_lo = kept_state
     if not single:
-        clips_hi = over_clips("add_pair_hi", *weight_grad("weight_grad_hi", True, over_tiles(qg_hi)))
-        clips_lo = over_clips("add_pair_lo", *weight_grad("weight_grad_lo", False, over_tiles(qg_lo)))
+        clips = []
+        for name, section_hi, query_grad in (("hi", True, qg_hi), ("lo", False, qg_lo)):
+            mine, sent = weight_grad("weight_grad_" + name, section_hi, over_tiles(query_grad))
+            clips.append(over_clips("add_pair_" + name, mine, along(sent, steps[-1])))
+        clips_hi, clips_lo = clips
 
     mine, theirs = call(
         add_kernel, [sds((rows, half), BF)] * 2, 20 * rows * half,

time: 122 us -> 113 us (0.926)
  waiting for transfers between devices: 64.5 us -> 49.4 us
  starting transfers between devices: 37.7 us -> 43.6 us
    ppermute x8, waiting for transfers between devices: 33.7 us -> 26.1 us  [along(): return lax.ppermute(value, 'fsdp', [(f, f ^ flip) for f in range(fsdps)])]
    ppermute x6, waiting for transfers between devices: 11.7 us -> 7.71 us  [swap(): return lax.ppermute(value, 'section', swap_pairs)]
    ppermute x12 -> x13, starting transfers between devices: 9.64 us -> 12.7 us  [across(): return lax.ppermute(value, 'seq', [(s, s ^ offset) for s in range(seqs)])]
    ppermute x6, starting transfers between devices: 7.95 us -> 9.82 us  [swap(): return lax.ppermute(value, 'section', swap_pairs)]
    ppermute x1, waiting for transfers between devices: 4.24 us -> 2.42 us  [per_device(): sum_other = lax.ppermute(leftsum, ('section', 'seq'), diagonal_pairs)]
    ppermute x12 -> x13, waiting for transfers between devices: 14.8 us -> 13.1 us  [across(): return lax.ppermute(value, 'seq', [(s, s ^ offset) for s in range(seqs)])]
    ppermute x0 -> x1, starting transfers between devices: none -> 1.28 us  [per_device(): lax.ppermute(msg_lo, 'section', [(i + 1, i) for i in range(0, sections, 2)])]
    unnamed x22 -> x19, local copies, waits for them, and re-layouts: 2.57 us -> 2.54 us
  transfers between devices with their start and end apart: 30 -> 32, of which waited for: 15 -> 19; matrix products, arithmetic and copies ran while one was open for 0% -> 0% of each run, Pallas kernels for 11% -> 11%
where the time goes in v3:
time: 113 us; the launch traced here: 112 us
  waiting for transfers between devices  49.4 us (44%)
  starting transfers between devices  43.6 us (39%)
  Pallas kernels  13.2 us (12%)
  local copies, waits for them, and re-layouts  2.63 us (2%)
  other arithmetic  1.87 us (2%)
  between operations  1.62 us (1%)
    ppermute x8, waiting for transfers between devices, along(): return lax.ppermute(value, 'fsdp', [(f, f ^ flip) for f in range(fsdps)])  26.1 us
    ppermute x8, starting transfers between devices, along(): return lax.ppermute(value, 'fsdp', [(f, f ^ flip) for f in range(fsdps)])  14.6 us
    pallas_call x15, Pallas kernels, call(): pl.pallas_call(kernel, out_shape=outs, in_specs=[pl.BlockSpec(memory_spac...  13.2 us
    ppermute x13, waiting for transfers between devices, across(): return lax.ppermute(value, 'seq', [(s, s ^ offset) for s in range(seqs)])  13.1 us
    ppermute x13, starting transfers between devices, across(): return lax.ppermute(value, 'seq', [(s, s ^ offset) for s in range(seqs)])  12.7 us
    ppermute x6, starting transfers between devices, swap(): return lax.ppermute(value, 'section', swap_pairs)  9.82 us
    ppermute x6, waiting for transfers between devices, swap(): return lax.ppermute(value, 'section', swap_pairs)  7.71 us
    unnamed x19, local copies, waits for them, and re-layouts  2.54 us
  transfers between devices with their start and end apart: 32, of which 19 were waited for; matrix products, arithmetic and copies ran while one was open for 0% of the time, Pallas kernels for 11%

profile of v3, /device:TPU:0, one launch (start us, length us, event | category | flops | bytes accessed | tf_op | source)
XLA Modules:
  0.0 112.3 jit_solution(14104331947522963487)
XLA Ops:
  0.6 1.0 broadcast_select_fusion.2
  1.7 3.0 %collective-permute-start.1 = (bf16[96,768]{1,0:T(8,128)(2,1)S(1)}, bf16[96,768]{1,0:T(8,128)(2,1)S(1)}, u32[]{:S(2)}, u32[]{:S(2)}) collective-permute-start(bf16[96,768]{1,0:T(8,128)(2,1)S(1)} %get-tuple-element.118), channel_id=1, source_target_pairs={{0,16},{16,0},{1,17},{17,1},{2,18},{18,2},{3,19},{19,3},{4,20},{20... | collective-permute-start | bytes 442376 | tf_op jit(solution)/shard_map/ppermute | solution.py:350
  4.7 1.0 copy-done
  6.7 1.6 %collective-permute-start.8 = (bf16[768,128]{1,0:T(8,128)(2,1)S(1)}, bf16[768,128]{1,0:T(8,128)(2,1)S(1)}, u32[]{:S(2)}, u32[]{:S(2)}) collective-permute-start(bf16[768,128]{1,0:T(8,128)(2,1)S(1)} %get-tuple-element.60), channel_id=1, source_target_pairs={{0,2},{1,3},{2,0},{3,1},{4,6},{5,7},{6,4},{7,5},{8,10},{9,11},{10,... | collective-permute-start | bytes 589832 | tf_op jit(solution)/shard_map/ppermute | solution.py:353
  9.7 2.7 %collective-permute-start.2 = (bf16[96,768]{1,0:T(8,128)(2,1)S(1)}, bf16[96,768]{1,0:T(8,128)(2,1)S(1)}, u32[]{:S(2)}, u32[]{:S(2)}) collective-permute-start(bf16[96,768]{1,0:T(8,128)(2,1)S(1)} %get-tuple-element.62), channel_id=1, source_target_pairs={{0,8},{4,12},{8,0},{12,4},{1,9},{5,13},{9,1},{13,5},{2,10},{6,14},... | collective-permute-start | bytes 442376 | tf_op jit(solution)/shard_map/ppermute | solution.py:356
  13.3 5.3 %collective-permute-done.2 = bf16[96,768]{1,0:T(8,128)(2,1)S(1)} collective-permute-done((bf16[96,768]{1,0:T(8,128)(2,1)S(1)}, bf16[96,768]{1,0:T(8,128)(2,1)S(1)}, u32[]{:S(2)}, u32[]{:S(2)}) %collective-permute-start.2) | collective-permute-done | bytes 147488 | tf_op jit(solution)/shard_map/ppermute | solution.py:356
  18.6 0.7 collective-permute-start.5
  20.5 2.8 %collective-permute-start.6 = (bf16[96,768]{1,0:T(8,128)(2,1)S(1)}, bf16[96,768]{1,0:T(8,128)(2,1)S(1)}, u32[]{:S(2)}, u32[]{:S(2)}) collective-permute-start(bf16[96,768]{1,0:T(8,128)(2,1)S(1)} %get-tuple-element.70), channel_id=1, source_target_pairs={{0,8},{4,12},{8,0},{12,4},{1,9},{5,13},{9,1},{13,5},{2,10},{6,14},... | collective-permute-start | bytes 442376 | tf_op jit(solution)/shard_map/ppermute | solution.py:356
  23.3 1.6 %collective-permute-start.10 = (bf16[1536,128]{1,0:T(8,128)(2,1)S(1)}, bf16[1536,128]{1,0:T(8,128)(2,1)S(1)}, u32[]{:S(2)}, u32[]{:S(2)}) collective-permute-start(bf16[1536,128]{1,0:T(8,128)(2,1)S(1)} %pad_maximum_fusion.refs_0_), channel_id=1, source_target_pairs={{0,16},{16,0},{1,17},{17,1},{2,18},{18,2},{3,19},{19,3},{4,20},{20... | collective-permute-start | bytes 1179656 | tf_op jit(solution)/shard_map/ppermute | solution.py:350
  24.9 4.8 %collective-permute-done.5 = bf16[192,768]{1,0:T(8,128)(2,1)S(1)} collective-permute-done((bf16[192,768]{1,0:T(8,128)(2,1)S(1)}, bf16[192,768]{1,0:T(8,128)(2,1)S(1)}, u32[]{:S(2)}, u32[]{:S(2)}) %collective-permute-start.5) | collective-permute-done | bytes 294944 | tf_op jit(solution)/shard_map/ppermute | solution.py:356
  30.7 1.3 %collective-permute-start.4 = (bf16[256,768]{1,0:T(8,128)(2,1)S(1)}, bf16[256,768]{1,0:T(8,128)(2,1)S(1)}, u32[]{:S(2)}, u32[]{:S(2)}) collective-permute-start(bf16[256,768]{1,0:T(8,128)(2,1)S(1)} %get-tuple-element.68.refs_3_.own_keys), channel_id=1, source_target_pairs={{0,1},{1,2},{2,3},{4,5},{5,6},{6,7},{8,9},{9,10},{10,11},{12,13},{... | collective-permute-start | bytes 1179656 | tf_op jit(solution)/shard_map/ppermute | solution.py:426
  32.0 0.8 collective-permute-start.7
  33.2 3.4 %collective-permute-done.11 = bf16[192,768]{1,0:T(8,128)(2,1)S(1)} collective-permute-done((bf16[192,768]{1,0:T(8,128)(2,1)S(1)}, bf16[192,768]{1,0:T(8,128)(2,1)S(1)}, u32[]{:S(2)}, u32[]{:S(2)}) %collective-permute-start.11) | collective-permute-done | bytes 294944 | tf_op jit(solution)/shard_map/ppermute | solution.py:353
  36.6 4.1 %collective-permute-done.7 = bf16[192,768]{1,0:T(8,128)(2,1)S(1)} collective-permute-done((bf16[192,768]{1,0:T(8,128)(2,1)S(1)}, bf16[192,768]{1,0:T(8,128)(2,1)S(1)}, u32[]{:S(2)}, u32[]{:S(2)}) %collective-permute-start.7) | collective-permute-done | bytes 294944 | tf_op jit(solution)/shard_map/ppermute | solution.py:356
  40.8 1.1 %collective-permute-start.12 = (bf16[768,768]{1,0:T(8,128)(2,1)S(1)}, bf16[768,768]{1,0:T(8,128)(2,1)S(1)}, u32[]{:S(2)}, u32[]{:S(2)}) collective-permute-start(bf16[768,768]{1,0:T(8,128)(2,1)S(1)} %constant_dynamic-update-slice_fusion.4.refs_4_), channel_id=1, source_target_pairs={{0,1},{1,0},{2,3},{3,2},{4,5},{5,4},{6,7},{7,6},{8,9},{9,8},{10,11... | collective-permute-start | bytes 3538952 | tf_op jit(solution)/shard_map/ppermute | solution.py:353
  42.6 2.0 %collective-permute-start.16 = (bf16[192,768]{1,0:T(8,128)(2,1)S(1)}, bf16[192,768]{1,0:T(8,128)(2,1)S(1)}, u32[]{:S(2)}, u32[]{:S(2)}) collective-permute-start(bf16[192,768]{1,0:T(8,128)(2,1)S(1)} %get-tuple-element.84), channel_id=1, source_target_pairs={{0,2},{1,3},{2,0},{3,1},{4,6},{5,7},{6,4},{7,5},{8,10},{9,11},{10,... | collective-permute-start | bytes 884744 | tf_op jit(solution)/shard_map/ppermute | solution.py:353
  44.7 1.5 %forward_hi.1 = (bf16[128,768]{1,0:T(8,128)(2,1)S(1)}, f32[768,256]{1,0:T(8,128)S(1)}, bf16[1536,768]{1,0:T(8,128)(2,1)S(1)}) custom-call(s32[1,1]{1,0:T(1,128)S(6)} %copy.18.refs_0_, bf16[128,1536]{1,0:T(8,128)(2,1)S(1)} %get-tuple-element.67.refs_1_, bf16[256,768]{1,0:T(8,128)(2,1)S(1)} %collective-permute-done.4.refs_2_.left_keys, ...), custom_call_target="tpu_custom_call" | custom-call | flops 352321536 | bytes 6881280 | tf_op jit(solution)/shard_map/forward_hi/pallas_call | solution.py:31
  46.2 2.9 %upper.1 = (bf16[128,768]{1,0:T(8,128)(2,1)S(1)}, f32[128,768]{1,0:T(8,128)S(1)}, bf16[128,896]{1,0:T(8,128)(2,1)S(1)}, bf16[128,768]{1,0:T(8,128)(2,1)S(1)}, f32[128,128]{1,0:T(8,128)S(1)}) custom-call(s32[1,2]{1,0:T(1,128)S(1)} %copy-done.5, bf16[128,768]{1,0:T(8,128)(2,1)S(1)} %get-tuple-element.64.dy, bf16[128,1536]{1,0:T(8,128)(2,1)S(1)} %get-tuple-element.65.acts, ...), custom_call_target="tpu_custom_call" | custom-call | flops 503316480 | bytes 5849088 | tf_op jit(solution)/shard_map/upper/pallas_call | solution.py:31
  49.1 1.6 %collective-permute-start.13 = (bf16[128,896]{1,0:T(8,128)(2,1)S(1)}, bf16[128,896]{1,0:T(8,128)(2,1)S(1)}, u32[]{:S(2)}, u32[]{:S(2)}) collective-permute-start(bf16[128,896]{1,0:T(8,128)(2,1)S(1)} %get-tuple-element.80.msg), channel_id=1, source_target_pairs={{0,16},{16,0},{1,17},{17,1},{2,18},{18,2},{3,19},{19,3},{4,20},{20... | collective-permute-start | bytes 688136 | tf_op jit(solution)/shard_map/ppermute | solution.py:350
  50.6 1.3 %collective-permute-start.14 = (bf16[128,768]{1,0:T(8,128)(2,1)S(1)}, bf16[128,768]{1,0:T(8,128)(2,1)S(1)}, u32[]{:S(2)}, u32[]{:S(2)}) collective-permute-start(bf16[128,768]{1,0:T(8,128)(2,1)S(1)} %get-tuple-element.81), channel_id=1, source_target_pairs={{1,0},{2,1},{3,2},{5,4},{6,5},{7,6},{9,8},{10,9},{11,10},{13,12},{... | collective-permute-start | bytes 589832 | tf_op jit(solution)/shard_map/ppermute | solution.py:487
  51.9 1.3 %collective-permute-start.15 = (f32[128,128]{1,0:T(8,128)S(1)}, f32[128,128]{1,0:T(8,128)S(1)}, u32[]{:S(2)}, u32[]{:S(2)}) collective-permute-start(f32[128,128]{1,0:T(8,128)S(1)} %get-tuple-element.82), channel_id=1, source_target_pairs={{1,16},{2,17},{3,18},{17,0},{18,1},{19,2},{5,20},{6,21},{7,22},{21... | collective-permute-start | bytes 196616 | tf_op jit(solution)/shard_map/ppermute | solution.py:488
  53.3 1.8 %collective-permute-start.18 = (bf16[384,768]{1,0:T(8,128)(2,1)S(1)}, bf16[384,768]{1,0:T(8,128)(2,1)S(1)}, u32[]{:S(2)}, u32[]{:S(2)}) collective-permute-start(bf16[384,768]{1,0:T(8,128)(2,1)S(1)} %constant_dynamic-update-slice_fusion.9.refs_4_), channel_id=1, source_target_pairs={{0,1},{1,0},{2,3},{3,2},{4,5},{5,4},{6,7},{7,6},{8,9},{9,8},{10,11... | collective-permute-start | bytes 1769480 | tf_op jit(solution)/shard_map/ppermute | solution.py:353
  55.1 2.4 %collective-permute-done.15.sum_other = f32[128,128]{1,0:T(8,128)S(1)} collective-permute-done((f32[128,128]{1,0:T(8,128)S(1)}, f32[128,128]{1,0:T(8,128)S(1)}, u32[]{:S(2)}, u32[]{:S(2)}) %collective-permute-start.15) | collective-permute-done | bytes 65568 | tf_op jit(solution)/shard_map/ppermute | solution.py:488
  57.9 2.7 %collective-permute-start.19 = (bf16[384,768]{1,0:T(8,128)(2,1)S(1)}, bf16[384,768]{1,0:T(8,128)(2,1)S(1)}, u32[]{:S(2)}, u32[]{:S(2)}) collective-permute-start(bf16[384,768]{1,0:T(8,128)(2,1)S(1)} %constant_dynamic-update-slice_fusion.12.refs_5_), channel_id=1, source_target_pairs={{0,1},{1,0},{2,3},{3,2},{4,5},{5,4},{6,7},{7,6},{8,9},{9,8},{10,11... | collective-permute-start | bytes 1769480 | tf_op jit(solution)/shard_map/ppermute | solution.py:353
  60.6 1.6 %collective-permute-done.19.refs_7_ = bf16[384,768]{1,0:T(8,128)(2,1)S(1)} collective-permute-done((bf16[384,768]{1,0:T(8,128)(2,1)S(1)}, bf16[384,768]{1,0:T(8,128)(2,1)S(1)}, u32[]{:S(2)}, u32[]{:S(2)}) %collective-permute-start.19) | collective-permute-done | bytes 589856 | tf_op jit(solution)/shard_map/ppermute | solution.py:353
  62.3 1.5 %forward_lo.1 = (bf16[128,768]{1,0:T(8,128)(2,1)S(1)}, f32[768,256]{1,0:T(8,128)S(1)}, bf16[1536,768]{1,0:T(8,128)(2,1)S(1)}) custom-call(s32[1,1]{1,0:T(1,128)S(6)} %copy.18.refs_0_, bf16[128,1536]{1,0:T(8,128)(2,1)S(1)} %get-tuple-element.83.refs_1_, bf16[256,768]{1,0:T(8,128)(2,1)S(1)} %collective-permute-done.4.refs_2_.left_keys, ...), custom_call_target="tpu_custom_call" | custom-call | flops 352321536 | bytes 6881280 | tf_op jit(solution)/shard_map/forward_lo/pallas_call | solution.py:31
  63.8 2.4 %lower.1 = (bf16[128,768]{1,0:T(8,128)(2,1)S(1)}, bf16[128,768]{1,0:T(8,128)(2,1)S(1)}, f32[128,768]{1,0:T(8,128)S(1)}, bf16[128,768]{1,0:T(8,128)(2,1)S(1)}) custom-call(s32[1,2]{1,0:T(1,128)S(1)} %copy-done.5, f32[128,768]{1,0:T(8,128)S(1)} %get-tuple-element.79.own, bf16[128,896]{1,0:T(8,128)(2,1)S(1)} %get-tuple-element.80.msg, ...), custom_call_target="tpu_custom_call" | custom-call | flops 201326592 | bytes 4505600 | tf_op jit(solution)/shard_map/lower/pallas_call | solution.py:31
  66.1 1.4 %collective-permute-done.21.refs_3_ = bf16[128,768]{1,0:T(8,128)(2,1)S(1)} collective-permute-done((bf16[128,768]{1,0:T(8,128)(2,1)S(1)}, bf16[128,768]{1,0:T(8,128)(2,1)S(1)}, u32[]{:S(2)}, u32[]{:S(2)}) %collective-permute-start.21) | collective-permute-done | bytes 196640 | tf_op jit(solution)/shard_map/ppermute | solution.py:353
  67.6 1.7 %collective-permute-done.22.refs_4_ = bf16[256,768]{1,0:T(8,128)(2,1)S(1)} collective-permute-done((bf16[256,768]{1,0:T(8,128)(2,1)S(1)}, bf16[256,768]{1,0:T(8,128)(2,1)S(1)}, u32[]{:S(2)}, u32[]{:S(2)}) %collective-permute-start.22) | collective-permute-done | bytes 393248 | tf_op jit(solution)/shard_map/ppermute | solution.py:353
  69.9 0.8 collective-permute-start.25
  70.7 1.3 %collective-permute-start.20 = (bf16[128,768]{1,0:T(8,128)(2,1)S(1)}, bf16[128,768]{1,0:T(8,128)(2,1)S(1)}, u32[]{:S(2)}, u32[]{:S(2)}) collective-permute-start(bf16[128,768]{1,0:T(8,128)(2,1)S(1)} %get-tuple-element.93), channel_id=1, source_target_pairs={{1,0},{2,1},{3,2},{5,4},{6,5},{7,6},{9,8},{10,9},{11,10},{13,12},{... | collective-permute-start | bytes 589832 | tf_op jit(solution)/shard_map/ppermute | solution.py:500
  72.0 1.6 %collective-permute-start.24 = (bf16[128,768]{1,0:T(8,128)(2,1)S(1)}, bf16[128,768]{1,0:T(8,128)(2,1)S(1)}, u32[]{:S(2)}, u32[]{:S(2)}) collective-permute-start(bf16[128,768]{1,0:T(8,128)(2,1)S(1)} %get-tuple-element.102.dy_mine), channel_id=1, source_target_pairs={{0,16},{16,0},{1,17},{17,1},{2,18},{18,2},{3,19},{19,3},{4,20},{20... | collective-permute-start | bytes 589832 | tf_op jit(solution)/shard_map/ppermute | solution.py:350
  73.5 2.1 %collective-permute-start.27 = (bf16[128,768]{1,0:T(8,128)(2,1)S(1)}, bf16[128,768]{1,0:T(8,128)(2,1)S(1)}, u32[]{:S(2)}, u32[]{:S(2)}) collective-permute-start(bf16[128,768]{1,0:T(8,128)(2,1)S(1)} %get-tuple-element.90.qg.refs_2_), channel_id=1, source_target_pairs={{0,2},{1,3},{2,0},{3,1},{4,6},{5,7},{6,4},{7,5},{8,10},{9,11},{10,... | collective-permute-start | bytes 589832 | tf_op jit(solution)/shard_map/ppermute | solution.py:353
  75.6 0.9 project_lo.1
  76.5 3.1 %collective-permute-done.24.dy_in = bf16[128,768]{1,0:T(8,128)(2,1)S(1)} collective-permute-done((bf16[128,768]{1,0:T(8,128)(2,1)S(1)}, bf16[128,768]{1,0:T(8,128)(2,1)S(1)}, u32[]{:S(2)}, u32[]{:S(2)}) %collective-permute-start.24) | collective-permute-done | bytes 196640 | tf_op jit(solution)/shard_map/ppermute | solution.py:350
  79.6 2.3 %collective-permute-done.27.refs_3_ = bf16[128,768]{1,0:T(8,128)(2,1)S(1)} collective-permute-done((bf16[128,768]{1,0:T(8,128)(2,1)S(1)}, bf16[128,768]{1,0:T(8,128)(2,1)S(1)}, u32[]{:S(2)}, u32[]{:S(2)}) %collective-permute-start.27) | collective-permute-done | bytes 196640 | tf_op jit(solution)/shard_map/ppermute | solution.py:353
  82.1 1.6 %collective-permute-done.28.refs_4_ = bf16[256,768]{1,0:T(8,128)(2,1)S(1)} collective-permute-done((bf16[256,768]{1,0:T(8,128)(2,1)S(1)}, bf16[256,768]{1,0:T(8,128)(2,1)S(1)}, u32[]{:S(2)}, u32[]{:S(2)}) %collective-permute-start.28) | collective-permute-done | bytes 393248 | tf_op jit(solution)/shard_map/ppermute | solution.py:353
  84.2 1.3 %collective-permute-start.29 = (bf16[192,768]{1,0:T(8,128)(2,1)S(1)}, bf16[192,768]{1,0:T(8,128)(2,1)S(1)}, u32[]{:S(2)}, u32[]{:S(2)}) collective-permute-start(bf16[192,768]{1,0:T(8,128)(2,1)S(1)} %get-tuple-element.109), channel_id=1, source_target_pairs={{0,4},{4,0},{8,12},{12,8},{1,5},{5,1},{9,13},{13,9},{2,6},{6,2},{1... | collective-permute-start | bytes 884744 | tf_op jit(solution)/shard_map/ppermute | solution.py:356
  85.6 1.3 %collective-permute-start.23 = (bf16[128,1536]{1,0:T(8,128)(2,1)S(1)}, bf16[128,1536]{1,0:T(8,128)(2,1)S(1)}, u32[]{:S(2)}, u32[]{:S(2)}) collective-permute-start(bf16[128,1536]{1,0:T(8,128)(2,1)S(1)} %get-tuple-element.100), channel_id=1, source_target_pairs={{16,0},{17,1},{18,2},{19,3},{20,4},{21,5},{22,6},{23,7},{24,8},{25... | collective-permute-start | bytes 1179656 | tf_op jit(solution)/shard_map/ppermute | solution.py:518
  86.9 3.1 %collective-permute-start.26 = (bf16[96,768]{1,0:T(8,128)(2,1)S(1)}, bf16[96,768]{1,0:T(8,128)(2,1)S(1)}, u32[]{:S(2)}, u32[]{:S(2)}) collective-permute-start(bf16[96,768]{1,0:T(8,128)(2,1)S(1)} %get-tuple-element.105), channel_id=1, source_target_pairs={{0,8},{4,12},{8,0},{12,4},{1,9},{5,13},{9,1},{13,5},{2,10},{6,14},... | collective-permute-start | bytes 442376 | tf_op jit(solution)/shard_map/ppermute | solution.py:356
  90.0 5.4 %collective-permute-done.26.hi_arrived = bf16[96,768]{1,0:T(8,128)(2,1)S(1)} collective-permute-done((bf16[96,768]{1,0:T(8,128)(2,1)S(1)}, bf16[96,768]{1,0:T(8,128)(2,1)S(1)}, u32[]{:S(2)}, u32[]{:S(2)}) %collective-permute-start.26) | collective-permute-done | bytes 147488 | tf_op jit(solution)/shard_map/ppermute | solution.py:356
  95.4 1.2 %collective-permute-done.29.arrived = bf16[192,768]{1,0:T(8,128)(2,1)S(1)} collective-permute-done((bf16[192,768]{1,0:T(8,128)(2,1)S(1)}, bf16[192,768]{1,0:T(8,128)(2,1)S(1)}, u32[]{:S(2)}, u32[]{:S(2)}) %collective-permute-start.29) | collective-permute-done | bytes 294944 | tf_op jit(solution)/shard_map/ppermute | solution.py:356
  96.6 2.3 %collective-permute-start.30 = (bf16[96,768]{1,0:T(8,128)(2,1)S(1)}, bf16[96,768]{1,0:T(8,128)(2,1)S(1)}, u32[]{:S(2)}, u32[]{:S(2)}) collective-permute-start(bf16[96,768]{1,0:T(8,128)(2,1)S(1)} %get-tuple-element.112), channel_id=1, source_target_pairs={{0,8},{4,12},{8,0},{12,4},{1,9},{5,13},{9,1},{13,5},{2,10},{6,14},... | collective-permute-start | bytes 442376 | tf_op jit(solution)/shard_map/ppermute | solution.py:356
  98.9 2.0 %finish.1 = bf16[128,1536]{1,0:T(8,128)(2,1)} custom-call(s32[1,2]{1,0:T(1,128)S(1)} %copy-done.5, f32[128,1536]{1,0:T(8,128)S(1)} %get-tuple-element.99.part, bf16[128,1536]{1,0:T(8,128)(2,1)S(1)} %collective-permute-done.23.msg_in, bf16[128,1536]{1,0:T(8,128)(2,1)S(1)} %get-tuple-element.101.acts, f32[8,1536]{1,0:T(8,128)S(1)} %get-tuple-element.66.vecs, ...), custom_call_target="tpu_custom_call" | custom-call | flops 3932160 | bytes 2408448 | tf_op jit(solution)/shard_map/finish/pallas_call | solution.py:31
  100.9 5.3 %collective-permute-done.30.lo_arrived = bf16[96,768]{1,0:T(8,128)(2,1)S(1)} collective-permute-done((bf16[96,768]{1,0:T(8,128)(2,1)S(1)}, bf16[96,768]{1,0:T(8,128)(2,1)S(1)}, u32[]{:S(2)}, u32[]{:S(2)}) %collective-permute-start.30) | collective-permute-done | bytes 147488 | tf_op jit(solution)/shard_map/ppermute | solution.py:356
  106.4 1.5 %collective-permute-start.31 = (bf16[96,768]{1,0:T(8,128)(2,1)S(1)}, bf16[96,768]{1,0:T(8,128)(2,1)S(1)}, u32[]{:S(2)}, u32[]{:S(2)}) collective-permute-start(bf16[96,768]{1,0:T(8,128)(2,1)S(1)} %get-tuple-element.115), channel_id=1, source_target_pairs={{0,16},{16,0},{1,17},{17,1},{2,18},{18,2},{3,19},{19,3},{4,20},{20... | collective-permute-start | bytes 442376 | tf_op jit(solution)/shard_map/ppermute | solution.py:350
  107.9 3.7 %collective-permute-done.31 = bf16[96,768]{1,0:T(8,128)(2,1)S(1)} collective-permute-done((bf16[96,768]{1,0:T(8,128)(2,1)S(1)}, bf16[96,768]{1,0:T(8,128)(2,1)S(1)}, u32[]{:S(2)}, u32[]{:S(2)}) %collective-permute-start.31) | collective-permute-done | bytes 147488 | tf_op jit(solution)/shard_map/ppermute | solution.py:350
  111.6 0.7 maximum_bitcast_fusion
  (62 shorter events, 7.9 us)
Async XLA Ops:
  1.7 8.0 %collective-permute-start.1 = (bf16[96,768]{1,0:T(8,128)(2,1)S(1)}, bf16[96,768]{1,0:T(8,128)(2,1)S(1)}, u32[]{:S(2)}, u32[]{:S(2)}) collective-permute-start(bf16[96,768]{1,0:T(8,128)(2,1)S(1)} %get-tuple-element.118), channel_id=1, source_target_pairs={{0,16},{16,0},{1,17},{17,1},{2,18},{18,2},{3,19},{19,3},{4,20},{20... | collective-permute-start | bytes 442376 | tf_op jit(solution)/shard_map/ppermute | solution.py:350
  4.7 1.0 copy-start
  5.7 0.7 copy-start.3
  6.7 6.4 %collective-permute-start.8 = (bf16[768,128]{1,0:T(8,128)(2,1)S(1)}, bf16[768,128]{1,0:T(8,128)(2,1)S(1)}, u32[]{:S(2)}, u32[]{:S(2)}) collective-permute-start(bf16[768,128]{1,0:T(8,128)(2,1)S(1)} %get-tuple-element.60), channel_id=1, source_target_pairs={{0,2},{1,3},{2,0},{3,1},{4,6},{5,7},{6,4},{7,5},{8,10},{9,11},{10,... | collective-permute-start | bytes 589832 | tf_op jit(solution)/shard_map/ppermute | solution.py:353
  8.3 0.7 copy-start.4
  9.1 11.4 %collective-permute-start = (bf16[144,1536]{1,0:T(8,128)(2,1)S(1)}, bf16[144,1536]{1,0:T(8,128)(2,1)S(1)}, u32[]{:S(2)}, u32[]{:S(2)}) collective-permute-start(bf16[144,1536]{1,0:T(8,128)(2,1)S(1)} %pack.1), channel_id=1, source_target_pairs={{0,16},{16,0},{1,17},{17,1},{2,18},{18,2},{3,19},{19,3},{4,20},{20... | collective-permute-start | bytes 1327112 | tf_op jit(solution)/shard_map/ppermute | solution.py:350
  9.7 8.9 %collective-permute-start.2 = (bf16[96,768]{1,0:T(8,128)(2,1)S(1)}, bf16[96,768]{1,0:T(8,128)(2,1)S(1)}, u32[]{:S(2)}, u32[]{:S(2)}) collective-permute-start(bf16[96,768]{1,0:T(8,128)(2,1)S(1)} %get-tuple-element.62), channel_id=1, source_target_pairs={{0,8},{4,12},{8,0},{12,4},{1,9},{5,13},{9,1},{13,5},{2,10},{6,14},... | collective-permute-start | bytes 442376 | tf_op jit(solution)/shard_map/ppermute | solution.py:356
  13.1 17.1 %copy-start.1 = (bf16[1,1,128,1536]{3,2,1,0:T(8,128)(2,1)S(1)}, bf16[1,1,128,1536]{3,2,1,0:T(8,128)(2,1)}, u32[]{:S(2)}) copy-start(bf16[1,1,128,1536]{3,2,1,0:T(8,128)(2,1)} %param.7) | copy-start | bytes 1179652
  13.1 17.1 %copy-start.2 = (bf16[1,128,1536]{2,1,0:T(8,128)(2,1)S(1)}, bf16[1,128,1536]{2,1,0:T(8,128)(2,1)}, u32[]{:S(2)}) copy-start(bf16[1,128,1536]{2,1,0:T(8,128)(2,1)} %param.8) | copy-start | bytes 1179652
  13.2 10.1 %collective-permute-start.9 = (bf16[768,128]{1,0:T(8,128)(2,1)S(1)}, bf16[768,128]{1,0:T(8,128)(2,1)S(1)}, u32[]{:S(2)}, u32[]{:S(2)}) collective-permute-start(bf16[768,128]{1,0:T(8,128)(2,1)S(1)} %pad_maximum_fusion.3), channel_id=1, source_target_pairs={{0,1},{1,0},{2,3},{3,2},{4,5},{5,4},{6,7},{7,6},{8,9},{9,8},{10,11... | collective-permute-start | bytes 589832 | tf_op jit(solution)/shard_map/ppermute | solution.py:353
  18.6 11.1 %collective-permute-start.5 = (bf16[192,768]{1,0:T(8,128)(2,1)S(1)}, bf16[192,768]{1,0:T(8,128)(2,1)S(1)}, u32[]{:S(2)}, u32[]{:S(2)}) collective-permute-start(bf16[192,768]{1,0:T(8,128)(2,1)S(1)} %get-tuple-element.129), channel_id=1, source_target_pairs={{0,4},{4,0},{8,12},{12,8},{1,5},{5,1},{9,13},{13,9},{2,6},{6,2},{1... | collective-permute-start | bytes 884744 | tf_op jit(solution)/shard_map/ppermute | solution.py:356
  19.4 10.9 %collective-permute-start.3 = (bf16[192,768]{1,0:T(8,128)(2,1)S(1)}, bf16[192,768]{1,0:T(8,128)(2,1)S(1)}, u32[]{:S(2)}, u32[]{:S(2)}) collective-permute-start(bf16[192,768]{1,0:T(8,128)(2,1)S(1)} %get-tuple-element.129), channel_id=1, source_target_pairs={{0,2},{1,3},{2,0},{3,1},{4,6},{5,7},{6,4},{7,5},{8,10},{9,11},{10,... | collective-permute-start | bytes 884744 | tf_op jit(solution)/shard_map/ppermute | solution.py:353
  20.5 11.5 %collective-permute-start.6 = (bf16[96,768]{1,0:T(8,128)(2,1)S(1)}, bf16[96,768]{1,0:T(8,128)(2,1)S(1)}, u32[]{:S(2)}, u32[]{:S(2)}) collective-permute-start(bf16[96,768]{1,0:T(8,128)(2,1)S(1)} %get-tuple-element.70), channel_id=1, source_target_pairs={{0,8},{4,12},{8,0},{12,4},{1,9},{5,13},{9,1},{13,5},{2,10},{6,14},... | collective-permute-start | bytes 442376 | tf_op jit(solution)/shard_map/ppermute | solution.py:356
  23.3 9.9 %collective-permute-start.10 = (bf16[1536,128]{1,0:T(8,128)(2,1)S(1)}, bf16[1536,128]{1,0:T(8,128)(2,1)S(1)}, u32[]{:S(2)}, u32[]{:S(2)}) collective-permute-start(bf16[1536,128]{1,0:T(8,128)(2,1)S(1)} %pad_maximum_fusion.refs_0_), channel_id=1, source_target_pairs={{0,16},{16,0},{1,17},{17,1},{2,18},{18,2},{3,19},{19,3},{4,20},{20... | collective-permute-start | bytes 1179656 | tf_op jit(solution)/shard_map/ppermute | solution.py:350
  29.7 6.9 %collective-permute-start.11 = (bf16[192,768]{1,0:T(8,128)(2,1)S(1)}, bf16[192,768]{1,0:T(8,128)(2,1)S(1)}, u32[]{:S(2)}, u32[]{:S(2)}) collective-permute-start(bf16[192,768]{1,0:T(8,128)(2,1)S(1)} %collective-permute-done.5), channel_id=1, source_target_pairs={{0,2},{1,3},{2,0},{3,1},{4,6},{5,7},{6,4},{7,5},{8,10},{9,11},{10,... | collective-permute-start | bytes 884744 | tf_op jit(solution)/shard_map/ppermute | solution.py:353
  30.7 10.1 %collective-permute-start.4 = (bf16[256,768]{1,0:T(8,128)(2,1)S(1)}, bf16[256,768]{1,0:T(8,128)(2,1)S(1)}, u32[]{:S(2)}, u32[]{:S(2)}) collective-permute-start(bf16[256,768]{1,0:T(8,128)(2,1)S(1)} %get-tuple-element.68.refs_3_.own_keys), channel_id=1, source_target_pairs={{0,1},{1,2},{2,3},{4,5},{5,6},{6,7},{8,9},{9,10},{10,11},{12,13},{... | collective-permute-start | bytes 1179656 | tf_op jit(solution)/shard_map/ppermute | solution.py:426
  32.0 8.7 %collective-permute-start.7 = (bf16[192,768]{1,0:T(8,128)(2,1)S(1)}, bf16[192,768]{1,0:T(8,128)(2,1)S(1)}, u32[]{:S(2)}, u32[]{:S(2)}) collective-permute-start(bf16[192,768]{1,0:T(8,128)(2,1)S(1)} %get-tuple-element.84), channel_id=1, source_target_pairs={{0,4},{4,0},{8,12},{12,8},{1,5},{5,1},{9,13},{13,9},{2,6},{6,2},{1... | collective-permute-start | bytes 884744 | tf_op jit(solution)/shard_map/ppermute | solution.py:356
  40.8 3.9 %collective-permute-start.12 = (bf16[768,768]{1,0:T(8,128)(2,1)S(1)}, bf16[768,768]{1,0:T(8,128)(2,1)S(1)}, u32[]{:S(2)}, u32[]{:S(2)}) collective-permute-start(bf16[768,768]{1,0:T(8,128)(2,1)S(1)} %constant_dynamic-update-slice_fusion.4.refs_4_), channel_id=1, source_target_pairs={{0,1},{1,0},{2,3},{3,2},{4,5},{5,4},{6,7},{7,6},{8,9},{9,8},{10,11... | collective-permute-start | bytes 3538952 | tf_op jit(solution)/shard_map/ppermute | solution.py:353
  42.6 10.7 %collective-permute-start.17 = (bf16[192,768]{1,0:T(8,128)(2,1)S(1)}, bf16[192,768]{1,0:T(8,128)(2,1)S(1)}, u32[]{:S(2)}, u32[]{:S(2)}) collective-permute-start(bf16[192,768]{1,0:T(8,128)(2,1)S(1)} %collective-permute-done.7), channel_id=1, source_target_pairs={{0,2},{1,3},{2,0},{3,1},{4,6},{5,7},{6,4},{7,5},{8,10},{9,11},{10,... | collective-permute-start | bytes 884744 | tf_op jit(solution)/shard_map/ppermute | solution.py:353
  42.6 15.2 %collective-permute-start.16 = (bf16[192,768]{1,0:T(8,128)(2,1)S(1)}, bf16[192,768]{1,0:T(8,128)(2,1)S(1)}, u32[]{:S(2)}, u32[]{:S(2)}) collective-permute-start(bf16[192,768]{1,0:T(8,128)(2,1)S(1)} %get-tuple-element.84), channel_id=1, source_target_pairs={{0,2},{1,3},{2,0},{3,1},{4,6},{5,7},{6,4},{7,5},{8,10},{9,11},{10,... | collective-permute-start | bytes 884744 | tf_op jit(solution)/shard_map/ppermute | solution.py:353
  44.7 1.5 %copy-start.5 = (s32[1,2]{1,0:T(1,128)S(1)}, s32[1,2]{1,0:T(1,128)}, u32[]{:S(2)}) copy-start(s32[1,2]{1,0:T(1,128)} %kept.5) | copy-start | bytes 28
  49.1 8.4 %collective-permute-start.13 = (bf16[128,896]{1,0:T(8,128)(2,1)S(1)}, bf16[128,896]{1,0:T(8,128)(2,1)S(1)}, u32[]{:S(2)}, u32[]{:S(2)}) collective-permute-start(bf16[128,896]{1,0:T(8,128)(2,1)S(1)} %get-tuple-element.80.msg), channel_id=1, source_target_pairs={{0,16},{16,0},{1,17},{17,1},{2,18},{18,2},{3,19},{19,3},{4,20},{20... | collective-permute-start | bytes 688136 | tf_op jit(solution)/shard_map/ppermute | solution.py:350
  50.6 6.9 %collective-permute-start.14 = (bf16[128,768]{1,0:T(8,128)(2,1)S(1)}, bf16[128,768]{1,0:T(8,128)(2,1)S(1)}, u32[]{:S(2)}, u32[]{:S(2)}) collective-permute-start(bf16[128,768]{1,0:T(8,128)(2,1)S(1)} %get-tuple-element.81), channel_id=1, source_target_pairs={{1,0},{2,1},{3,2},{5,4},{6,5},{7,6},{9,8},{10,9},{11,10},{13,12},{... | collective-permute-start | bytes 589832 | tf_op jit(solution)/shard_map/ppermute | solution.py:487
  51.9 5.6 %collective-permute-start.15 = (f32[128,128]{1,0:T(8,128)S(1)}, f32[128,128]{1,0:T(8,128)S(1)}, u32[]{:S(2)}, u32[]{:S(2)}) collective-permute-start(f32[128,128]{1,0:T(8,128)S(1)} %get-tuple-element.82), channel_id=1, source_target_pairs={{1,16},{2,17},{3,18},{17,0},{18,1},{19,2},{5,20},{6,21},{7,22},{21... | collective-permute-start | bytes 196616 | tf_op jit(solution)/shard_map/ppermute | solution.py:488
  53.3 7.4 %collective-permute-start.18 = (bf16[384,768]{1,0:T(8,128)(2,1)S(1)}, bf16[384,768]{1,0:T(8,128)(2,1)S(1)}, u32[]{:S(2)}, u32[]{:S(2)}) collective-permute-start(bf16[384,768]{1,0:T(8,128)(2,1)S(1)} %constant_dynamic-update-slice_fusion.9.refs_4_), channel_id=1, source_target_pairs={{0,1},{1,0},{2,3},{3,2},{4,5},{5,4},{6,7},{7,6},{8,9},{9,8},{10,11... | collective-permute-start | bytes 1769480 | tf_op jit(solution)/shard_map/ppermute | solution.py:353
  57.9 4.3 %collective-permute-start.19 = (bf16[384,768]{1,0:T(8,128)(2,1)S(1)}, bf16[384,768]{1,0:T(8,128)(2,1)S(1)}, u32[]{:S(2)}, u32[]{:S(2)}) collective-permute-start(bf16[384,768]{1,0:T(8,128)(2,1)S(1)} %constant_dynamic-update-slice_fusion.12.refs_5_), channel_id=1, source_target_pairs={{0,1},{1,0},{2,3},{3,2},{4,5},{5,4},{6,7},{7,6},{8,9},{9,8},{10,11... | collective-permute-start | bytes 1769480 | tf_op jit(solution)/shard_map/ppermute | solution.py:353
  60.6 6.9 %collective-permute-start.21 = (bf16[128,768]{1,0:T(8,128)(2,1)S(1)}, bf16[128,768]{1,0:T(8,128)(2,1)S(1)}, u32[]{:S(2)}, u32[]{:S(2)}) collective-permute-start(bf16[128,768]{1,0:T(8,128)(2,1)S(1)} %get-tuple-element.95.refs_2_), channel_id=1, source_target_pairs={{0,2},{1,3},{2,0},{3,1},{4,6},{5,7},{6,4},{7,5},{8,10},{9,11},{10,... | collective-permute-start | bytes 589832 | tf_op jit(solution)/shard_map/ppermute | solution.py:353
  67.5 1.8 %collective-permute-start.22 = (bf16[256,768]{1,0:T(8,128)(2,1)S(1)}, bf16[256,768]{1,0:T(8,128)(2,1)S(1)}, u32[]{:S(2)}, u32[]{:S(2)}) collective-permute-start(bf16[256,768]{1,0:T(8,128)(2,1)S(1)} %pad_maximum_fusion.1), channel_id=1, source_target_pairs={{0,1},{1,0},{2,3},{3,2},{4,5},{5,4},{6,7},{7,6},{8,9},{9,8},{10,11... | collective-permute-start | bytes 1179656 | tf_op jit(solution)/shard_map/ppermute | solution.py:353
  69.9 12.0 %collective-permute-start.25 = (bf16[192,768]{1,0:T(8,128)(2,1)S(1)}, bf16[192,768]{1,0:T(8,128)(2,1)S(1)}, u32[]{:S(2)}, u32[]{:S(2)}) collective-permute-start(bf16[192,768]{1,0:T(8,128)(2,1)S(1)} %get-tuple-element.103), channel_id=1, source_target_pairs={{0,4},{4,0},{8,12},{12,8},{1,5},{5,1},{9,13},{13,9},{2,6},{6,2},{1... | collective-permute-start | bytes 884744 | tf_op jit(solution)/shard_map/ppermute | solution.py:356
  70.7 5.0 %collective-permute-start.20 = (bf16[128,768]{1,0:T(8,128)(2,1)S(1)}, bf16[128,768]{1,0:T(8,128)(2,1)S(1)}, u32[]{:S(2)}, u32[]{:S(2)}) collective-permute-start(bf16[128,768]{1,0:T(8,128)(2,1)S(1)} %get-tuple-element.93), channel_id=1, source_target_pairs={{1,0},{2,1},{3,2},{5,4},{6,5},{7,6},{9,8},{10,9},{11,10},{13,12},{... | collective-permute-start | bytes 589832 | tf_op jit(solution)/shard_map/ppermute | solution.py:500
  72.0 7.7 %collective-permute-start.24 = (bf16[128,768]{1,0:T(8,128)(2,1)S(1)}, bf16[128,768]{1,0:T(8,128)(2,1)S(1)}, u32[]{:S(2)}, u32[]{:S(2)}) collective-permute-start(bf16[128,768]{1,0:T(8,128)(2,1)S(1)} %get-tuple-element.102.dy_mine), channel_id=1, source_target_pairs={{0,16},{16,0},{1,17},{17,1},{2,18},{18,2},{3,19},{19,3},{4,20},{20... | collective-permute-start | bytes 589832 | tf_op jit(solution)/shard_map/ppermute | solution.py:350
  73.5 8.4 %collective-permute-start.27 = (bf16[128,768]{1,0:T(8,128)(2,1)S(1)}, bf16[128,768]{1,0:T(8,128)(2,1)S(1)}, u32[]{:S(2)}, u32[]{:S(2)}) collective-permute-start(bf16[128,768]{1,0:T(8,128)(2,1)S(1)} %get-tuple-element.90.qg.refs_2_), channel_id=1, source_target_pairs={{0,2},{1,3},{2,0},{3,1},{4,6},{5,7},{6,4},{7,5},{8,10},{9,11},{10,... | collective-permute-start | bytes 589832 | tf_op jit(solution)/shard_map/ppermute | solution.py:353
  81.9 1.8 %collective-permute-start.28 = (bf16[256,768]{1,0:T(8,128)(2,1)S(1)}, bf16[256,768]{1,0:T(8,128)(2,1)S(1)}, u32[]{:S(2)}, u32[]{:S(2)}) collective-permute-start(bf16[256,768]{1,0:T(8,128)(2,1)S(1)} %pad_maximum_fusion.2), channel_id=1, source_target_pairs={{0,1},{1,0},{2,3},{3,2},{4,5},{5,4},{6,7},{7,6},{8,9},{9,8},{10,11... | collective-permute-start | bytes 1179656 | tf_op jit(solution)/shard_map/ppermute | solution.py:353
  84.2 12.3 %collective-permute-start.29 = (bf16[192,768]{1,0:T(8,128)(2,1)S(1)}, bf16[192,768]{1,0:T(8,128)(2,1)S(1)}, u32[]{:S(2)}, u32[]{:S(2)}) collective-permute-start(bf16[192,768]{1,0:T(8,128)(2,1)S(1)} %get-tuple-element.109), channel_id=1, source_target_pairs={{0,4},{4,0},{8,12},{12,8},{1,5},{5,1},{9,13},{13,9},{2,6},{6,2},{1... | collective-permute-start | bytes 884744 | tf_op jit(solution)/shard_map/ppermute | solution.py:356
  85.6 13.4 %collective-permute-start.23 = (bf16[128,1536]{1,0:T(8,128)(2,1)S(1)}, bf16[128,1536]{1,0:T(8,128)(2,1)S(1)}, u32[]{:S(2)}, u32[]{:S(2)}) collective-permute-start(bf16[128,1536]{1,0:T(8,128)(2,1)S(1)} %get-tuple-element.100), channel_id=1, source_target_pairs={{16,0},{17,1},{18,2},{19,3},{20,4},{21,5},{22,6},{23,7},{24,8},{25... | collective-permute-start | bytes 1179656 | tf_op jit(solution)/shard_map/ppermute | solution.py:518
  86.9 8.5 %collective-permute-start.26 = (bf16[96,768]{1,0:T(8,128)(2,1)S(1)}, bf16[96,768]{1,0:T(8,128)(2,1)S(1)}, u32[]{:S(2)}, u32[]{:S(2)}) collective-permute-start(bf16[96,768]{1,0:T(8,128)(2,1)S(1)} %get-tuple-element.105), channel_id=1, source_target_pairs={{0,8},{4,12},{8,0},{12,4},{1,9},{5,13},{9,1},{13,5},{2,10},{6,14},... | collective-permute-start | bytes 442376 | tf_op jit(solution)/shard_map/ppermute | solution.py:356
  96.6 9.7 %collective-permute-start.30 = (bf16[96,768]{1,0:T(8,128)(2,1)S(1)}, bf16[96,768]{1,0:T(8,128)(2,1)S(1)}, u32[]{:S(2)}, u32[]{:S(2)}) collective-permute-start(bf16[96,768]{1,0:T(8,128)(2,1)S(1)} %get-tuple-element.112), channel_id=1, source_target_pairs={{0,8},{4,12},{8,0},{12,4},{1,9},{5,13},{9,1},{13,5},{2,10},{6,14},... | collective-permute-start | bytes 442376 | tf_op jit(solution)/shard_map/ppermute | solution.py:356
  106.4 5.2 %collective-permute-start.31 = (bf16[96,768]{1,0:T(8,128)(2,1)S(1)}, bf16[96,768]{1,0:T(8,128)(2,1)S(1)}, u32[]{:S(2)}, u32[]{:S(2)}) collective-permute-start(bf16[96,768]{1,0:T(8,128)(2,1)S(1)} %get-tuple-element.115), channel_id=1, source_target_pairs={{0,16},{16,0},{1,17},{17,1},{2,18},{18,2},{3,19},{19,3},{4,20},{20... | collective-permute-start | bytes 442376 | tf_op jit(solution)/shard_map/ppermute | solution.py:350

commit v4 on v3

--- a/solution.py
+++ b/solution.py
@@ -503,14 +503,14 @@
             gathered_hi = over_tiles(tied(qg_hi, *exchanged), after=[qg_lo])
             mine_hi, sent_hi = weight_grad("weight_grad_hi", True, gathered_hi)
             first_hi = along(sent_hi, steps[-1])
-            left_in_lo = tied(left_in_lo, mine_hi)
+            clips_hi = over_clips("add_pair_hi", mine_hi, first_hi)
+            left_in_lo = tied(left_in_lo, clips_hi[1], dy_in)
         part_lo, msg_lo = call(
             project_kernel, [sds((tile, dim), F32), sds((tile, dim), BF)], matmul_flops,
             "project_lo", qg_lo, weights_lo, key_own, left_in_lo,
         )
         if single:
-            gathered_lo = over_tiles(qg_lo, after=[first_hi, msg_lo, dy_in])
-            clips_hi = over_clips("add_pair_hi", mine_hi, first_hi)
+            gathered_lo = over_tiles(qg_lo, after=[first_hi])
             gathered_lo[-1] = tied(gathered_lo[-1], clips_hi[0])
             mine_lo, sent_lo = weight_grad("weight_grad_lo", False, gathered_lo)
             first_lo = along(sent_lo, steps[-1])
@@ -540,7 +540,7 @@
 
     mine, theirs = call(
         add_kernel, [sds((rows, half), BF)] * 2, 20 * rows * half,
-        "add_clips", *clips_hi, clips_lo[0], tied(clips_lo[1], result),
+        "add_clips", *clips_hi, *clips_lo,
     )
     other = swap(theirs)
     first = jnp.where(side == 0, mine, other)

time: 113 us -> 114 us (level); the launches traced: 112 us -> 112 us
  waiting for transfers between devices: 49.4 us -> 47.9 us
    ppermute x6, waiting for transfers between devices: 7.71 us -> 1.8 us  [swap(): return lax.ppermute(value, 'section', swap_pairs)]
    ppermute x13, waiting for transfers between devices: 13.1 us -> 15.6 us  [across(): return lax.ppermute(value, 'seq', [(s, s ^ offset) for s in range(seqs)])]
    ppermute x1, waiting for transfers between devices: 0.01 us -> 2.49 us  [per_device(): lax.ppermute(msg_lo, 'section', [(i + 1, i) for i in range(0, sections, 2)])]
    ppermute x13, starting transfers between devices: 12.7 us -> 10.9 us  [across(): return lax.ppermute(value, 'seq', [(s, s ^ offset) for s in range(seqs)])]
    ppermute x8, starting transfers between devices: 14.6 us -> 16.1 us  [along(): return lax.ppermute(value, 'fsdp', [(f, f ^ flip) for f in range(fsdps)])]
where the time goes in v4:
time: 114 us; the launch traced here: 112 us
  waiting for transfers between devices  47.9 us (42%)
  starting transfers between devices  44.2 us (39%)
  Pallas kernels  13.2 us (12%)
  local copies, waits for them, and re-layouts  2.63 us (2%)
  other arithmetic  1.87 us (2%)
  between operations  1.63 us (1%)
    ppermute x8, waiting for transfers between devices, along(): return lax.ppermute(value, 'fsdp', [(f, f ^ flip) for f in range(fsdps)])  25.6 us
    ppermute x8, starting transfers between devices, along(): return lax.ppermute(value, 'fsdp', [(f, f ^ flip) for f in range(fsdps)])  16.1 us
    ppermute x13, waiting for transfers between devices, across(): return lax.ppermute(value, 'seq', [(s, s ^ offset) for s in range(seqs)])  15.6 us
    pallas_call x15, Pallas kernels, call(): pl.pallas_call(kernel, out_shape=outs, in_specs=[pl.BlockSpec(memory_spac...  13.2 us
    ppermute x13, starting transfers between devices, across(): return lax.ppermute(value, 'seq', [(s, s ^ offset) for s in range(seqs)])  10.9 us
    ppermute x6, starting transfers between devices, swap(): return lax.ppermute(value, 'section', swap_pairs)  10.7 us
    unnamed x19, local copies, waits for them, and re-layouts  2.54 us
    ppermute x1, waiting for transfers between devices, per_device(): lax.ppermute(msg_lo, 'section', [(i + 1, i) for i in range(0, sections, 2)])  2.49 us
  transfers between devices with their start and end apart: 32, of which 19 were waited for; matrix products, arithmetic and copies ran while one was open for 0% of the time, Pallas kernels for 11%

profile of v4, /device:TPU:0, one launch (start us, length us, event | category | flops | bytes accessed | tf_op | source)
XLA Modules:
  0.0 111.5 jit_solution(18263071947962611897)
XLA Ops:
  0.6 1.0 broadcast_select_fusion.2
  1.7 3.0 %collective-permute-start.1 = (bf16[96,768]{1,0:T(8,128)(2,1)S(1)}, bf16[96,768]{1,0:T(8,128)(2,1)S(1)}, u32[]{:S(2)}, u32[]{:S(2)}) collective-permute-start(bf16[96,768]{1,0:T(8,128)(2,1)S(1)} %get-tuple-element.116), channel_id=1, source_target_pairs={{0,16},{16,0},{1,17},{17,1},{2,18},{18,2},{3,19},{19,3},{4,20},{20... | collective-permute-start | bytes 442376 | tf_op jit(solution)/shard_map/ppermute | solution.py:350
  4.7 1.0 copy-done
  5.7 0.7 copy-done.3
  6.7 1.6 %collective-permute-start.8 = (bf16[768,128]{1,0:T(8,128)(2,1)S(1)}, bf16[768,128]{1,0:T(8,128)(2,1)S(1)}, u32[]{:S(2)}, u32[]{:S(2)}) collective-permute-start(bf16[768,128]{1,0:T(8,128)(2,1)S(1)} %get-tuple-element.59), channel_id=1, source_target_pairs={{0,2},{1,3},{2,0},{3,1},{4,6},{5,7},{6,4},{7,5},{8,10},{9,11},{10,... | collective-permute-start | bytes 589832 | tf_op jit(solution)/shard_map/ppermute | solution.py:353
  8.3 0.7 copy-done.4
  9.7 2.7 %collective-permute-start.2 = (bf16[96,768]{1,0:T(8,128)(2,1)S(1)}, bf16[96,768]{1,0:T(8,128)(2,1)S(1)}, u32[]{:S(2)}, u32[]{:S(2)}) collective-permute-start(bf16[96,768]{1,0:T(8,128)(2,1)S(1)} %get-tuple-element.61), channel_id=1, source_target_pairs={{0,8},{4,12},{8,0},{12,4},{1,9},{5,13},{9,1},{13,5},{2,10},{6,14},... | collective-permute-start | bytes 442376 | tf_op jit(solution)/shard_map/ppermute | solution.py:356
  12.4 0.7 collective-permute-done.8
  13.3 5.3 %collective-permute-done.2 = bf16[96,768]{1,0:T(8,128)(2,1)S(1)} collective-permute-done((bf16[96,768]{1,0:T(8,128)(2,1)S(1)}, bf16[96,768]{1,0:T(8,128)(2,1)S(1)}, u32[]{:S(2)}, u32[]{:S(2)}) %collective-permute-start.2) | collective-permute-done | bytes 147488 | tf_op jit(solution)/shard_map/ppermute | solution.py:356
  18.6 0.7 collective-permute-start.5
  20.5 2.8 %collective-permute-start.6 = (bf16[96,768]{1,0:T(8,128)(2,1)S(1)}, bf16[96,768]{1,0:T(8,128)(2,1)S(1)}, u32[]{:S(2)}, u32[]{:S(2)}) collective-permute-start(bf16[96,768]{1,0:T(8,128)(2,1)S(1)} %get-tuple-element.69), channel_id=1, source_target_pairs={{0,8},{4,12},{8,0},{12,4},{1,9},{5,13},{9,1},{13,5},{2,10},{6,14},... | collective-permute-start | bytes 442376 | tf_op jit(solution)/shard_map/ppermute | solution.py:356
  23.3 1.6 %collective-permute-start.10 = (bf16[1536,128]{1,0:T(8,128)(2,1)S(1)}, bf16[1536,128]{1,0:T(8,128)(2,1)S(1)}, u32[]{:S(2)}, u32[]{:S(2)}) collective-permute-start(bf16[1536,128]{1,0:T(8,128)(2,1)S(1)} %pad_maximum_fusion.refs_0_), channel_id=1, source_target_pairs={{0,16},{16,0},{1,17},{17,1},{2,18},{18,2},{3,19},{19,3},{4,20},{20... | collective-permute-start | bytes 1179656 | tf_op jit(solution)/shard_map/ppermute | solution.py:350
  24.9 4.8 %collective-permute-done.5 = bf16[192,768]{1,0:T(8,128)(2,1)S(1)} collective-permute-done((bf16[192,768]{1,0:T(8,128)(2,1)S(1)}, bf16[192,768]{1,0:T(8,128)(2,1)S(1)}, u32[]{:S(2)}, u32[]{:S(2)}) %collective-permute-start.5) | collective-permute-done | bytes 294944 | tf_op jit(solution)/shard_map/ppermute | solution.py:356
  30.7 1.3 %collective-permute-start.4 = (bf16[256,768]{1,0:T(8,128)(2,1)S(1)}, bf16[256,768]{1,0:T(8,128)(2,1)S(1)}, u32[]{:S(2)}, u32[]{:S(2)}) collective-permute-start(bf16[256,768]{1,0:T(8,128)(2,1)S(1)} %get-tuple-element.67.refs_3_.own_keys), channel_id=1, source_target_pairs={{0,1},{1,2},{2,3},{4,5},{5,6},{6,7},{8,9},{9,10},{10,11},{12,13},{... | collective-permute-start | bytes 1179656 | tf_op jit(solution)/shard_map/ppermute | solution.py:426
  32.0 0.8 collective-permute-start.7
  33.2 3.4 %collective-permute-done.11 = bf16[192,768]{1,0:T(8,128)(2,1)S(1)} collective-permute-done((bf16[192,768]{1,0:T(8,128)(2,1)S(1)}, bf16[192,768]{1,0:T(8,128)(2,1)S(1)}, u32[]{:S(2)}, u32[]{:S(2)}) %collective-permute-start.11) | collective-permute-done | bytes 294944 | tf_op jit(solution)/shard_map/ppermute | solution.py:353
  36.6 4.1 %collective-permute-done.7 = bf16[192,768]{1,0:T(8,128)(2,1)S(1)} collective-permute-done((bf16[192,768]{1,0:T(8,128)(2,1)S(1)}, bf16[192,768]{1,0:T(8,128)(2,1)S(1)}, u32[]{:S(2)}, u32[]{:S(2)}) %collective-permute-start.7) | collective-permute-done | bytes 294944 | tf_op jit(solution)/shard_map/ppermute | solution.py:356
  40.8 1.1 %collective-permute-start.12 = (bf16[768,768]{1,0:T(8,128)(2,1)S(1)}, bf16[768,768]{1,0:T(8,128)(2,1)S(1)}, u32[]{:S(2)}, u32[]{:S(2)}) collective-permute-start(bf16[768,768]{1,0:T(8,128)(2,1)S(1)} %constant_dynamic-update-slice_fusion.4.refs_4_), channel_id=1, source_target_pairs={{0,1},{1,0},{2,3},{3,2},{4,5},{5,4},{6,7},{7,6},{8,9},{9,8},{10,11... | collective-permute-start | bytes 3538952 | tf_op jit(solution)/shard_map/ppermute | solution.py:353
  42.6 2.0 %collective-permute-start.16 = (bf16[192,768]{1,0:T(8,128)(2,1)S(1)}, bf16[192,768]{1,0:T(8,128)(2,1)S(1)}, u32[]{:S(2)}, u32[]{:S(2)}) collective-permute-start(bf16[192,768]{1,0:T(8,128)(2,1)S(1)} %get-tuple-element.83), channel_id=1, source_target_pairs={{0,2},{1,3},{2,0},{3,1},{4,6},{5,7},{6,4},{7,5},{8,10},{9,11},{10,... | collective-permute-start | bytes 884744 | tf_op jit(solution)/shard_map/ppermute | solution.py:353
  44.7 1.5 %forward_hi.1 = (bf16[128,768]{1,0:T(8,128)(2,1)S(1)}, f32[768,256]{1,0:T(8,128)S(1)}, bf16[1536,768]{1,0:T(8,128)(2,1)S(1)}) custom-call(s32[1,1]{1,0:T(1,128)S(6)} %copy.18.refs_0_, bf16[128,1536]{1,0:T(8,128)(2,1)S(1)} %get-tuple-element.66.refs_1_, bf16[256,768]{1,0:T(8,128)(2,1)S(1)} %collective-permute-done.4.refs_2_.left_keys, ...), custom_call_target="tpu_custom_call" | custom-call | flops 352321536 | bytes 6881280 | tf_op jit(solution)/shard_map/forward_hi/pallas_call | solution.py:31
  46.2 2.9 %upper.1 = (bf16[128,768]{1,0:T(8,128)(2,1)S(1)}, f32[128,768]{1,0:T(8,128)S(1)}, bf16[128,896]{1,0:T(8,128)(2,1)S(1)}, bf16[128,768]{1,0:T(8,128)(2,1)S(1)}, f32[128,128]{1,0:T(8,128)S(1)}) custom-call(s32[1,2]{1,0:T(1,128)S(1)} %copy-done.5, bf16[128,768]{1,0:T(8,128)(2,1)S(1)} %get-tuple-element.63.dy, bf16[128,1536]{1,0:T(8,128)(2,1)S(1)} %get-tuple-element.64.acts, ...), custom_call_target="tpu_custom_call" | custom-call | flops 503316480 | bytes 5849088 | tf_op jit(solution)/shard_map/upper/pallas_call | solution.py:31
  49.1 1.6 %collective-permute-start.13 = (bf16[128,896]{1,0:T(8,128)(2,1)S(1)}, bf16[128,896]{1,0:T(8,128)(2,1)S(1)}, u32[]{:S(2)}, u32[]{:S(2)}) collective-permute-start(bf16[128,896]{1,0:T(8,128)(2,1)S(1)} %get-tuple-element.79.msg), channel_id=1, source_target_pairs={{0,16},{16,0},{1,17},{17,1},{2,18},{18,2},{3,19},{19,3},{4,20},{20... | collective-permute-start | bytes 688136 | tf_op jit(solution)/shard_map/ppermute | solution.py:350
  50.6 1.3 %collective-permute-start.14 = (bf16[128,768]{1,0:T(8,128)(2,1)S(1)}, bf16[128,768]{1,0:T(8,128)(2,1)S(1)}, u32[]{:S(2)}, u32[]{:S(2)}) collective-permute-start(bf16[128,768]{1,0:T(8,128)(2,1)S(1)} %get-tuple-element.80), channel_id=1, source_target_pairs={{1,0},{2,1},{3,2},{5,4},{6,5},{7,6},{9,8},{10,9},{11,10},{13,12},{... | collective-permute-start | bytes 589832 | tf_op jit(solution)/shard_map/ppermute | solution.py:487
  51.9 1.3 %collective-permute-start.15 = (f32[128,128]{1,0:T(8,128)S(1)}, f32[128,128]{1,0:T(8,128)S(1)}, u32[]{:S(2)}, u32[]{:S(2)}) collective-permute-start(f32[128,128]{1,0:T(8,128)S(1)} %get-tuple-element.81), channel_id=1, source_target_pairs={{1,16},{2,17},{3,18},{17,0},{18,1},{19,2},{5,20},{6,21},{7,22},{21... | collective-permute-start | bytes 196616 | tf_op jit(solution)/shard_map/ppermute | solution.py:488
  53.3 1.8 %collective-permute-start.18 = (bf16[384,768]{1,0:T(8,128)(2,1)S(1)}, bf16[384,768]{1,0:T(8,128)(2,1)S(1)}, u32[]{:S(2)}, u32[]{:S(2)}) collective-permute-start(bf16[384,768]{1,0:T(8,128)(2,1)S(1)} %constant_dynamic-update-slice_fusion.9.refs_4_), channel_id=1, source_target_pairs={{0,1},{1,0},{2,3},{3,2},{4,5},{5,4},{6,7},{7,6},{8,9},{9,8},{10,11... | collective-permute-start | bytes 1769480 | tf_op jit(solution)/shard_map/ppermute | solution.py:353
  55.1 2.4 %collective-permute-done.15.sum_other = f32[128,128]{1,0:T(8,128)S(1)} collective-permute-done((f32[128,128]{1,0:T(8,128)S(1)}, f32[128,128]{1,0:T(8,128)S(1)}, u32[]{:S(2)}, u32[]{:S(2)}) %collective-permute-start.15) | collective-permute-done | bytes 65568 | tf_op jit(solution)/shard_map/ppermute | solution.py:488
  57.9 2.7 %collective-permute-start.19 = (bf16[384,768]{1,0:T(8,128)(2,1)S(1)}, bf16[384,768]{1,0:T(8,128)(2,1)S(1)}, u32[]{:S(2)}, u32[]{:S(2)}) collective-permute-start(bf16[384,768]{1,0:T(8,128)(2,1)S(1)} %constant_dynamic-update-slice_fusion.12.refs_5_), channel_id=1, source_target_pairs={{0,1},{1,0},{2,3},{3,2},{4,5},{5,4},{6,7},{7,6},{8,9},{9,8},{10,11... | collective-permute-start | bytes 1769480 | tf_op jit(solution)/shard_map/ppermute | solution.py:353
  60.6 1.6 %collective-permute-done.19.refs_7_ = bf16[384,768]{1,0:T(8,128)(2,1)S(1)} collective-permute-done((bf16[384,768]{1,0:T(8,128)(2,1)S(1)}, bf16[384,768]{1,0:T(8,128)(2,1)S(1)}, u32[]{:S(2)}, u32[]{:S(2)}) %collective-permute-start.19) | collective-permute-done | bytes 589856 | tf_op jit(solution)/shard_map/ppermute | solution.py:353
  62.3 1.5 %forward_lo.1 = (bf16[128,768]{1,0:T(8,128)(2,1)S(1)}, f32[768,256]{1,0:T(8,128)S(1)}, bf16[1536,768]{1,0:T(8,128)(2,1)S(1)}) custom-call(s32[1,1]{1,0:T(1,128)S(6)} %copy.18.refs_0_, bf16[128,1536]{1,0:T(8,128)(2,1)S(1)} %get-tuple-element.82.refs_1_, bf16[256,768]{1,0:T(8,128)(2,1)S(1)} %collective-permute-done.4.refs_2_.left_keys, ...), custom_call_target="tpu_custom_call" | custom-call | flops 352321536 | bytes 6881280 | tf_op jit(solution)/shard_map/forward_lo/pallas_call | solution.py:31
  63.8 2.4 %lower.1 = (bf16[128,768]{1,0:T(8,128)(2,1)S(1)}, bf16[128,768]{1,0:T(8,128)(2,1)S(1)}, f32[128,768]{1,0:T(8,128)S(1)}, bf16[128,768]{1,0:T(8,128)(2,1)S(1)}) custom-call(s32[1,2]{1,0:T(1,128)S(1)} %copy-done.5, f32[128,768]{1,0:T(8,128)S(1)} %get-tuple-element.78.own, bf16[128,896]{1,0:T(8,128)(2,1)S(1)} %get-tuple-element.79.msg, ...), custom_call_target="tpu_custom_call" | custom-call | flops 201326592 | bytes 4505600 | tf_op jit(solution)/shard_map/lower/pallas_call | solution.py:31
  66.1 1.4 %collective-permute-done.21.refs_3_ = bf16[128,768]{1,0:T(8,128)(2,1)S(1)} collective-permute-done((bf16[128,768]{1,0:T(8,128)(2,1)S(1)}, bf16[128,768]{1,0:T(8,128)(2,1)S(1)}, u32[]{:S(2)}, u32[]{:S(2)}) %collective-permute-start.21) | collective-permute-done | bytes 196640 | tf_op jit(solution)/shard_map/ppermute | solution.py:353
  67.6 1.7 %collective-permute-done.22.refs_4_ = bf16[256,768]{1,0:T(8,128)(2,1)S(1)} collective-permute-done((bf16[256,768]{1,0:T(8,128)(2,1)S(1)}, bf16[256,768]{1,0:T(8,128)(2,1)S(1)}, u32[]{:S(2)}, u32[]{:S(2)}) %collective-permute-start.22) | collective-permute-done | bytes 393248 | tf_op jit(solution)/shard_map/ppermute | solution.py:353
  69.9 0.8 collective-permute-start.23
  71.0 6.4 %collective-permute-done.27.refs_3_ = bf16[128,768]{1,0:T(8,128)(2,1)S(1)} collective-permute-done((bf16[128,768]{1,0:T(8,128)(2,1)S(1)}, bf16[128,768]{1,0:T(8,128)(2,1)S(1)}, u32[]{:S(2)}, u32[]{:S(2)}) %collective-permute-start.27) | collective-permute-done | bytes 196640 | tf_op jit(solution)/shard_map/ppermute | solution.py:353
  77.3 1.6 %collective-permute-done.23.arrived = bf16[192,768]{1,0:T(8,128)(2,1)S(1)} collective-permute-done((bf16[192,768]{1,0:T(8,128)(2,1)S(1)}, bf16[192,768]{1,0:T(8,128)(2,1)S(1)}, u32[]{:S(2)}, u32[]{:S(2)}) %collective-permute-start.23) | collective-permute-done | bytes 294944 | tf_op jit(solution)/shard_map/ppermute | solution.py:356
  79.1 1.3 %collective-permute-start.20 = (bf16[128,768]{1,0:T(8,128)(2,1)S(1)}, bf16[128,768]{1,0:T(8,128)(2,1)S(1)}, u32[]{:S(2)}, u32[]{:S(2)}) collective-permute-start(bf16[128,768]{1,0:T(8,128)(2,1)S(1)} %get-tuple-element.92), channel_id=1, source_target_pairs={{1,0},{2,1},{3,2},{5,4},{6,5},{7,6},{9,8},{10,9},{11,10},{13,12},{... | collective-permute-start | bytes 589832 | tf_op jit(solution)/shard_map/ppermute | solution.py:500
  80.4 1.6 %collective-permute-start.25 = (bf16[128,768]{1,0:T(8,128)(2,1)S(1)}, bf16[128,768]{1,0:T(8,128)(2,1)S(1)}, u32[]{:S(2)}, u32[]{:S(2)}) collective-permute-start(bf16[128,768]{1,0:T(8,128)(2,1)S(1)} %get-tuple-element.99.dy_mine), channel_id=1, source_target_pairs={{0,16},{16,0},{1,17},{17,1},{2,18},{18,2},{3,19},{19,3},{4,20},{20... | collective-permute-start | bytes 589832 | tf_op jit(solution)/shard_map/ppermute | solution.py:350
  82.5 0.8 collective-permute-start.29
  83.3 4.0 %collective-permute-start.24 = (bf16[96,768]{1,0:T(8,128)(2,1)S(1)}, bf16[96,768]{1,0:T(8,128)(2,1)S(1)}, u32[]{:S(2)}, u32[]{:S(2)}) collective-permute-start(bf16[96,768]{1,0:T(8,128)(2,1)S(1)} %get-tuple-element.98), channel_id=1, source_target_pairs={{0,8},{4,12},{8,0},{12,4},{1,9},{5,13},{9,1},{13,5},{2,10},{6,14},... | collective-permute-start | bytes 442376 | tf_op jit(solution)/shard_map/ppermute | solution.py:356
  88.1 5.7 %collective-permute-done.24.hi_arrived = bf16[96,768]{1,0:T(8,128)(2,1)S(1)} collective-permute-done((bf16[96,768]{1,0:T(8,128)(2,1)S(1)}, bf16[96,768]{1,0:T(8,128)(2,1)S(1)}, u32[]{:S(2)}, u32[]{:S(2)}) %collective-permute-start.24) | collective-permute-done | bytes 147488 | tf_op jit(solution)/shard_map/ppermute | solution.py:356
  93.8 0.9 project_lo.1
  94.7 1.3 %collective-permute-start.26 = (bf16[128,1536]{1,0:T(8,128)(2,1)S(1)}, bf16[128,1536]{1,0:T(8,128)(2,1)S(1)}, u32[]{:S(2)}, u32[]{:S(2)}) collective-permute-start(bf16[128,1536]{1,0:T(8,128)(2,1)S(1)} %get-tuple-element.102), channel_id=1, source_target_pairs={{16,0},{17,1},{18,2},{19,3},{20,4},{21,5},{22,6},{23,7},{24,8},{25... | collective-permute-start | bytes 1179656 | tf_op jit(solution)/shard_map/ppermute | solution.py:518
  96.1 3.4 %collective-permute-start.30 = (bf16[96,768]{1,0:T(8,128)(2,1)S(1)}, bf16[96,768]{1,0:T(8,128)(2,1)S(1)}, u32[]{:S(2)}, u32[]{:S(2)}) collective-permute-start(bf16[96,768]{1,0:T(8,128)(2,1)S(1)} %get-tuple-element.111), channel_id=1, source_target_pairs={{0,8},{4,12},{8,0},{12,4},{1,9},{5,13},{9,1},{13,5},{2,10},{6,14},... | collective-permute-start | bytes 442376 | tf_op jit(solution)/shard_map/ppermute | solution.py:356
  99.5 4.0 %collective-permute-done.30.lo_arrived = bf16[96,768]{1,0:T(8,128)(2,1)S(1)} collective-permute-done((bf16[96,768]{1,0:T(8,128)(2,1)S(1)}, bf16[96,768]{1,0:T(8,128)(2,1)S(1)}, u32[]{:S(2)}, u32[]{:S(2)}) %collective-permute-start.30) | collective-permute-done | bytes 147488 | tf_op jit(solution)/shard_map/ppermute | solution.py:356
  103.6 2.4 %collective-permute-start.31 = (bf16[96,768]{1,0:T(8,128)(2,1)S(1)}, bf16[96,768]{1,0:T(8,128)(2,1)S(1)}, u32[]{:S(2)}, u32[]{:S(2)}) collective-permute-start(bf16[96,768]{1,0:T(8,128)(2,1)S(1)} %get-tuple-element.113), channel_id=1, source_target_pairs={{0,16},{16,0},{1,17},{17,1},{2,18},{18,2},{3,19},{19,3},{4,20},{20... | collective-permute-start | bytes 442376 | tf_op jit(solution)/shard_map/ppermute | solution.py:350
  106.1 2.5 %collective-permute-done.26.msg_in = bf16[128,1536]{1,0:T(8,128)(2,1)S(1)} collective-permute-done((bf16[128,1536]{1,0:T(8,128)(2,1)S(1)}, bf16[128,1536]{1,0:T(8,128)(2,1)S(1)}, u32[]{:S(2)}, u32[]{:S(2)}) %collective-permute-start.26) | collective-permute-done | bytes 393248 | tf_op jit(solution)/shard_map/ppermute | solution.py:518
  108.6 2.0 %finish.1 = bf16[128,1536]{1,0:T(8,128)(2,1)} custom-call(s32[1,2]{1,0:T(1,128)S(1)} %copy-done.5, f32[128,1536]{1,0:T(8,128)S(1)} %get-tuple-element.101.part, bf16[128,1536]{1,0:T(8,128)(2,1)S(1)} %collective-permute-done.26.msg_in, bf16[128,1536]{1,0:T(8,128)(2,1)S(1)} %get-tuple-element.103.acts, f32[8,1536]{1,0:T(8,128)S(1)} %get-tuple-element.65.vecs, ...), custom_call_target="tpu_custom_call" | custom-call | flops 3932160 | bytes 2408448 | tf_op jit(solution)/shard_map/finish/pallas_call | solution.py:31
  110.8 0.7 maximum_bitcast_fusion
  (62 shorter events, 6.9 us)
Async XLA Ops:
  1.7 8.0 %collective-permute-start.1 = (bf16[96,768]{1,0:T(8,128)(2,1)S(1)}, bf16[96,768]{1,0:T(8,128)(2,1)S(1)}, u32[]{:S(2)}, u32[]{:S(2)}) collective-permute-start(bf16[96,768]{1,0:T(8,128)(2,1)S(1)} %get-tuple-element.116), channel_id=1, source_target_pairs={{0,16},{16,0},{1,17},{17,1},{2,18},{18,2},{3,19},{19,3},{4,20},{20... | collective-permute-start | bytes 442376 | tf_op jit(solution)/shard_map/ppermute | solution.py:350
  4.7 1.0 copy-start
  5.7 0.7 copy-start.3
  6.7 6.4 %collective-permute-start.8 = (bf16[768,128]{1,0:T(8,128)(2,1)S(1)}, bf16[768,128]{1,0:T(8,128)(2,1)S(1)}, u32[]{:S(2)}, u32[]{:S(2)}) collective-permute-start(bf16[768,128]{1,0:T(8,128)(2,1)S(1)} %get-tuple-element.59), channel_id=1, source_target_pairs={{0,2},{1,3},{2,0},{3,1},{4,6},{5,7},{6,4},{7,5},{8,10},{9,11},{10,... | collective-permute-start | bytes 589832 | tf_op jit(solution)/shard_map/ppermute | solution.py:353
  8.3 0.7 copy-start.4
  9.1 11.4 %collective-permute-start = (bf16[144,1536]{1,0:T(8,128)(2,1)S(1)}, bf16[144,1536]{1,0:T(8,128)(2,1)S(1)}, u32[]{:S(2)}, u32[]{:S(2)}) collective-permute-start(bf16[144,1536]{1,0:T(8,128)(2,1)S(1)} %pack.1), channel_id=1, source_target_pairs={{0,16},{16,0},{1,17},{17,1},{2,18},{18,2},{3,19},{19,3},{4,20},{20... | collective-permute-start | bytes 1327112 | tf_op jit(solution)/shard_map/ppermute | solution.py:350
  9.7 8.9 %collective-permute-start.2 = (bf16[96,768]{1,0:T(8,128)(2,1)S(1)}, bf16[96,768]{1,0:T(8,128)(2,1)S(1)}, u32[]{:S(2)}, u32[]{:S(2)}) collective-permute-start(bf16[96,768]{1,0:T(8,128)(2,1)S(1)} %get-tuple-element.61), channel_id=1, source_target_pairs={{0,8},{4,12},{8,0},{12,4},{1,9},{5,13},{9,1},{13,5},{2,10},{6,14},... | collective-permute-start | bytes 442376 | tf_op jit(solution)/shard_map/ppermute | solution.py:356
  13.1 17.1 %copy-start.1 = (bf16[1,1,128,1536]{3,2,1,0:T(8,128)(2,1)S(1)}, bf16[1,1,128,1536]{3,2,1,0:T(8,128)(2,1)}, u32[]{:S(2)}) copy-start(bf16[1,1,128,1536]{3,2,1,0:T(8,128)(2,1)} %param.7) | copy-start | bytes 1179652
  13.1 17.1 %copy-start.2 = (bf16[1,128,1536]{2,1,0:T(8,128)(2,1)S(1)}, bf16[1,128,1536]{2,1,0:T(8,128)(2,1)}, u32[]{:S(2)}) copy-start(bf16[1,128,1536]{2,1,0:T(8,128)(2,1)} %param.8) | copy-start | bytes 1179652
  13.2 10.1 %collective-permute-start.9 = (bf16[768,128]{1,0:T(8,128)(2,1)S(1)}, bf16[768,128]{1,0:T(8,128)(2,1)S(1)}, u32[]{:S(2)}, u32[]{:S(2)}) collective-permute-start(bf16[768,128]{1,0:T(8,128)(2,1)S(1)} %pad_maximum_fusion.3), channel_id=1, source_target_pairs={{0,1},{1,0},{2,3},{3,2},{4,5},{5,4},{6,7},{7,6},{8,9},{9,8},{10,11... | collective-permute-start | bytes 589832 | tf_op jit(solution)/shard_map/ppermute | solution.py:353
  18.6 11.1 %collective-permute-start.5 = (bf16[192,768]{1,0:T(8,128)(2,1)S(1)}, bf16[192,768]{1,0:T(8,128)(2,1)S(1)}, u32[]{:S(2)}, u32[]{:S(2)}) collective-permute-start(bf16[192,768]{1,0:T(8,128)(2,1)S(1)} %get-tuple-element.127), channel_id=1, source_target_pairs={{0,4},{4,0},{8,12},{12,8},{1,5},{5,1},{9,13},{13,9},{2,6},{6,2},{1... | collective-permute-start | bytes 884744 | tf_op jit(solution)/shard_map/ppermute | solution.py:356
  19.4 10.9 %collective-permute-start.3 = (bf16[192,768]{1,0:T(8,128)(2,1)S(1)}, bf16[192,768]{1,0:T(8,128)(2,1)S(1)}, u32[]{:S(2)}, u32[]{:S(2)}) collective-permute-start(bf16[192,768]{1,0:T(8,128)(2,1)S(1)} %get-tuple-element.127), channel_id=1, source_target_pairs={{0,2},{1,3},{2,0},{3,1},{4,6},{5,7},{6,4},{7,5},{8,10},{9,11},{10,... | collective-permute-start | bytes 884744 | tf_op jit(solution)/shard_map/ppermute | solution.py:353
  20.5 11.5 %collective-permute-start.6 = (bf16[96,768]{1,0:T(8,128)(2,1)S(1)}, bf16[96,768]{1,0:T(8,128)(2,1)S(1)}, u32[]{:S(2)}, u32[]{:S(2)}) collective-permute-start(bf16[96,768]{1,0:T(8,128)(2,1)S(1)} %get-tuple-element.69), channel_id=1, source_target_pairs={{0,8},{4,12},{8,0},{12,4},{1,9},{5,13},{9,1},{13,5},{2,10},{6,14},... | collective-permute-start | bytes 442376 | tf_op jit(solution)/shard_map/ppermute | solution.py:356
  23.3 9.9 %collective-permute-start.10 = (bf16[1536,128]{1,0:T(8,128)(2,1)S(1)}, bf16[1536,128]{1,0:T(8,128)(2,1)S(1)}, u32[]{:S(2)}, u32[]{:S(2)}) collective-permute-start(bf16[1536,128]{1,0:T(8,128)(2,1)S(1)} %pad_maximum_fusion.refs_0_), channel_id=1, source_target_pairs={{0,16},{16,0},{1,17},{17,1},{2,18},{18,2},{3,19},{19,3},{4,20},{20... | collective-permute-start | bytes 1179656 | tf_op jit(solution)/shard_map/ppermute | solution.py:350
  29.7 6.9 %collective-permute-start.11 = (bf16[192,768]{1,0:T(8,128)(2,1)S(1)}, bf16[192,768]{1,0:T(8,128)(2,1)S(1)}, u32[]{:S(2)}, u32[]{:S(2)}) collective-permute-start(bf16[192,768]{1,0:T(8,128)(2,1)S(1)} %collective-permute-done.5), channel_id=1, source_target_pairs={{0,2},{1,3},{2,0},{3,1},{4,6},{5,7},{6,4},{7,5},{8,10},{9,11},{10,... | collective-permute-start | bytes 884744 | tf_op jit(solution)/shard_map/ppermute | solution.py:353
  30.7 10.1 %collective-permute-start.4 = (bf16[256,768]{1,0:T(8,128)(2,1)S(1)}, bf16[256,768]{1,0:T(8,128)(2,1)S(1)}, u32[]{:S(2)}, u32[]{:S(2)}) collective-permute-start(bf16[256,768]{1,0:T(8,128)(2,1)S(1)} %get-tuple-element.67.refs_3_.own_keys), channel_id=1, source_target_pairs={{0,1},{1,2},{2,3},{4,5},{5,6},{6,7},{8,9},{9,10},{10,11},{12,13},{... | collective-permute-start | bytes 1179656 | tf_op jit(solution)/shard_map/ppermute | solution.py:426
  32.0 8.7 %collective-permute-start.7 = (bf16[192,768]{1,0:T(8,128)(2,1)S(1)}, bf16[192,768]{1,0:T(8,128)(2,1)S(1)}, u32[]{:S(2)}, u32[]{:S(2)}) collective-permute-start(bf16[192,768]{1,0:T(8,128)(2,1)S(1)} %get-tuple-element.83), channel_id=1, source_target_pairs={{0,4},{4,0},{8,12},{12,8},{1,5},{5,1},{9,13},{13,9},{2,6},{6,2},{1... | collective-permute-start | bytes 884744 | tf_op jit(solution)/shard_map/ppermute | solution.py:356
  40.8 3.9 %collective-permute-start.12 = (bf16[768,768]{1,0:T(8,128)(2,1)S(1)}, bf16[768,768]{1,0:T(8,128)(2,1)S(1)}, u32[]{:S(2)}, u32[]{:S(2)}) collective-permute-start(bf16[768,768]{1,0:T(8,128)(2,1)S(1)} %constant_dynamic-update-slice_fusion.4.refs_4_), channel_id=1, source_target_pairs={{0,1},{1,0},{2,3},{3,2},{4,5},{5,4},{6,7},{7,6},{8,9},{9,8},{10,11... | collective-permute-start | bytes 3538952 | tf_op jit(solution)/shard_map/ppermute | solution.py:353
  42.6 10.7 %collective-permute-start.17 = (bf16[192,768]{1,0:T(8,128)(2,1)S(1)}, bf16[192,768]{1,0:T(8,128)(2,1)S(1)}, u32[]{:S(2)}, u32[]{:S(2)}) collective-permute-start(bf16[192,768]{1,0:T(8,128)(2,1)S(1)} %collective-permute-done.7), channel_id=1, source_target_pairs={{0,2},{1,3},{2,0},{3,1},{4,6},{5,7},{6,4},{7,5},{8,10},{9,11},{10,... | collective-permute-start | bytes 884744 | tf_op jit(solution)/shard_map/ppermute | solution.py:353
  42.6 15.2 %collective-permute-start.16 = (bf16[192,768]{1,0:T(8,128)(2,1)S(1)}, bf16[192,768]{1,0:T(8,128)(2,1)S(1)}, u32[]{:S(2)}, u32[]{:S(2)}) collective-permute-start(bf16[192,768]{1,0:T(8,128)(2,1)S(1)} %get-tuple-element.83), channel_id=1, source_target_pairs={{0,2},{1,3},{2,0},{3,1},{4,6},{5,7},{6,4},{7,5},{8,10},{9,11},{10,... | collective-permute-start | bytes 884744 | tf_op jit(solution)/shard_map/ppermute | solution.py:353
  44.7 1.5 %copy-start.5 = (s32[1,2]{1,0:T(1,128)S(1)}, s32[1,2]{1,0:T(1,128)}, u32[]{:S(2)}) copy-start(s32[1,2]{1,0:T(1,128)} %kept.5) | copy-start | bytes 28
  49.1 8.4 %collective-permute-start.13 = (bf16[128,896]{1,0:T(8,128)(2,1)S(1)}, bf16[128,896]{1,0:T(8,128)(2,1)S(1)}, u32[]{:S(2)}, u32[]{:S(2)}) collective-permute-start(bf16[128,896]{1,0:T(8,128)(2,1)S(1)} %get-tuple-element.79.msg), channel_id=1, source_target_pairs={{0,16},{16,0},{1,17},{17,1},{2,18},{18,2},{3,19},{19,3},{4,20},{20... | collective-permute-start | bytes 688136 | tf_op jit(solution)/shard_map/ppermute | solution.py:350
  50.6 6.9 %collective-permute-start.14 = (bf16[128,768]{1,0:T(8,128)(2,1)S(1)}, bf16[128,768]{1,0:T(8,128)(2,1)S(1)}, u32[]{:S(2)}, u32[]{:S(2)}) collective-permute-start(bf16[128,768]{1,0:T(8,128)(2,1)S(1)} %get-tuple-element.80), channel_id=1, source_target_pairs={{1,0},{2,1},{3,2},{5,4},{6,5},{7,6},{9,8},{10,9},{11,10},{13,12},{... | collective-permute-start | bytes 589832 | tf_op jit(solution)/shard_map/ppermute | solution.py:487
  51.9 5.6 %collective-permute-start.15 = (f32[128,128]{1,0:T(8,128)S(1)}, f32[128,128]{1,0:T(8,128)S(1)}, u32[]{:S(2)}, u32[]{:S(2)}) collective-permute-start(f32[128,128]{1,0:T(8,128)S(1)} %get-tuple-element.81), channel_id=1, source_target_pairs={{1,16},{2,17},{3,18},{17,0},{18,1},{19,2},{5,20},{6,21},{7,22},{21... | collective-permute-start | bytes 196616 | tf_op jit(solution)/shard_map/ppermute | solution.py:488
  53.3 7.4 %collective-permute-start.18 = (bf16[384,768]{1,0:T(8,128)(2,1)S(1)}, bf16[384,768]{1,0:T(8,128)(2,1)S(1)}, u32[]{:S(2)}, u32[]{:S(2)}) collective-permute-start(bf16[384,768]{1,0:T(8,128)(2,1)S(1)} %constant_dynamic-update-slice_fusion.9.refs_4_), channel_id=1, source_target_pairs={{0,1},{1,0},{2,3},{3,2},{4,5},{5,4},{6,7},{7,6},{8,9},{9,8},{10,11... | collective-permute-start | bytes 1769480 | tf_op jit(solution)/shard_map/ppermute | solution.py:353
  57.9 4.3 %collective-permute-start.19 = (bf16[384,768]{1,0:T(8,128)(2,1)S(1)}, bf16[384,768]{1,0:T(8,128)(2,1)S(1)}, u32[]{:S(2)}, u32[]{:S(2)}) collective-permute-start(bf16[384,768]{1,0:T(8,128)(2,1)S(1)} %constant_dynamic-update-slice_fusion.12.refs_5_), channel_id=1, source_target_pairs={{0,1},{1,0},{2,3},{3,2},{4,5},{5,4},{6,7},{7,6},{8,9},{9,8},{10,11... | collective-permute-start | bytes 1769480 | tf_op jit(solution)/shard_map/ppermute | solution.py:353
  60.6 6.9 %collective-permute-start.21 = (bf16[128,768]{1,0:T(8,128)(2,1)S(1)}, bf16[128,768]{1,0:T(8,128)(2,1)S(1)}, u32[]{:S(2)}, u32[]{:S(2)}) collective-permute-start(bf16[128,768]{1,0:T(8,128)(2,1)S(1)} %get-tuple-element.94.refs_2_), channel_id=1, source_target_pairs={{0,2},{1,3},{2,0},{3,1},{4,6},{5,7},{6,4},{7,5},{8,10},{9,11},{10,... | collective-permute-start | bytes 589832 | tf_op jit(solution)/shard_map/ppermute | solution.py:353
  67.5 1.8 %collective-permute-start.22 = (bf16[256,768]{1,0:T(8,128)(2,1)S(1)}, bf16[256,768]{1,0:T(8,128)(2,1)S(1)}, u32[]{:S(2)}, u32[]{:S(2)}) collective-permute-start(bf16[256,768]{1,0:T(8,128)(2,1)S(1)} %pad_maximum_fusion.1), channel_id=1, source_target_pairs={{0,1},{1,0},{2,3},{3,2},{4,5},{5,4},{6,7},{7,6},{8,9},{9,8},{10,11... | collective-permute-start | bytes 1179656 | tf_op jit(solution)/shard_map/ppermute | solution.py:353
  69.9 9.1 %collective-permute-start.23 = (bf16[192,768]{1,0:T(8,128)(2,1)S(1)}, bf16[192,768]{1,0:T(8,128)(2,1)S(1)}, u32[]{:S(2)}, u32[]{:S(2)}) collective-permute-start(bf16[192,768]{1,0:T(8,128)(2,1)S(1)} %get-tuple-element.97), channel_id=1, source_target_pairs={{0,4},{4,0},{8,12},{12,8},{1,5},{5,1},{9,13},{13,9},{2,6},{6,2},{1... | collective-permute-start | bytes 884744 | tf_op jit(solution)/shard_map/ppermute | solution.py:356
  70.7 6.7 %collective-permute-start.27 = (bf16[128,768]{1,0:T(8,128)(2,1)S(1)}, bf16[128,768]{1,0:T(8,128)(2,1)S(1)}, u32[]{:S(2)}, u32[]{:S(2)}) collective-permute-start(bf16[128,768]{1,0:T(8,128)(2,1)S(1)} %get-tuple-element.89.qg.refs_2_), channel_id=1, source_target_pairs={{0,2},{1,3},{2,0},{3,1},{4,6},{5,7},{6,4},{7,5},{8,10},{9,11},{10,... | collective-permute-start | bytes 589832 | tf_op jit(solution)/shard_map/ppermute | solution.py:353
  79.0 3.0 %collective-permute-start.28 = (bf16[256,768]{1,0:T(8,128)(2,1)S(1)}, bf16[256,768]{1,0:T(8,128)(2,1)S(1)}, u32[]{:S(2)}, u32[]{:S(2)}) collective-permute-start(bf16[256,768]{1,0:T(8,128)(2,1)S(1)} %pad_maximum_fusion.2), channel_id=1, source_target_pairs={{0,1},{1,0},{2,3},{3,2},{4,5},{5,4},{6,7},{7,6},{8,9},{9,8},{10,11... | collective-permute-start | bytes 1179656 | tf_op jit(solution)/shard_map/ppermute | solution.py:353
  79.1 8.3 %collective-permute-start.20 = (bf16[128,768]{1,0:T(8,128)(2,1)S(1)}, bf16[128,768]{1,0:T(8,128)(2,1)S(1)}, u32[]{:S(2)}, u32[]{:S(2)}) collective-permute-start(bf16[128,768]{1,0:T(8,128)(2,1)S(1)} %get-tuple-element.92), channel_id=1, source_target_pairs={{1,0},{2,1},{3,2},{5,4},{6,5},{7,6},{9,8},{10,9},{11,10},{13,12},{... | collective-permute-start | bytes 589832 | tf_op jit(solution)/shard_map/ppermute | solution.py:500
  80.4 7.7 %collective-permute-start.25 = (bf16[128,768]{1,0:T(8,128)(2,1)S(1)}, bf16[128,768]{1,0:T(8,128)(2,1)S(1)}, u32[]{:S(2)}, u32[]{:S(2)}) collective-permute-start(bf16[128,768]{1,0:T(8,128)(2,1)S(1)} %get-tuple-element.99.dy_mine), channel_id=1, source_target_pairs={{0,16},{16,0},{1,17},{17,1},{2,18},{18,2},{3,19},{19,3},{4,20},{20... | collective-permute-start | bytes 589832 | tf_op jit(solution)/shard_map/ppermute | solution.py:350
  82.5 13.5 %collective-permute-start.29 = (bf16[192,768]{1,0:T(8,128)(2,1)S(1)}, bf16[192,768]{1,0:T(8,128)(2,1)S(1)}, u32[]{:S(2)}, u32[]{:S(2)}) collective-permute-start(bf16[192,768]{1,0:T(8,128)(2,1)S(1)} %get-tuple-element.108), channel_id=1, source_target_pairs={{0,4},{4,0},{8,12},{12,8},{1,5},{5,1},{9,13},{13,9},{2,6},{6,2},{1... | collective-permute-start | bytes 884744 | tf_op jit(solution)/shard_map/ppermute | solution.py:356
  83.3 10.4 %collective-permute-start.24 = (bf16[96,768]{1,0:T(8,128)(2,1)S(1)}, bf16[96,768]{1,0:T(8,128)(2,1)S(1)}, u32[]{:S(2)}, u32[]{:S(2)}) collective-permute-start(bf16[96,768]{1,0:T(8,128)(2,1)S(1)} %get-tuple-element.98), channel_id=1, source_target_pairs={{0,8},{4,12},{8,0},{12,4},{1,9},{5,13},{9,1},{13,5},{2,10},{6,14},... | collective-permute-start | bytes 442376 | tf_op jit(solution)/shard_map/ppermute | solution.py:356
  94.7 13.9 %collective-permute-start.26 = (bf16[128,1536]{1,0:T(8,128)(2,1)S(1)}, bf16[128,1536]{1,0:T(8,128)(2,1)S(1)}, u32[]{:S(2)}, u32[]{:S(2)}) collective-permute-start(bf16[128,1536]{1,0:T(8,128)(2,1)S(1)} %get-tuple-element.102), channel_id=1, source_target_pairs={{16,0},{17,1},{18,2},{19,3},{20,4},{21,5},{22,6},{23,7},{24,8},{25... | collective-permute-start | bytes 1179656 | tf_op jit(solution)/shard_map/ppermute | solution.py:518
  96.1 7.5 %collective-permute-start.30 = (bf16[96,768]{1,0:T(8,128)(2,1)S(1)}, bf16[96,768]{1,0:T(8,128)(2,1)S(1)}, u32[]{:S(2)}, u32[]{:S(2)}) collective-permute-start(bf16[96,768]{1,0:T(8,128)(2,1)S(1)} %get-tuple-element.111), channel_id=1, source_target_pairs={{0,8},{4,12},{8,0},{12,4},{1,9},{5,13},{9,1},{13,5},{2,10},{6,14},... | collective-permute-start | bytes 442376 | tf_op jit(solution)/shard_map/ppermute | solution.py:356
  103.6 7.1 %collective-permute-start.31 = (bf16[96,768]{1,0:T(8,128)(2,1)S(1)}, bf16[96,768]{1,0:T(8,128)(2,1)S(1)}, u32[]{:S(2)}, u32[]{:S(2)}) collective-permute-start(bf16[96,768]{1,0:T(8,128)(2,1)S(1)} %get-tuple-element.113), channel_id=1, source_target_pairs={{0,16},{16,0},{1,17},{17,1},{2,18},{18,2},{3,19},{19,3},{4,20},{20... | collective-permute-start | bytes 442376 | tf_op jit(solution)/shard_map/ppermute | solution.py:350

commit v5 on v4

--- a/solution.py
+++ b/solution.py
@@ -504,7 +504,7 @@
             mine_hi, sent_hi = weight_grad("weight_grad_hi", True, gathered_hi)
             first_hi = along(sent_hi, steps[-1])
             clips_hi = over_clips("add_pair_hi", mine_hi, first_hi)
-            left_in_lo = tied(left_in_lo, clips_hi[1], dy_in)
+            left_in_lo = tied(left_in_lo, clips_hi[0], dy_in)
         part_lo, msg_lo = call(
             project_kernel, [sds((tile, dim), F32), sds((tile, dim), BF)], matmul_flops,
             "project_lo", qg_lo, weights_lo, key_own, left_in_lo,

time: 114 us -> 112 us (0.982); the launches traced: 112 us -> 112 us
  waiting for transfers between devices: 47.9 us -> 50.9 us
  starting transfers between devices: 44.2 us -> 41.3 us
    ppermute x8, waiting for transfers between devices: 25.6 us -> 28.6 us  [along(): return lax.ppermute(value, 'fsdp', [(f, f ^ flip) for f in range(fsdps)])]
    ppermute x1, waiting for transfers between devices: 2.49 us -> 0.01 us  [per_device(): lax.ppermute(msg_lo, 'section', [(i + 1, i) for i in range(0, sections, 2)])]
    ppermute x6, waiting for transfers between devices: 1.8 us -> 4.22 us  [swap(): return lax.ppermute(value, 'section', swap_pairs)]
    ppermute x6, starting transfers between devices: 10.7 us -> 8.87 us  [swap(): return lax.ppermute(value, 'section', swap_pairs)]
where the time goes in v5:
time: 112 us
  waiting for transfers between devices  50.9 us (45%)
  starting transfers between devices  41.3 us (37%)
  Pallas kernels  13.2 us (12%)
  local copies, waits for them, and re-layouts  2.63 us (2%)
  other arithmetic  1.87 us (2%)
  between operations  1.62 us (1%)
    ppermute x8, waiting for transfers between devices, along(): return lax.ppermute(value, 'fsdp', [(f, f ^ flip) for f in range(fsdps)])  28.6 us
    ppermute x13, waiting for transfers between devices, across(): return lax.ppermute(value, 'seq', [(s, s ^ offset) for s in range(seqs)])  15.6 us
    ppermute x8, starting transfers between devices, along(): return lax.ppermute(value, 'fsdp', [(f, f ^ flip) for f in range(fsdps)])  15 us
    pallas_call x15, Pallas kernels, call(): pl.pallas_call(kernel, out_shape=outs, in_specs=[pl.BlockSpec(memory_spac...  13.2 us
    ppermute x13, starting transfers between devices, across(): return lax.ppermute(value, 'seq', [(s, s ^ offset) for s in range(seqs)])  10.9 us
    ppermute x6, starting transfers between devices, swap(): return lax.ppermute(value, 'section', swap_pairs)  8.87 us
    ppermute x6, waiting for transfers between devices, swap(): return lax.ppermute(value, 'section', swap_pairs)  4.22 us
    unnamed x19, local copies, waits for them, and re-layouts  2.54 us
  transfers between devices with their start and end apart: 32, of which 19 were waited for; matrix products, arithmetic and copies ran while one was open for 0% of the time, Pallas kernels for 11%

profile of v5, /device:TPU:0, one launch (start us, length us, event | category | flops | bytes accessed | tf_op | source)
XLA Modules:
  0.0 111.5 jit_solution(4947371282603429559)
XLA Ops:
  0.6 1.0 broadcast_select_fusion.2
  1.7 3.0 %collective-permute-start.1 = (bf16[96,768]{1,0:T(8,128)(2,1)S(1)}, bf16[96,768]{1,0:T(8,128)(2,1)S(1)}, u32[]{:S(2)}, u32[]{:S(2)}) collective-permute-start(bf16[96,768]{1,0:T(8,128)(2,1)S(1)} %get-tuple-element.116), channel_id=1, source_target_pairs={{0,16},{16,0},{1,17},{17,1},{2,18},{18,2},{3,19},{19,3},{4,20},{20... | collective-permute-start | bytes 442376 | tf_op jit(solution)/shard_map/ppermute | solution.py:350
  4.7 1.0 copy-done
  5.7 0.7 copy-done.3
  6.7 1.6 %collective-permute-start.8 = (bf16[768,128]{1,0:T(8,128)(2,1)S(1)}, bf16[768,128]{1,0:T(8,128)(2,1)S(1)}, u32[]{:S(2)}, u32[]{:S(2)}) collective-permute-start(bf16[768,128]{1,0:T(8,128)(2,1)S(1)} %get-tuple-element.59), channel_id=1, source_target_pairs={{0,2},{1,3},{2,0},{3,1},{4,6},{5,7},{6,4},{7,5},{8,10},{9,11},{10,... | collective-permute-start | bytes 589832 | tf_op jit(solution)/shard_map/ppermute | solution.py:353
  8.3 0.7 copy-done.4
  9.7 2.7 %collective-permute-start.2 = (bf16[96,768]{1,0:T(8,128)(2,1)S(1)}, bf16[96,768]{1,0:T(8,128)(2,1)S(1)}, u32[]{:S(2)}, u32[]{:S(2)}) collective-permute-start(bf16[96,768]{1,0:T(8,128)(2,1)S(1)} %get-tuple-element.61), channel_id=1, source_target_pairs={{0,8},{4,12},{8,0},{12,4},{1,9},{5,13},{9,1},{13,5},{2,10},{6,14},... | collective-permute-start | bytes 442376 | tf_op jit(solution)/shard_map/ppermute | solution.py:356
  12.4 0.7 collective-permute-done.8
  13.3 5.3 %collective-permute-done.2 = bf16[96,768]{1,0:T(8,128)(2,1)S(1)} collective-permute-done((bf16[96,768]{1,0:T(8,128)(2,1)S(1)}, bf16[96,768]{1,0:T(8,128)(2,1)S(1)}, u32[]{:S(2)}, u32[]{:S(2)}) %collective-permute-start.2) | collective-permute-done | bytes 147488 | tf_op jit(solution)/shard_map/ppermute | solution.py:356
  18.6 0.7 collective-permute-start.5
  20.5 2.8 %collective-permute-start.6 = (bf16[96,768]{1,0:T(8,128)(2,1)S(1)}, bf16[96,768]{1,0:T(8,128)(2,1)S(1)}, u32[]{:S(2)}, u32[]{:S(2)}) collective-permute-start(bf16[96,768]{1,0:T(8,128)(2,1)S(1)} %get-tuple-element.69), channel_id=1, source_target_pairs={{0,8},{4,12},{8,0},{12,4},{1,9},{5,13},{9,1},{13,5},{2,10},{6,14},... | collective-permute-start | bytes 442376 | tf_op jit(solution)/shard_map/ppermute | solution.py:356
  23.3 1.6 %collective-permute-start.10 = (bf16[1536,128]{1,0:T(8,128)(2,1)S(1)}, bf16[1536,128]{1,0:T(8,128)(2,1)S(1)}, u32[]{:S(2)}, u32[]{:S(2)}) collective-permute-start(bf16[1536,128]{1,0:T(8,128)(2,1)S(1)} %pad_maximum_fusion.refs_0_), channel_id=1, source_target_pairs={{0,16},{16,0},{1,17},{17,1},{2,18},{18,2},{3,19},{19,3},{4,20},{20... | collective-permute-start | bytes 1179656 | tf_op jit(solution)/shard_map/ppermute | solution.py:350
  24.9 4.8 %collective-permute-done.5 = bf16[192,768]{1,0:T(8,128)(2,1)S(1)} collective-permute-done((bf16[192,768]{1,0:T(8,128)(2,1)S(1)}, bf16[192,768]{1,0:T(8,128)(2,1)S(1)}, u32[]{:S(2)}, u32[]{:S(2)}) %collective-permute-start.5) | collective-permute-done | bytes 294944 | tf_op jit(solution)/shard_map/ppermute | solution.py:356
  30.7 1.3 %collective-permute-start.4 = (bf16[256,768]{1,0:T(8,128)(2,1)S(1)}, bf16[256,768]{1,0:T(8,128)(2,1)S(1)}, u32[]{:S(2)}, u32[]{:S(2)}) collective-permute-start(bf16[256,768]{1,0:T(8,128)(2,1)S(1)} %get-tuple-element.67.refs_3_.own_keys), channel_id=1, source_target_pairs={{0,1},{1,2},{2,3},{4,5},{5,6},{6,7},{8,9},{9,10},{10,11},{12,13},{... | collective-permute-start | bytes 1179656 | tf_op jit(solution)/shard_map/ppermute | solution.py:426
  32.0 0.8 collective-permute-start.7
  33.2 3.4 %collective-permute-done.11 = bf16[192,768]{1,0:T(8,128)(2,1)S(1)} collective-permute-done((bf16[192,768]{1,0:T(8,128)(2,1)S(1)}, bf16[192,768]{1,0:T(8,128)(2,1)S(1)}, u32[]{:S(2)}, u32[]{:S(2)}) %collective-permute-start.11) | collective-permute-done | bytes 294944 | tf_op jit(solution)/shard_map/ppermute | solution.py:353
  36.6 4.1 %collective-permute-done.7 = bf16[192,768]{1,0:T(8,128)(2,1)S(1)} collective-permute-done((bf16[192,768]{1,0:T(8,128)(2,1)S(1)}, bf16[192,768]{1,0:T(8,128)(2,1)S(1)}, u32[]{:S(2)}, u32[]{:S(2)}) %collective-permute-start.7) | collective-permute-done | bytes 294944 | tf_op jit(solution)/shard_map/ppermute | solution.py:356
  40.8 1.1 %collective-permute-start.12 = (bf16[768,768]{1,0:T(8,128)(2,1)S(1)}, bf16[768,768]{1,0:T(8,128)(2,1)S(1)}, u32[]{:S(2)}, u32[]{:S(2)}) collective-permute-start(bf16[768,768]{1,0:T(8,128)(2,1)S(1)} %constant_dynamic-update-slice_fusion.4.refs_4_), channel_id=1, source_target_pairs={{0,1},{1,0},{2,3},{3,2},{4,5},{5,4},{6,7},{7,6},{8,9},{9,8},{10,11... | collective-permute-start | bytes 3538952 | tf_op jit(solution)/shard_map/ppermute | solution.py:353
  42.6 2.0 %collective-permute-start.16 = (bf16[192,768]{1,0:T(8,128)(2,1)S(1)}, bf16[192,768]{1,0:T(8,128)(2,1)S(1)}, u32[]{:S(2)}, u32[]{:S(2)}) collective-permute-start(bf16[192,768]{1,0:T(8,128)(2,1)S(1)} %get-tuple-element.83), channel_id=1, source_target_pairs={{0,2},{1,3},{2,0},{3,1},{4,6},{5,7},{6,4},{7,5},{8,10},{9,11},{10,... | collective-permute-start | bytes 884744 | tf_op jit(solution)/shard_map/ppermute | solution.py:353
  44.7 1.5 %forward_hi.1 = (bf16[128,768]{1,0:T(8,128)(2,1)S(1)}, f32[768,256]{1,0:T(8,128)S(1)}, bf16[1536,768]{1,0:T(8,128)(2,1)S(1)}) custom-call(s32[1,1]{1,0:T(1,128)S(6)} %copy.18.refs_0_, bf16[128,1536]{1,0:T(8,128)(2,1)S(1)} %get-tuple-element.66.refs_1_, bf16[256,768]{1,0:T(8,128)(2,1)S(1)} %collective-permute-done.4.refs_2_.left_keys, ...), custom_call_target="tpu_custom_call" | custom-call | flops 352321536 | bytes 6881280 | tf_op jit(solution)/shard_map/forward_hi/pallas_call | solution.py:31
  46.2 2.9 %upper.1 = (bf16[128,768]{1,0:T(8,128)(2,1)S(1)}, f32[128,768]{1,0:T(8,128)S(1)}, bf16[128,896]{1,0:T(8,128)(2,1)S(1)}, bf16[128,768]{1,0:T(8,128)(2,1)S(1)}, f32[128,128]{1,0:T(8,128)S(1)}) custom-call(s32[1,2]{1,0:T(1,128)S(1)} %copy-done.5, bf16[128,768]{1,0:T(8,128)(2,1)S(1)} %get-tuple-element.63.dy, bf16[128,1536]{1,0:T(8,128)(2,1)S(1)} %get-tuple-element.64.acts, ...), custom_call_target="tpu_custom_call" | custom-call | flops 503316480 | bytes 5849088 | tf_op jit(solution)/shard_map/upper/pallas_call | solution.py:31
  49.1 1.6 %collective-permute-start.13 = (bf16[128,896]{1,0:T(8,128)(2,1)S(1)}, bf16[128,896]{1,0:T(8,128)(2,1)S(1)}, u32[]{:S(2)}, u32[]{:S(2)}) collective-permute-start(bf16[128,896]{1,0:T(8,128)(2,1)S(1)} %get-tuple-element.79.msg), channel_id=1, source_target_pairs={{0,16},{16,0},{1,17},{17,1},{2,18},{18,2},{3,19},{19,3},{4,20},{20... | collective-permute-start | bytes 688136 | tf_op jit(solution)/shard_map/ppermute | solution.py:350
  50.6 1.3 %collective-permute-start.14 = (bf16[128,768]{1,0:T(8,128)(2,1)S(1)}, bf16[128,768]{1,0:T(8,128)(2,1)S(1)}, u32[]{:S(2)}, u32[]{:S(2)}) collective-permute-start(bf16[128,768]{1,0:T(8,128)(2,1)S(1)} %get-tuple-element.80), channel_id=1, source_target_pairs={{1,0},{2,1},{3,2},{5,4},{6,5},{7,6},{9,8},{10,9},{11,10},{13,12},{... | collective-permute-start | bytes 589832 | tf_op jit(solution)/shard_map/ppermute | solution.py:487
  51.9 1.3 %collective-permute-start.15 = (f32[128,128]{1,0:T(8,128)S(1)}, f32[128,128]{1,0:T(8,128)S(1)}, u32[]{:S(2)}, u32[]{:S(2)}) collective-permute-start(f32[128,128]{1,0:T(8,128)S(1)} %get-tuple-element.81), channel_id=1, source_target_pairs={{1,16},{2,17},{3,18},{17,0},{18,1},{19,2},{5,20},{6,21},{7,22},{21... | collective-permute-start | bytes 196616 | tf_op jit(solution)/shard_map/ppermute | solution.py:488
  53.3 1.8 %collective-permute-start.18 = (bf16[384,768]{1,0:T(8,128)(2,1)S(1)}, bf16[384,768]{1,0:T(8,128)(2,1)S(1)}, u32[]{:S(2)}, u32[]{:S(2)}) collective-permute-start(bf16[384,768]{1,0:T(8,128)(2,1)S(1)} %constant_dynamic-update-slice_fusion.9.refs_4_), channel_id=1, source_target_pairs={{0,1},{1,0},{2,3},{3,2},{4,5},{5,4},{6,7},{7,6},{8,9},{9,8},{10,11... | collective-permute-start | bytes 1769480 | tf_op jit(solution)/shard_map/ppermute | solution.py:353
  55.1 2.4 %collective-permute-done.15.sum_other = f32[128,128]{1,0:T(8,128)S(1)} collective-permute-done((f32[128,128]{1,0:T(8,128)S(1)}, f32[128,128]{1,0:T(8,128)S(1)}, u32[]{:S(2)}, u32[]{:S(2)}) %collective-permute-start.15) | collective-permute-done | bytes 65568 | tf_op jit(solution)/shard_map/ppermute | solution.py:488
  57.9 2.7 %collective-permute-start.19 = (bf16[384,768]{1,0:T(8,128)(2,1)S(1)}, bf16[384,768]{1,0:T(8,128)(2,1)S(1)}, u32[]{:S(2)}, u32[]{:S(2)}) collective-permute-start(bf16[384,768]{1,0:T(8,128)(2,1)S(1)} %constant_dynamic-update-slice_fusion.12.refs_5_), channel_id=1, source_target_pairs={{0,1},{1,0},{2,3},{3,2},{4,5},{5,4},{6,7},{7,6},{8,9},{9,8},{10,11... | collective-permute-start | bytes 1769480 | tf_op jit(solution)/shard_map/ppermute | solution.py:353
  60.6 1.6 %collective-permute-done.19.refs_7_ = bf16[384,768]{1,0:T(8,128)(2,1)S(1)} collective-permute-done((bf16[384,768]{1,0:T(8,128)(2,1)S(1)}, bf16[384,768]{1,0:T(8,128)(2,1)S(1)}, u32[]{:S(2)}, u32[]{:S(2)}) %collective-permute-start.19) | collective-permute-done | bytes 589856 | tf_op jit(solution)/shard_map/ppermute | solution.py:353
  62.3 1.5 %forward_lo.1 = (bf16[128,768]{1,0:T(8,128)(2,1)S(1)}, f32[768,256]{1,0:T(8,128)S(1)}, bf16[1536,768]{1,0:T(8,128)(2,1)S(1)}) custom-call(s32[1,1]{1,0:T(1,128)S(6)} %copy.18.refs_0_, bf16[128,1536]{1,0:T(8,128)(2,1)S(1)} %get-tuple-element.82.refs_1_, bf16[256,768]{1,0:T(8,128)(2,1)S(1)} %collective-permute-done.4.refs_2_.left_keys, ...), custom_call_target="tpu_custom_call" | custom-call | flops 352321536 | bytes 6881280 | tf_op jit(solution)/shard_map/forward_lo/pallas_call | solution.py:31
  63.8 2.4 %lower.1 = (bf16[128,768]{1,0:T(8,128)(2,1)S(1)}, bf16[128,768]{1,0:T(8,128)(2,1)S(1)}, f32[128,768]{1,0:T(8,128)S(1)}, bf16[128,768]{1,0:T(8,128)(2,1)S(1)}) custom-call(s32[1,2]{1,0:T(1,128)S(1)} %copy-done.5, f32[128,768]{1,0:T(8,128)S(1)} %get-tuple-element.78.own, bf16[128,896]{1,0:T(8,128)(2,1)S(1)} %get-tuple-element.79.msg, ...), custom_call_target="tpu_custom_call" | custom-call | flops 201326592 | bytes 4505600 | tf_op jit(solution)/shard_map/lower/pallas_call | solution.py:31
  66.1 1.4 %collective-permute-done.21.refs_3_ = bf16[128,768]{1,0:T(8,128)(2,1)S(1)} collective-permute-done((bf16[128,768]{1,0:T(8,128)(2,1)S(1)}, bf16[128,768]{1,0:T(8,128)(2,1)S(1)}, u32[]{:S(2)}, u32[]{:S(2)}) %collective-permute-start.21) | collective-permute-done | bytes 196640 | tf_op jit(solution)/shard_map/ppermute | solution.py:353
  67.6 1.7 %collective-permute-done.22.refs_4_ = bf16[256,768]{1,0:T(8,128)(2,1)S(1)} collective-permute-done((bf16[256,768]{1,0:T(8,128)(2,1)S(1)}, bf16[256,768]{1,0:T(8,128)(2,1)S(1)}, u32[]{:S(2)}, u32[]{:S(2)}) %collective-permute-start.22) | collective-permute-done | bytes 393248 | tf_op jit(solution)/shard_map/ppermute | solution.py:353
  69.9 0.8 collective-permute-start.23
  71.0 6.4 %collective-permute-done.27.refs_3_ = bf16[128,768]{1,0:T(8,128)(2,1)S(1)} collective-permute-done((bf16[128,768]{1,0:T(8,128)(2,1)S(1)}, bf16[128,768]{1,0:T(8,128)(2,1)S(1)}, u32[]{:S(2)}, u32[]{:S(2)}) %collective-permute-start.27) | collective-permute-done | bytes 196640 | tf_op jit(solution)/shard_map/ppermute | solution.py:353
  77.3 1.6 %collective-permute-done.23.arrived = bf16[192,768]{1,0:T(8,128)(2,1)S(1)} collective-permute-done((bf16[192,768]{1,0:T(8,128)(2,1)S(1)}, bf16[192,768]{1,0:T(8,128)(2,1)S(1)}, u32[]{:S(2)}, u32[]{:S(2)}) %collective-permute-start.23) | collective-permute-done | bytes 294944 | tf_op jit(solution)/shard_map/ppermute | solution.py:356
  79.1 1.3 %collective-permute-start.20 = (bf16[128,768]{1,0:T(8,128)(2,1)S(1)}, bf16[128,768]{1,0:T(8,128)(2,1)S(1)}, u32[]{:S(2)}, u32[]{:S(2)}) collective-permute-start(bf16[128,768]{1,0:T(8,128)(2,1)S(1)} %get-tuple-element.92), channel_id=1, source_target_pairs={{1,0},{2,1},{3,2},{5,4},{6,5},{7,6},{9,8},{10,9},{11,10},{13,12},{... | collective-permute-start | bytes 589832 | tf_op jit(solution)/shard_map/ppermute | solution.py:500
  80.4 1.6 %collective-permute-start.24 = (bf16[128,768]{1,0:T(8,128)(2,1)S(1)}, bf16[128,768]{1,0:T(8,128)(2,1)S(1)}, u32[]{:S(2)}, u32[]{:S(2)}) collective-permute-start(bf16[128,768]{1,0:T(8,128)(2,1)S(1)} %get-tuple-element.99.dy_mine), channel_id=1, source_target_pairs={{0,16},{16,0},{1,17},{17,1},{2,18},{18,2},{3,19},{19,3},{4,20},{20... | collective-permute-start | bytes 589832 | tf_op jit(solution)/shard_map/ppermute | solution.py:350
  82.5 0.8 collective-permute-start.29
  83.3 4.0 %collective-permute-start.26 = (bf16[96,768]{1,0:T(8,128)(2,1)S(1)}, bf16[96,768]{1,0:T(8,128)(2,1)S(1)}, u32[]{:S(2)}, u32[]{:S(2)}) collective-permute-start(bf16[96,768]{1,0:T(8,128)(2,1)S(1)} %get-tuple-element.104), channel_id=1, source_target_pairs={{0,8},{4,12},{8,0},{12,4},{1,9},{5,13},{9,1},{13,5},{2,10},{6,14},... | collective-permute-start | bytes 442376 | tf_op jit(solution)/shard_map/ppermute | solution.py:356
  88.1 0.9 project_lo.1
  88.9 1.3 %collective-permute-start.25 = (bf16[128,1536]{1,0:T(8,128)(2,1)S(1)}, bf16[128,1536]{1,0:T(8,128)(2,1)S(1)}, u32[]{:S(2)}, u32[]{:S(2)}) collective-permute-start(bf16[128,1536]{1,0:T(8,128)(2,1)S(1)} %get-tuple-element.102), channel_id=1, source_target_pairs={{16,0},{17,1},{18,2},{19,3},{20,4},{21,5},{22,6},{23,7},{24,8},{25... | collective-permute-start | bytes 1179656 | tf_op jit(solution)/shard_map/ppermute | solution.py:518
  90.2 3.5 %collective-permute-done.26.hi_arrived = bf16[96,768]{1,0:T(8,128)(2,1)S(1)} collective-permute-done((bf16[96,768]{1,0:T(8,128)(2,1)S(1)}, bf16[96,768]{1,0:T(8,128)(2,1)S(1)}, u32[]{:S(2)}, u32[]{:S(2)}) %collective-permute-start.26) | collective-permute-done | bytes 147488 | tf_op jit(solution)/shard_map/ppermute | solution.py:356
  93.8 1.7 %collective-permute-done.29.arrived = bf16[192,768]{1,0:T(8,128)(2,1)S(1)} collective-permute-done((bf16[192,768]{1,0:T(8,128)(2,1)S(1)}, bf16[192,768]{1,0:T(8,128)(2,1)S(1)}, u32[]{:S(2)}, u32[]{:S(2)}) %collective-permute-start.29) | collective-permute-done | bytes 294944 | tf_op jit(solution)/shard_map/ppermute | solution.py:356
  95.6 2.4 %collective-permute-start.30 = (bf16[96,768]{1,0:T(8,128)(2,1)S(1)}, bf16[96,768]{1,0:T(8,128)(2,1)S(1)}, u32[]{:S(2)}, u32[]{:S(2)}) collective-permute-start(bf16[96,768]{1,0:T(8,128)(2,1)S(1)} %get-tuple-element.111), channel_id=1, source_target_pairs={{0,8},{4,12},{8,0},{12,4},{1,9},{5,13},{9,1},{13,5},{2,10},{6,14},... | collective-permute-start | bytes 442376 | tf_op jit(solution)/shard_map/ppermute | solution.py:356
  98.0 7.5 %collective-permute-done.30.lo_arrived = bf16[96,768]{1,0:T(8,128)(2,1)S(1)} collective-permute-done((bf16[96,768]{1,0:T(8,128)(2,1)S(1)}, bf16[96,768]{1,0:T(8,128)(2,1)S(1)}, u32[]{:S(2)}, u32[]{:S(2)}) %collective-permute-start.30) | collective-permute-done | bytes 147488 | tf_op jit(solution)/shard_map/ppermute | solution.py:356
  106.2 2.0 %finish.1 = bf16[128,1536]{1,0:T(8,128)(2,1)} custom-call(s32[1,2]{1,0:T(1,128)S(1)} %copy-done.5, f32[128,1536]{1,0:T(8,128)S(1)} %get-tuple-element.101.part, bf16[128,1536]{1,0:T(8,128)(2,1)S(1)} %collective-permute-done.25.msg_in, bf16[128,1536]{1,0:T(8,128)(2,1)S(1)} %get-tuple-element.103.acts, f32[8,1536]{1,0:T(8,128)S(1)} %get-tuple-element.65.vecs, ...), custom_call_target="tpu_custom_call" | custom-call | flops 3932160 | bytes 2408448 | tf_op jit(solution)/shard_map/finish/pallas_call | solution.py:31
  108.2 2.6 %collective-permute-done.31 = bf16[96,768]{1,0:T(8,128)(2,1)S(1)} collective-permute-done((bf16[96,768]{1,0:T(8,128)(2,1)S(1)}, bf16[96,768]{1,0:T(8,128)(2,1)S(1)}, u32[]{:S(2)}, u32[]{:S(2)}) %collective-permute-start.31) | collective-permute-done | bytes 147488 | tf_op jit(solution)/shard_map/ppermute | solution.py:350
  110.8 0.7 maximum_bitcast_fusion
  (62 shorter events, 7.4 us)
Async XLA Ops:
  1.7 8.0 %collective-permute-start.1 = (bf16[96,768]{1,0:T(8,128)(2,1)S(1)}, bf16[96,768]{1,0:T(8,128)(2,1)S(1)}, u32[]{:S(2)}, u32[]{:S(2)}) collective-permute-start(bf16[96,768]{1,0:T(8,128)(2,1)S(1)} %get-tuple-element.116), channel_id=1, source_target_pairs={{0,16},{16,0},{1,17},{17,1},{2,18},{18,2},{3,19},{19,3},{4,20},{20... | collective-permute-start | bytes 442376 | tf_op jit(solution)/shard_map/ppermute | solution.py:350
  4.7 1.0 copy-start
  5.7 0.7 copy-start.3
  6.7 6.4 %collective-permute-start.8 = (bf16[768,128]{1,0:T(8,128)(2,1)S(1)}, bf16[768,128]{1,0:T(8,128)(2,1)S(1)}, u32[]{:S(2)}, u32[]{:S(2)}) collective-permute-start(bf16[768,128]{1,0:T(8,128)(2,1)S(1)} %get-tuple-element.59), channel_id=1, source_target_pairs={{0,2},{1,3},{2,0},{3,1},{4,6},{5,7},{6,4},{7,5},{8,10},{9,11},{10,... | collective-permute-start | bytes 589832 | tf_op jit(solution)/shard_map/ppermute | solution.py:353
  8.3 0.7 copy-start.4
  9.1 11.4 %collective-permute-start = (bf16[144,1536]{1,0:T(8,128)(2,1)S(1)}, bf16[144,1536]{1,0:T(8,128)(2,1)S(1)}, u32[]{:S(2)}, u32[]{:S(2)}) collective-permute-start(bf16[144,1536]{1,0:T(8,128)(2,1)S(1)} %pack.1), channel_id=1, source_target_pairs={{0,16},{16,0},{1,17},{17,1},{2,18},{18,2},{3,19},{19,3},{4,20},{20... | collective-permute-start | bytes 1327112 | tf_op jit(solution)/shard_map/ppermute | solution.py:350
  9.7 8.9 %collective-permute-start.2 = (bf16[96,768]{1,0:T(8,128)(2,1)S(1)}, bf16[96,768]{1,0:T(8,128)(2,1)S(1)}, u32[]{:S(2)}, u32[]{:S(2)}) collective-permute-start(bf16[96,768]{1,0:T(8,128)(2,1)S(1)} %get-tuple-element.61), channel_id=1, source_target_pairs={{0,8},{4,12},{8,0},{12,4},{1,9},{5,13},{9,1},{13,5},{2,10},{6,14},... | collective-permute-start | bytes 442376 | tf_op jit(solution)/shard_map/ppermute | solution.py:356
  13.1 17.1 %copy-start.1 = (bf16[1,1,128,1536]{3,2,1,0:T(8,128)(2,1)S(1)}, bf16[1,1,128,1536]{3,2,1,0:T(8,128)(2,1)}, u32[]{:S(2)}) copy-start(bf16[1,1,128,1536]{3,2,1,0:T(8,128)(2,1)} %param.7) | copy-start | bytes 1179652
  13.1 17.1 %copy-start.2 = (bf16[1,128,1536]{2,1,0:T(8,128)(2,1)S(1)}, bf16[1,128,1536]{2,1,0:T(8,128)(2,1)}, u32[]{:S(2)}) copy-start(bf16[1,128,1536]{2,1,0:T(8,128)(2,1)} %param.8) | copy-start | bytes 1179652
  13.2 10.1 %collective-permute-start.9 = (bf16[768,128]{1,0:T(8,128)(2,1)S(1)}, bf16[768,128]{1,0:T(8,128)(2,1)S(1)}, u32[]{:S(2)}, u32[]{:S(2)}) collective-permute-start(bf16[768,128]{1,0:T(8,128)(2,1)S(1)} %pad_maximum_fusion.3), channel_id=1, source_target_pairs={{0,1},{1,0},{2,3},{3,2},{4,5},{5,4},{6,7},{7,6},{8,9},{9,8},{10,11... | collective-permute-start | bytes 589832 | tf_op jit(solution)/shard_map/ppermute | solution.py:353
  18.6 11.1 %collective-permute-start.5 = (bf16[192,768]{1,0:T(8,128)(2,1)S(1)}, bf16[192,768]{1,0:T(8,128)(2,1)S(1)}, u32[]{:S(2)}, u32[]{:S(2)}) collective-permute-start(bf16[192,768]{1,0:T(8,128)(2,1)S(1)} %get-tuple-element.127), channel_id=1, source_target_pairs={{0,4},{4,0},{8,12},{12,8},{1,5},{5,1},{9,13},{13,9},{2,6},{6,2},{1... | collective-permute-start | bytes 884744 | tf_op jit(solution)/shard_map/ppermute | solution.py:356
  19.4 10.9 %collective-permute-start.3 = (bf16[192,768]{1,0:T(8,128)(2,1)S(1)}, bf16[192,768]{1,0:T(8,128)(2,1)S(1)}, u32[]{:S(2)}, u32[]{:S(2)}) collective-permute-start(bf16[192,768]{1,0:T(8,128)(2,1)S(1)} %get-tuple-element.127), channel_id=1, source_target_pairs={{0,2},{1,3},{2,0},{3,1},{4,6},{5,7},{6,4},{7,5},{8,10},{9,11},{10,... | collective-permute-start | bytes 884744 | tf_op jit(solution)/shard_map/ppermute | solution.py:353
  20.5 11.5 %collective-permute-start.6 = (bf16[96,768]{1,0:T(8,128)(2,1)S(1)}, bf16[96,768]{1,0:T(8,128)(2,1)S(1)}, u32[]{:S(2)}, u32[]{:S(2)}) collective-permute-start(bf16[96,768]{1,0:T(8,128)(2,1)S(1)} %get-tuple-element.69), channel_id=1, source_target_pairs={{0,8},{4,12},{8,0},{12,4},{1,9},{5,13},{9,1},{13,5},{2,10},{6,14},... | collective-permute-start | bytes 442376 | tf_op jit(solution)/shard_map/ppermute | solution.py:356
  23.3 9.9 %collective-permute-start.10 = (bf16[1536,128]{1,0:T(8,128)(2,1)S(1)}, bf16[1536,128]{1,0:T(8,128)(2,1)S(1)}, u32[]{:S(2)}, u32[]{:S(2)}) collective-permute-start(bf16[1536,128]{1,0:T(8,128)(2,1)S(1)} %pad_maximum_fusion.refs_0_), channel_id=1, source_target_pairs={{0,16},{16,0},{1,17},{17,1},{2,18},{18,2},{3,19},{19,3},{4,20},{20... | collective-permute-start | bytes 1179656 | tf_op jit(solution)/shard_map/ppermute | solution.py:350
  29.7 6.9 %collective-permute-start.11 = (bf16[192,768]{1,0:T(8,128)(2,1)S(1)}, bf16[192,768]{1,0:T(8,128)(2,1)S(1)}, u32[]{:S(2)}, u32[]{:S(2)}) collective-permute-start(bf16[192,768]{1,0:T(8,128)(2,1)S(1)} %collective-permute-done.5), channel_id=1, source_target_pairs={{0,2},{1,3},{2,0},{3,1},{4,6},{5,7},{6,4},{7,5},{8,10},{9,11},{10,... | collective-permute-start | bytes 884744 | tf_op jit(solution)/shard_map/ppermute | solution.py:353
  30.7 10.1 %collective-permute-start.4 = (bf16[256,768]{1,0:T(8,128)(2,1)S(1)}, bf16[256,768]{1,0:T(8,128)(2,1)S(1)}, u32[]{:S(2)}, u32[]{:S(2)}) collective-permute-start(bf16[256,768]{1,0:T(8,128)(2,1)S(1)} %get-tuple-element.67.refs_3_.own_keys), channel_id=1, source_target_pairs={{0,1},{1,2},{2,3},{4,5},{5,6},{6,7},{8,9},{9,10},{10,11},{12,13},{... | collective-permute-start | bytes 1179656 | tf_op jit(solution)/shard_map/ppermute | solution.py:426
  32.0 8.7 %collective-permute-start.7 = (bf16[192,768]{1,0:T(8,128)(2,1)S(1)}, bf16[192,768]{1,0:T(8,128)(2,1)S(1)}, u32[]{:S(2)}, u32[]{:S(2)}) collective-permute-start(bf16[192,768]{1,0:T(8,128)(2,1)S(1)} %get-tuple-element.83), channel_id=1, source_target_pairs={{0,4},{4,0},{8,12},{12,8},{1,5},{5,1},{9,13},{13,9},{2,6},{6,2},{1... | collective-permute-start | bytes 884744 | tf_op jit(solution)/shard_map/ppermute | solution.py:356
  40.8 3.9 %collective-permute-start.12 = (bf16[768,768]{1,0:T(8,128)(2,1)S(1)}, bf16[768,768]{1,0:T(8,128)(2,1)S(1)}, u32[]{:S(2)}, u32[]{:S(2)}) collective-permute-start(bf16[768,768]{1,0:T(8,128)(2,1)S(1)} %constant_dynamic-update-slice_fusion.4.refs_4_), channel_id=1, source_target_pairs={{0,1},{1,0},{2,3},{3,2},{4,5},{5,4},{6,7},{7,6},{8,9},{9,8},{10,11... | collective-permute-start | bytes 3538952 | tf_op jit(solution)/shard_map/ppermute | solution.py:353
  42.6 10.7 %collective-permute-start.17 = (bf16[192,768]{1,0:T(8,128)(2,1)S(1)}, bf16[192,768]{1,0:T(8,128)(2,1)S(1)}, u32[]{:S(2)}, u32[]{:S(2)}) collective-permute-start(bf16[192,768]{1,0:T(8,128)(2,1)S(1)} %collective-permute-done.7), channel_id=1, source_target_pairs={{0,2},{1,3},{2,0},{3,1},{4,6},{5,7},{6,4},{7,5},{8,10},{9,11},{10,... | collective-permute-start | bytes 884744 | tf_op jit(solution)/shard_map/ppermute | solution.py:353
  42.6 15.2 %collective-permute-start.16 = (bf16[192,768]{1,0:T(8,128)(2,1)S(1)}, bf16[192,768]{1,0:T(8,128)(2,1)S(1)}, u32[]{:S(2)}, u32[]{:S(2)}) collective-permute-start(bf16[192,768]{1,0:T(8,128)(2,1)S(1)} %get-tuple-element.83), channel_id=1, source_target_pairs={{0,2},{1,3},{2,0},{3,1},{4,6},{5,7},{6,4},{7,5},{8,10},{9,11},{10,... | collective-permute-start | bytes 884744 | tf_op jit(solution)/shard_map/ppermute | solution.py:353
  44.7 1.5 %copy-start.5 = (s32[1,2]{1,0:T(1,128)S(1)}, s32[1,2]{1,0:T(1,128)}, u32[]{:S(2)}) copy-start(s32[1,2]{1,0:T(1,128)} %kept.5) | copy-start | bytes 28
  49.1 8.4 %collective-permute-start.13 = (bf16[128,896]{1,0:T(8,128)(2,1)S(1)}, bf16[128,896]{1,0:T(8,128)(2,1)S(1)}, u32[]{:S(2)}, u32[]{:S(2)}) collective-permute-start(bf16[128,896]{1,0:T(8,128)(2,1)S(1)} %get-tuple-element.79.msg), channel_id=1, source_target_pairs={{0,16},{16,0},{1,17},{17,1},{2,18},{18,2},{3,19},{19,3},{4,20},{20... | collective-permute-start | bytes 688136 | tf_op jit(solution)/shard_map/ppermute | solution.py:350
  50.6 6.9 %collective-permute-start.14 = (bf16[128,768]{1,0:T(8,128)(2,1)S(1)}, bf16[128,768]{1,0:T(8,128)(2,1)S(1)}, u32[]{:S(2)}, u32[]{:S(2)}) collective-permute-start(bf16[128,768]{1,0:T(8,128)(2,1)S(1)} %get-tuple-element.80), channel_id=1, source_target_pairs={{1,0},{2,1},{3,2},{5,4},{6,5},{7,6},{9,8},{10,9},{11,10},{13,12},{... | collective-permute-start | bytes 589832 | tf_op jit(solution)/shard_map/ppermute | solution.py:487
  51.9 5.6 %collective-permute-start.15 = (f32[128,128]{1,0:T(8,128)S(1)}, f32[128,128]{1,0:T(8,128)S(1)}, u32[]{:S(2)}, u32[]{:S(2)}) collective-permute-start(f32[128,128]{1,0:T(8,128)S(1)} %get-tuple-element.81), channel_id=1, source_target_pairs={{1,16},{2,17},{3,18},{17,0},{18,1},{19,2},{5,20},{6,21},{7,22},{21... | collective-permute-start | bytes 196616 | tf_op jit(solution)/shard_map/ppermute | solution.py:488
  53.3 7.4 %collective-permute-start.18 = (bf16[384,768]{1,0:T(8,128)(2,1)S(1)}, bf16[384,768]{1,0:T(8,128)(2,1)S(1)}, u32[]{:S(2)}, u32[]{:S(2)}) collective-permute-start(bf16[384,768]{1,0:T(8,128)(2,1)S(1)} %constant_dynamic-update-slice_fusion.9.refs_4_), channel_id=1, source_target_pairs={{0,1},{1,0},{2,3},{3,2},{4,5},{5,4},{6,7},{7,6},{8,9},{9,8},{10,11... | collective-permute-start | bytes 1769480 | tf_op jit(solution)/shard_map/ppermute | solution.py:353
  57.9 4.3 %collective-permute-start.19 = (bf16[384,768]{1,0:T(8,128)(2,1)S(1)}, bf16[384,768]{1,0:T(8,128)(2,1)S(1)}, u32[]{:S(2)}, u32[]{:S(2)}) collective-permute-start(bf16[384,768]{1,0:T(8,128)(2,1)S(1)} %constant_dynamic-update-slice_fusion.12.refs_5_), channel_id=1, source_target_pairs={{0,1},{1,0},{2,3},{3,2},{4,5},{5,4},{6,7},{7,6},{8,9},{9,8},{10,11... | collective-permute-start | bytes 1769480 | tf_op jit(solution)/shard_map/ppermute | solution.py:353
  60.6 6.9 %collective-permute-start.21 = (bf16[128,768]{1,0:T(8,128)(2,1)S(1)}, bf16[128,768]{1,0:T(8,128)(2,1)S(1)}, u32[]{:S(2)}, u32[]{:S(2)}) collective-permute-start(bf16[128,768]{1,0:T(8,128)(2,1)S(1)} %get-tuple-element.94.refs_2_), channel_id=1, source_target_pairs={{0,2},{1,3},{2,0},{3,1},{4,6},{5,7},{6,4},{7,5},{8,10},{9,11},{10,... | collective-permute-start | bytes 589832 | tf_op jit(solution)/shard_map/ppermute | solution.py:353
  67.5 1.8 %collective-permute-start.22 = (bf16[256,768]{1,0:T(8,128)(2,1)S(1)}, bf16[256,768]{1,0:T(8,128)(2,1)S(1)}, u32[]{:S(2)}, u32[]{:S(2)}) collective-permute-start(bf16[256,768]{1,0:T(8,128)(2,1)S(1)} %pad_maximum_fusion.1), channel_id=1, source_target_pairs={{0,1},{1,0},{2,3},{3,2},{4,5},{5,4},{6,7},{7,6},{8,9},{9,8},{10,11... | collective-permute-start | bytes 1179656 | tf_op jit(solution)/shard_map/ppermute | solution.py:353
  69.9 9.1 %collective-permute-start.23 = (bf16[192,768]{1,0:T(8,128)(2,1)S(1)}, bf16[192,768]{1,0:T(8,128)(2,1)S(1)}, u32[]{:S(2)}, u32[]{:S(2)}) collective-permute-start(bf16[192,768]{1,0:T(8,128)(2,1)S(1)} %get-tuple-element.97), channel_id=1, source_target_pairs={{0,4},{4,0},{8,12},{12,8},{1,5},{5,1},{9,13},{13,9},{2,6},{6,2},{1... | collective-permute-start | bytes 884744 | tf_op jit(solution)/shard_map/ppermute | solution.py:356
  70.7 6.7 %collective-permute-start.27 = (bf16[128,768]{1,0:T(8,128)(2,1)S(1)}, bf16[128,768]{1,0:T(8,128)(2,1)S(1)}, u32[]{:S(2)}, u32[]{:S(2)}) collective-permute-start(bf16[128,768]{1,0:T(8,128)(2,1)S(1)} %get-tuple-element.89.qg.refs_2_), channel_id=1, source_target_pairs={{0,2},{1,3},{2,0},{3,1},{4,6},{5,7},{6,4},{7,5},{8,10},{9,11},{10,... | collective-permute-start | bytes 589832 | tf_op jit(solution)/shard_map/ppermute | solution.py:353
  79.0 3.0 %collective-permute-start.28 = (bf16[256,768]{1,0:T(8,128)(2,1)S(1)}, bf16[256,768]{1,0:T(8,128)(2,1)S(1)}, u32[]{:S(2)}, u32[]{:S(2)}) collective-permute-start(bf16[256,768]{1,0:T(8,128)(2,1)S(1)} %pad_maximum_fusion.2), channel_id=1, source_target_pairs={{0,1},{1,0},{2,3},{3,2},{4,5},{5,4},{6,7},{7,6},{8,9},{9,8},{10,11... | collective-permute-start | bytes 1179656 | tf_op jit(solution)/shard_map/ppermute | solution.py:353
  79.1 8.3 %collective-permute-start.20 = (bf16[128,768]{1,0:T(8,128)(2,1)S(1)}, bf16[128,768]{1,0:T(8,128)(2,1)S(1)}, u32[]{:S(2)}, u32[]{:S(2)}) collective-permute-start(bf16[128,768]{1,0:T(8,128)(2,1)S(1)} %get-tuple-element.92), channel_id=1, source_target_pairs={{1,0},{2,1},{3,2},{5,4},{6,5},{7,6},{9,8},{10,9},{11,10},{13,12},{... | collective-permute-start | bytes 589832 | tf_op jit(solution)/shard_map/ppermute | solution.py:500
  80.4 7.7 %collective-permute-start.24 = (bf16[128,768]{1,0:T(8,128)(2,1)S(1)}, bf16[128,768]{1,0:T(8,128)(2,1)S(1)}, u32[]{:S(2)}, u32[]{:S(2)}) collective-permute-start(bf16[128,768]{1,0:T(8,128)(2,1)S(1)} %get-tuple-element.99.dy_mine), channel_id=1, source_target_pairs={{0,16},{16,0},{1,17},{17,1},{2,18},{18,2},{3,19},{19,3},{4,20},{20... | collective-permute-start | bytes 589832 | tf_op jit(solution)/shard_map/ppermute | solution.py:350
  82.5 13.0 %collective-permute-start.29 = (bf16[192,768]{1,0:T(8,128)(2,1)S(1)}, bf16[192,768]{1,0:T(8,128)(2,1)S(1)}, u32[]{:S(2)}, u32[]{:S(2)}) collective-permute-start(bf16[192,768]{1,0:T(8,128)(2,1)S(1)} %get-tuple-element.108), channel_id=1, source_target_pairs={{0,4},{4,0},{8,12},{12,8},{1,5},{5,1},{9,13},{13,9},{2,6},{6,2},{1... | collective-permute-start | bytes 884744 | tf_op jit(solution)/shard_map/ppermute | solution.py:356
  83.3 10.4 %collective-permute-start.26 = (bf16[96,768]{1,0:T(8,128)(2,1)S(1)}, bf16[96,768]{1,0:T(8,128)(2,1)S(1)}, u32[]{:S(2)}, u32[]{:S(2)}) collective-permute-start(bf16[96,768]{1,0:T(8,128)(2,1)S(1)} %get-tuple-element.104), channel_id=1, source_target_pairs={{0,8},{4,12},{8,0},{12,4},{1,9},{5,13},{9,1},{13,5},{2,10},{6,14},... | collective-permute-start | bytes 442376 | tf_op jit(solution)/shard_map/ppermute | solution.py:356
  88.9 17.2 %collective-permute-start.25 = (bf16[128,1536]{1,0:T(8,128)(2,1)S(1)}, bf16[128,1536]{1,0:T(8,128)(2,1)S(1)}, u32[]{:S(2)}, u32[]{:S(2)}) collective-permute-start(bf16[128,1536]{1,0:T(8,128)(2,1)S(1)} %get-tuple-element.102), channel_id=1, source_target_pairs={{16,0},{17,1},{18,2},{19,3},{20,4},{21,5},{22,6},{23,7},{24,8},{25... | collective-permute-start | bytes 1179656 | tf_op jit(solution)/shard_map/ppermute | solution.py:518
  95.6 9.9 %collective-permute-start.30 = (bf16[96,768]{1,0:T(8,128)(2,1)S(1)}, bf16[96,768]{1,0:T(8,128)(2,1)S(1)}, u32[]{:S(2)}, u32[]{:S(2)}) collective-permute-start(bf16[96,768]{1,0:T(8,128)(2,1)S(1)} %get-tuple-element.111), channel_id=1, source_target_pairs={{0,8},{4,12},{8,0},{12,4},{1,9},{5,13},{9,1},{13,5},{2,10},{6,14},... | collective-permute-start | bytes 442376 | tf_op jit(solution)/shard_map/ppermute | solution.py:356
  105.6 5.2 %collective-permute-start.31 = (bf16[96,768]{1,0:T(8,128)(2,1)S(1)}, bf16[96,768]{1,0:T(8,128)(2,1)S(1)}, u32[]{:S(2)}, u32[]{:S(2)}) collective-permute-start(bf16[96,768]{1,0:T(8,128)(2,1)S(1)} %get-tuple-element.113), channel_id=1, source_target_pairs={{0,16},{16,0},{1,17},{17,1},{2,18},{18,2},{3,19},{19,3},{4,20},{20... | collective-permute-start | bytes 442376 | tf_op jit(solution)/shard_map/ppermute | solution.py:350
